TPU v7x, 512 devices: a whole 4x8x8 slice. The times are simulated.
512 devices in a mesh: section: 16 (over x_hi, z), kvp: 16 (over x_lo, y), tp: 2 (over core).
Axes of the slice: x: 4 (x_hi: 2, x_lo: 2; x = x_hi * 2 + x_lo), y: 8, z: 8, core: 2. Of those that a mesh axis runs over, the one named last changes fastest.
Arguments:
- entering: bfloat16 [16, 128, 4096], P('section', 'tp', 'kvp'), may hold values from -6 to 6
- feed: bfloat16 [1, 128, 4096], P(None, 'tp', 'kvp'), may hold values from -6 to 6
- gain: float32 [16, 4096], P('section'), may hold values from 0.5 to 1.5
- wq: bfloat16 [16, 4096, 2, 2048], P('section', None, 'tp', 'kvp'), may hold values from -0.09375 to 0.09375
- wkv: bfloat16 [16, 4096, 2, 512], P('section', None, 'tp', 'kvp'), may hold values from -0.21875 to 0.21875
- wo: bfloat16 [16, 4096, 4096], P('section', 'tp', 'kvp'), may hold values from -0.09375 to 0.09375
- cache: bfloat16 [16, 2, 4, 8192, 128], P('section', None, 'tp', 'kvp'), may hold values from -180 to 180
- prefix_len: int32 [16, 16], P('section', 'kvp'), may hold values from 1 to 256, as said below
- owner: int32 [2, 16], P(None, 'section'), may hold values from 0 to 15
Outputs:
- states: bfloat16 [2, 16, 128, 4096], P(None, 'section', 'tp', 'kvp')
- new_cache: bfloat16 [16, 2, 4, 8192, 128], P('section', None, 'tp', 'kvp')
Inputs may be any that keep to these rules, and one draw needn't show every extreme that they name: `prefix_len`: in every layer some shard holds exactly 256 filled slots.
All inputs are finite; a program needn't handle non-finite values.
Results may differ from a plain program's by a relative error of at most 0.03.
The roundings to bfloat16 on the way count: a program that leaves them out, or rounds other values in their place, can miss the bound.
Values may be sent and summed in bfloat16 or wider, within the bound.
No kernel may reach another device: no remote copies, remote signals or barrier semaphores. Data moves between devices by JAX's collectives and lax.ppermute only.
A program may use at most 128 MiB of HBM per device.

v0:
```python
import math

import jax
import jax.numpy as jnp
from jax import lax
from jax.sharding import PartitionSpec as P

H = 32
KVH = 4
HD = 128
NCH = 2


EPS = 1e-05


def shifted(block, axis, distance):
    devices = range(lax.axis_size(axis))
    route = [(i - distance, i) for i in devices if i - distance in devices]
    return lax.ppermute(block, axis, route)


def combined_all(part, axis, combine):
    gathered = jax.tree.map(lambda a: lax.all_gather(a, axis), part)

    def take(source):
        return jax.tree.map(lambda a: lax.dynamic_index_in_dim(a, source, 0, False), gathered)

    return lax.fori_loop(
        1, lax.axis_size(axis), lambda source, state: combine(state, take(source)), take(0)
    )


def gather_rows(piece):
    columns = lax.all_gather(piece, "kvp", axis=1, tiled=True)
    return lax.all_gather(columns, "tp", axis=0, tiled=True)


def combine(former, latter):
    former_max, former_sum, former_out = former
    latter_max, latter_sum, latter_out = latter
    top_max = jnp.maximum(former_max, latter_max)
    former_weight = jnp.exp(former_max - top_max)
    latter_weight = jnp.exp(latter_max - top_max)
    totals = former_sum * former_weight + latter_sum * latter_weight
    merged = former_out * former_weight[..., None] + latter_out * latter_weight[..., None]
    return (top_max, totals, merged)


def body(entering, feed, gain, wq, wkv, wo, cache, prefix_len, owner):
    shard_id = lax.axis_index("kvp")
    section_id = lax.axis_index("section")
    span_rows = entering.shape[1] * 2
    group_size = H // KVH
    score_scale = 1.0 / math.sqrt(HD)
    cache_now = cache[0]
    filled = prefix_len[0, 0]
    row_index = jnp.arange(span_rows, dtype=jnp.int32)
    slot_index = jnp.arange(cache_now.shape[2], dtype=jnp.int32)
    outputs = []
    previous = None
    for moment in range(NCH):
        if moment == 0:
            x_shard = entering[0]
        else:
            passed = shifted(previous, "section", 1)
            x_shard = jnp.where(section_id == 0, feed[moment - 1], passed)
        widened = x_shard.astype(jnp.float32)
        full_rows = gather_rows(x_shard).astype(jnp.float32)
        inverse = lax.rsqrt(jnp.mean(full_rows * full_rows, axis=1, keepdims=True) + EPS)
        normed = (full_rows * inverse * gain[0]).astype(jnp.bfloat16)
        query_part = jnp.dot(normed, wq[0, :, 0, :], preferred_element_type=jnp.float32).astype(
            jnp.bfloat16
        )
        keyval_part = jnp.dot(normed, wkv[0, :, 0, :], preferred_element_type=jnp.float32).astype(
            jnp.bfloat16
        )
        queries, keyvals = (
            lax.all_gather(query_part, "kvp", axis=1, tiled=True),
            lax.all_gather(keyval_part, "kvp", axis=1, tiled=True),
        )
        local_heads = keyvals.shape[1] // (2 * HD)
        fresh = jnp.transpose(keyvals.reshape(span_rows, local_heads, 2, HD), (2, 1, 0, 3))
        is_owner = owner[moment, 0] == shard_id
        updated = lax.dynamic_update_slice(cache_now, fresh, (0, 0, filled, 0))
        cache_now = jnp.where(is_owner, updated, cache_now)
        query_heads = queries.reshape(span_rows, local_heads, group_size, HD)
        scores = (
            jnp.einsum(
                "rkgd,kpd->rkgp", query_heads, cache_now[0], preferred_element_type=jnp.float32
            )
            * score_scale
        )
        limits = filled + jnp.where(is_owner, row_index + 1, 0)
        bias = jnp.where(slot_index[None, :] < limits[:, None], 0.0, -1e30).astype(jnp.float32)
        masked = scores + bias[:, None, None, :]
        maxima = jnp.max(masked, axis=-1)
        expon = jnp.exp(masked - maxima[..., None])
        denoms = jnp.sum(expon, axis=-1)
        probs = expon.astype(jnp.bfloat16)
        partial_out = jnp.einsum(
            "rkgp,kpd->rkgd", probs, cache_now[1], preferred_element_type=jnp.float32
        )
        head_count = local_heads * group_size
        maxima = maxima.reshape(span_rows, head_count)
        denoms = denoms.reshape(span_rows, head_count)
        partial_out = partial_out.reshape(span_rows, head_count, HD)
        top_max, totals, merged = combined_all((maxima, denoms, partial_out), "kvp", combine)
        attended = (
            (merged / totals[..., None]).reshape(span_rows, head_count * HD).astype(jnp.bfloat16)
        )
        mixed_out = lax.psum_scatter(
            jnp.dot(attended, wo[0], preferred_element_type=jnp.float32),
            "tp",
            scatter_dimension=0,
            tiled=True,
        )
        result = (widened + mixed_out).astype(jnp.bfloat16)
        outputs.append(result)
        previous = result
        filled = filled + jnp.where(is_owner, span_rows, 0).astype(jnp.int32)
    return (jnp.stack(outputs)[:, None], cache_now[None])


def solution(mesh):
    in_specs = (
        P("section", "tp", "kvp"),
        P(None, "tp", "kvp"),
        P("section", None),
        P("section", None, "tp", "kvp"),
        P("section", None, "tp", "kvp"),
        P("section", "tp", "kvp"),
        P("section", None, "tp", "kvp", None),
        P("section", "kvp"),
        P(None, "section"),
    )
    out_specs = (P(None, "section", "tp", "kvp"), P("section", None, "tp", "kvp", None))
    return jax.shard_map(body, mesh=mesh, in_specs=in_specs, out_specs=out_specs, check_vma=False)
```

profile of v0, /device:TPU:7, one launch (start us, length us, event | category | flops | bytes accessed | tf_op | source)
XLA Modules:
  0.0 760.0 jit_solution(7897682958857896527)
XLA Ops:
  8.4 31.3 %all-gather = bf16[1,64,4096]{2,1,0:T(8,128)(2,1)} all-gather(bf16[1,64,256]{2,1,0:T(8,128)(2,1)} %param.13), channel_id=2, replica_groups=mesh['section'=16,'kvp'=16,'tp'=2] {'kvp'}, dimensions={2}, use_global_device_ids=true | all-gather | bytes 557056 | tf_op jit(solution)/shard_map/all_gather | solution.py:35
  42.5 22.1 %all-gather.13.cloned.1.call-done = bf16[1,128,4096]{2,1,0:T(8,128)(2,1)} async-done(((bf16[1,64,4096]{2,1,0:T(8,128)(2,1)}), bf16[1,128,4096]{2,1,0:T(8,128)(2,1)}) %all-gather.13.cloned.1.call-update) | async-done | bytes 1048592 | tf_op jit(solution)/shard_map/all_gather | solution.py:36
  68.0 26.2 %all_gather.44 = bf16[128,512]{0,1:T(8,128)(2,1)S(1)} all-gather(bf16[128,32]{0,1:T(8,128)(2,1)S(1)} %convolution_convert_fusion.3), channel_id=1, replica_groups=mesh['section'=16,'kvp'=16,'tp'=2] {'kvp'}, dimensions={1}, use_global_device_ids=true | all-gather | bytes 139264 | tf_op jit(solution)/shard_map/all_gather | solution.py:80
  96.1 25.7 %all_gather.45 = bf16[128,2048]{1,0:T(8,128)(2,1)S(1)} all-gather(bf16[128,128]{1,0:T(8,128)(2,1)S(1)} %convolution_convert_fusion.1), channel_id=1, replica_groups=mesh['section'=16,'kvp'=16,'tp'=2] {'kvp'}, dimensions={1}, use_global_device_ids=true | all-gather | bytes 557056 | tf_op jit(solution)/shard_map/all_gather | solution.py:79
  123.2 1.9 copy-done.1
  127.7 3.0 fusion.7
  130.7 24.9 %all_gather.47 = f32[16,128,16]{1,2,0:T(8,128)S(1)} all-gather(f32[1,128,16]{1,2,0:T(8,128)S(1)} %bitcast.189), channel_id=1, replica_groups=mesh['section'=16,'kvp'=16,'tp'=2] {'kvp'}, dimensions={0}, use_global_device_ids=true | all-gather | bytes 139264 | tf_op jit(solution)/shard_map/all_gather | solution.py:24
  155.6 27.8 %all_gather.46 = f32[16,128,16]{1,2,0:T(8,128)S(1)} all-gather(f32[1,128,16]{1,2,0:T(8,128)S(1)} %bitcast.186), channel_id=1, replica_groups=mesh['section'=16,'kvp'=16,'tp'=2] {'kvp'}, dimensions={0}, use_global_device_ids=true | all-gather | bytes 139264 | tf_op jit(solution)/shard_map/all_gather | solution.py:24
  183.4 144.8 %all-gather.7.cloned.1.call-done = f32[16,128,16,128]{3,2,1,0:T(8,128)} async-done(((f32[1,128,16,128]{3,2,1,0:T(8,128)}), f32[16,128,16,128]{3,2,1,0:T(8,128)}) %all-gather.7.cloned.1.call-update) | async-done | bytes 16777232 | tf_op jit(solution)/shard_map/all_gather | solution.py:24
  329.5 32.1 %while.38 = (s32[]{:T(128)}, f32[128,16]{0,1:T(8,128)S(1)}, f32[128,16]{0,1:T(8,128)S(1)}, f32[128,16,128]{2,1,0:T(8,128)S(1)}, f32[16,128,16]{1,2,0:T(8,128)S(1...) while((s32[]{:T(128)}, f32[128,16]{0,1:T(8,128)S(1)}, ...), condition=%wide.region_4.5_spmd, body=%wide.region_3.4_spmd.sunk | while | flops 798725 | bytes 3260559 | solution.py:29
  329.7 1.9 fusion.64
  331.9 1.9 fusion.64
  334.0 1.9 fusion.64
  336.2 1.9 fusion.64
  338.3 1.9 fusion.64
  340.4 1.9 fusion.64
  342.6 1.9 fusion.64
  363.1 14.8 %reduce-scatter.3.cloned.1.call-done = f32[64,256]{1,0:T(8,128)} async-done(((f32[128,256]{1,0:T(8,128)}), f32[64,256]{1,0:T(8,128)}) %reduce-scatter.3.cloned.1.call-update) | async-done | bytes 65552 | tf_op jit(solution)/shard_map/reduce_scatter | solution.py:112
  378.8 3.3 collective-permute-start
  382.1 5.0 collective-permute-done
  387.1 30.5 %all_gather.49 = bf16[64,4096]{1,0:T(8,128)(2,1)} all-gather(bf16[64,256]{1,0:T(8,128)(2,1)S(1)} %bitcast_select_fusion.2), channel_id=1, replica_groups=mesh['section'=16,'kvp'=16,'tp'=2] {'kvp'}, dimensions={1}, use_global_device_ids=true | all-gather | bytes 557056 | tf_op jit(solution)/shard_map/all_gather | solution.py:35
  418.3 19.5 %all-gather.9.cloned.1.call-done = bf16[128,4096]{1,0:T(8,128)(2,1)} async-done(((bf16[64,4096]{1,0:T(8,128)(2,1)}), bf16[128,4096]{1,0:T(8,128)(2,1)}) %all-gather.9.cloned.1.call-update) | async-done | bytes 1048592 | tf_op jit(solution)/shard_map/all_gather | solution.py:36
  441.1 26.2 %all_gather.51 = bf16[128,512]{0,1:T(8,128)(2,1)S(1)} all-gather(bf16[128,32]{0,1:T(8,128)(2,1)S(1)} %convolution_convert_fusion.2), channel_id=1, replica_groups=mesh['section'=16,'kvp'=16,'tp'=2] {'kvp'}, dimensions={1}, use_global_device_ids=true | all-gather | bytes 139264 | tf_op jit(solution)/shard_map/all_gather | solution.py:80
  468.1 2.2 convolution_convert_fusion
  470.3 25.7 %all_gather.52 = bf16[128,2048]{1,0:T(8,128)(2,1)S(1)} all-gather(bf16[128,128]{1,0:T(8,128)(2,1)S(1)} %convolution_convert_fusion), channel_id=1, replica_groups=mesh['section'=16,'kvp'=16,'tp'=2] {'kvp'}, dimensions={1}, use_global_device_ids=true | all-gather | bytes 557056 | tf_op jit(solution)/shard_map/all_gather | solution.py:79
  496.9 1.9 copy-done.2
  501.3 3.0 fusion.9
  504.4 24.9 %all_gather.54 = f32[16,128,16]{1,2,0:T(8,128)S(1)} all-gather(f32[1,128,16]{1,2,0:T(8,128)S(1)} %bitcast.190), channel_id=1, replica_groups=mesh['section'=16,'kvp'=16,'tp'=2] {'kvp'}, dimensions={0}, use_global_device_ids=true | all-gather | bytes 139264 | tf_op jit(solution)/shard_map/all_gather | solution.py:24
  529.2 27.8 %all_gather.53 = f32[16,128,16]{1,2,0:T(8,128)S(1)} all-gather(f32[1,128,16]{1,2,0:T(8,128)S(1)} %bitcast.187), channel_id=1, replica_groups=mesh['section'=16,'kvp'=16,'tp'=2] {'kvp'}, dimensions={0}, use_global_device_ids=true | all-gather | bytes 139264 | tf_op jit(solution)/shard_map/all_gather | solution.py:24
  557.0 144.9 %all-gather.11.cloned.1.call-done = f32[16,128,16,128]{3,2,1,0:T(8,128)} async-done(((f32[1,128,16,128]{3,2,1,0:T(8,128)}), f32[16,128,16,128]{3,2,1,0:T(8,128)}) %all-gather.11.cloned.1.call-update) | async-done | bytes 16777232 | tf_op jit(solution)/shard_map/all_gather | solution.py:24
  703.2 32.1 %while.39 = (s32[]{:T(128)}, f32[128,16]{0,1:T(8,128)S(1)}, f32[128,16]{0,1:T(8,128)S(1)}, f32[128,16,128]{2,1,0:T(8,128)S(1)}, f32[16,128,16]{1,2,0:T(8,128)S(1...) while((s32[]{:T(128)}, f32[128,16]{0,1:T(8,128)S(1)}, ...), condition=%wide.region_10.11_spmd, body=%wide.region_9.10_spmd.sunk | while | flops 798725 | bytes 3260559 | solution.py:29
  736.7 14.9 %reduce-scatter.5.cloned.1.call-done = f32[64,256]{1,0:T(8,128)} async-done(((f32[128,256]{1,0:T(8,128)}), f32[64,256]{1,0:T(8,128)}) %reduce-scatter.5.cloned.1.call-update) | async-done | bytes 65552 | tf_op jit(solution)/shard_map/reduce_scatter | solution.py:112
  (184 shorter events, 77.0 us)
Async XLA Ops:
  7.2 354.9 %copy-start = (bf16[1,2048,256]{2,1,0:T(8,128)(2,1)S(1)}, bf16[1,2048,256]{2,1,0:T(8,128)(2,1)}, u32[]{:S(2)}) copy-start(bf16[1,2048,256]{2,1,0:T(8,128)(2,1)} %param.18) | copy-start | bytes 3145732
  7.2 87.1 %copy-start.8 = (f32[1,4096]{1,0:T(1,128)S(1)}, f32[1,4096]{1,0:T(1,128)}, u32[]{:S(2)}) copy-start(f32[1,4096]{1,0:T(1,128)} %param.15) | copy-start | bytes 49156
  7.2 87.1 %copy-start.6 = (bf16[1,4096,1,128]{3,1,2,0:T(8,128)(2,1)S(1)}, bf16[1,4096,1,128]{3,1,2,0:T(8,128)(2,1)}, u32[]{:S(2)}) copy-start(bf16[1,4096,1,128]{3,1,2,0:T(8,128)(2,1)} %param.16) | copy-start | bytes 3145732
  7.2 57.4 %all-gather.13.cloned.1.call-start = ((), (), s32[]{:S(2)}) async-start(), calls=%async_computation.7 | async-start | bytes 1572864 | tf_op jit(solution)/shard_map/all_gather | solution.py:36
  39.8 288.4 %all-gather.7.cloned.1.call-start = ((), (), s32[]{:S(2)}) async-start(), calls=%async_computation.2 | async-start | bytes 17825792 | tf_op jit(solution)/shard_map/all_gather | solution.py:24
  123.2 1.9 copy-start.1
  127.6 250.3 %reduce-scatter.3.cloned.1.call-start = ((), (), s32[]{:S(2)}) async-start(), calls=%async_computation.3 | async-start | bytes 196608 | tf_op jit(solution)/shard_map/reduce_scatter | solution.py:112
  329.5 48.5 %copy-start.4 = (bf16[1,64,256]{2,1,0:T(8,128)(2,1)S(1)}, bf16[1,64,256]{2,1,0:T(8,128)(2,1)}, u32[]{:S(2)}) copy-start(bf16[1,64,256]{2,1,0:T(8,128)(2,1)} %param.13) | copy-start | bytes 98308
  329.5 57.6 %copy-start.5 = (bf16[1,64,256]{2,1,0:T(8,128)(2,1)S(1)}, bf16[1,64,256]{2,1,0:T(8,128)(2,1)}, u32[]{:S(2)}) copy-start(bf16[1,64,256]{2,1,0:T(8,128)(2,1)} %param.14) | copy-start | bytes 98308
  361.6 77.8 %copy-start.7 = (bf16[1,4096,1,32]{1,3,2,0:T(8,128)(2,1)S(1)}, bf16[1,4096,1,32]{1,3,2,0:T(8,128)(2,1)}, u32[]{:S(2)}) copy-start(bf16[1,4096,1,32]{1,3,2,0:T(8,128)(2,1)} %param.17) | copy-start | bytes 786436
  363.1 74.8 %all-gather.9.cloned.1.call-start = ((), (), s32[]{:S(2)}) async-start(), calls=%async_computation.4 | async-start | bytes 1572864 | tf_op jit(solution)/shard_map/all_gather | solution.py:36
  378.8 8.3 %collective-permute-start = (bf16[64,256]{1,0:T(8,128)(2,1)S(1)}, bf16[64,256]{1,0:T(8,128)(2,1)S(1)}, u32[]{:S(2)}, u32[]{:S(2)}) collective-permute-start(bf16[64,256]{1,0:T(8,128)(2,1)S(1)} %fusion.50), channel_id=1, source_target_pairs={{0,32},{32,64},{64,96},{96,128},{128,160},{160,192},{192,224},{224... | collective-permute-start | bytes 98312 | tf_op jit(solution)/shard_map/ppermute | solution.py:20
  417.6 284.3 %all-gather.11.cloned.1.call-start = ((), (), s32[]{:S(2)}) async-start(), calls=%async_computation.5 | async-start | bytes 17825792 | tf_op jit(solution)/shard_map/all_gather | solution.py:24
  468.0 28.8 %copy-start.3 = (bf16[2,2,512,128]{3,2,1,0:T(8,128)(2,1)}, bf16[2,2,512,128]{3,2,1,0:T(8,128)(2,1)S(1)}, u32[]{:S(2)}) copy-start(bf16[2,2,512,128]{3,2,1,0:T(8,128)(2,1)S(1)} %select_n.127) | copy-start | bytes 1572868
  496.9 1.9 copy-start.2
  501.3 250.3 %reduce-scatter.5.cloned.1.call-start = ((), (), s32[]{:S(2)}) async-start(), calls=%async_computation.6 | async-start | bytes 196608 | tf_op jit(solution)/shard_map/reduce_scatter | solution.py:112
Sparse Core Ops, SparseCore 0:
  39.9 24.6 all-gather.12
  127.8 200.3 all-gather.6
  363.2 14.7 reduce-scatter.2
  417.7 20.0 all-gather.8
  501.4 200.4 all-gather.10
  736.9 14.7 reduce-scatter.4
where the time goes:
time: 764 us; the launch traced here: 760 us
  waiting for transfers between devices  366 us (48%)
  blocking collectives  271 us (35%)
  other arithmetic  69.6 us (9%)
  local copies, waits for them, and re-layouts  19.4 us (3%)
  between operations  16.4 us (2%)
  matrix products  13 us (2%)
    all_gather x2, waiting for transfers between devices, combined_all(): gathered = jax.tree.map(lambda a: lax.all_gather(a, axis), part)  290 us
    all_gather x4, blocking collectives, combined_all(): gathered = jax.tree.map(lambda a: lax.all_gather(a, axis), part)  105 us
    all_gather x2, blocking collectives, gather_rows(): columns = lax.all_gather(piece, 'kvp', axis=1, tiled=True)  61.8 us
    add x30, other arithmetic, combine(): former_out * former_weight[..., None]  56.7 us
    all_gather x2, blocking collectives, body(): lax.all_gather(keyval_part, 'kvp', axis=1, tiled=True)  52.4 us
    all_gather x2, blocking collectives, body(): lax.all_gather(query_part, 'kvp', axis=1, tiled=True)  51.4 us
    all_gather x2, waiting for transfers between devices, gather_rows(): return lax.all_gather(columns, 'tp', axis=0, tiled=True)  41.6 us
    reduce_scatter x2, waiting for transfers between devices, body(): lax.psum_scatter(jnp.dot(attended, wo[0], preferred_element_type=jnp.floa...  29.7 us
  transfers between devices with their start and end apart: 7, of which 7 were waited for; matrix products, arithmetic and copies ran while one was open for 1% of the time, Pallas kernels for 0%

commit v1 on v0

v1 whole, which is shorter than its diff:
```python
import functools
import math

import jax
import jax.numpy as jnp
from jax import lax
from jax.experimental import pallas as pl
from jax.experimental.pallas import tpu as pltpu
from jax.sharding import PartitionSpec as P

HD = 128
NCH = 2
EPS = 1e-05
N = 16
RING = 8
ROWS = 64
SPAN = 128
PRE = 256
D = 4096
COLS = 256
SCALE = 1.0 / math.sqrt(HD)
LOW = -1e30
F32 = jnp.float32
BF16 = jnp.bfloat16
RINGS = [list(range(RING)), list(range(RING, N))]
VMEM = pl.BlockSpec(memory_space=pltpu.VMEM)
SMEM = pl.BlockSpec(memory_space=pltpu.SMEM)
PARAMS = pltpu.CompilerParams(vmem_limit_bytes=40 * 1024 * 1024)


def dot(a, b):
    return jnp.dot(a, b, preferred_element_type=F32)


def dot_t(a, b):
    return lax.dot_general(a, b, (((1,), (1,)), ((), ())), preferred_element_type=F32)


def normalise(place, mine, other, gain, normed):
    t = place[0]
    for half, ref in ((t, mine), (1 - t, other)):
        total = jnp.zeros((ROWS, COLS), F32)
        for j in range(N):
            part = ref[j].astype(F32)
            total = total + part * part
        inverse = lax.rsqrt(jnp.sum(total, axis=1, keepdims=True) / D + EPS)
        rows = pl.ds(pl.multiple_of(half * ROWS, ROWS), ROWS)
        for j in range(N):
            cols = slice(j * COLS, (j + 1) * COLS)
            normed[rows, cols] = (ref[j].astype(F32) * inverse * gain[:, cols]).astype(BF16)


def project_first(place, lens, mine, other, gain, wq, wkv, q_out, kv_out, normed):
    normalise(place, mine, other, gain, normed)
    q_out[...] = dot(normed[...], wq[...]).astype(BF16)
    kv = dot(normed[...], wkv[...]).T.astype(BF16)
    filled = jnp.full((16, SPAN), lens[0].astype(F32), F32).astype(BF16)
    for j in range(N):
        kv_out[j, 0:32] = kv
        kv_out[j, 32:48] = filled


def project_later(place, mine, other, gain, wq, wkv, q_out, kv_out, normed):
    normalise(place, mine, other, gain, normed)
    q_out[...] = dot(normed[...], wq[...]).astype(BF16)
    kv_out[...] = dot_t(normed[...], wkv[...]).astype(BF16)


def attend(place, q_ref, held, first, *rest, later):
    if later:
        second, out, scores = rest
    else:
        out, scores = rest
    g = place[1]
    q = q_ref[...]
    slot = lax.broadcasted_iota(jnp.int32, (1, PRE), 1).astype(F32)
    top = jnp.full((SPAN, PRE), LOW, F32)
    for k in range(RING):
        for o in range(2):
            shard = (g if o == 0 else 1 - g) * RING + k
            filled = first[shard, 32:48][0:1].astype(F32)
            filled = jnp.concatenate([filled, filled], axis=1)
            s = dot_t(q, held[k, o, 0]) * SCALE
            s = jnp.where(slot < filled, s, LOW)
            b = (k * 2 + o) * PRE
            scores[:, b : b + PRE] = s
            top = jnp.maximum(top, s)
    top = jnp.max(top, axis=1, keepdims=True)
    row = lax.broadcasted_iota(jnp.int32, (SPAN, SPAN), 0)
    col = lax.broadcasted_iota(jnp.int32, (SPAN, SPAN), 1)
    keys = jnp.concatenate([first[g * RING + i, 0:32] for i in range(4)], axis=0)
    values = jnp.concatenate([first[g * RING + 4 + i, 0:32] for i in range(4)], axis=0)
    fresh = [dot(q, keys) * SCALE]
    if later:
        fresh.append(dot_t(q, second[:, 0:HD]) * SCALE)
    fresh[-1] = jnp.where(col <= row, fresh[-1], LOW)
    for s in fresh:
        top = jnp.maximum(top, jnp.max(s, axis=1, keepdims=True))
    total = jnp.zeros((SPAN, PRE), F32)
    acc = jnp.zeros((SPAN, HD), F32)
    for k in range(RING):
        for o in range(2):
            b = (k * 2 + o) * PRE
            e = jnp.exp(scores[:, b : b + PRE] - top)
            total = total + e
            acc = acc + dot(e.astype(BF16), held[k, o, 1])
    total = jnp.sum(total, axis=1, keepdims=True)
    for i, s in enumerate(fresh):
        e = jnp.exp(s - top)
        total = total + jnp.sum(e, axis=1, keepdims=True)
        if i == 0:
            acc = acc + dot_t(e.astype(BF16), values)
        else:
            acc = acc + dot(e.astype(BF16), second[:, HD : 2 * HD])
    result = (acc / total).astype(BF16)
    for j in range(N):
        out[j] = result


def mix(place, att, wo, x_ref, mine, other):
    t = place[0]
    acc = jnp.zeros((SPAN, COLS), F32)
    for j in range(N):
        acc = acc + dot(att[j], wo[j * HD : (j + 1) * HD, :])
    top, bottom = acc[0:ROWS], acc[ROWS:SPAN]
    mine[...] = x_ref[...].astype(F32) + jnp.where(t == 0, top, bottom)
    other[...] = jnp.where(t == 0, bottom, top)


def spread(block):
    return lax.all_to_all(block, "kvp", 0, 0, tiled=True)


def swap(block):
    return lax.ppermute(block, "tp", [(0, 1), (1, 0)])


def shape(*dims, dtype=BF16):
    return jax.ShapeDtypeStruct(dims, dtype)


def body(entering, feed, gain, wq, wkv, wo, cache, prefix_len, owner):
    shard_id = lax.axis_index("kvp")
    section_id = lax.axis_index("section")
    g = shard_id // RING
    place = jnp.stack([lax.axis_index("tp"), g]).astype(jnp.int32)
    filled = prefix_len[0, 0]
    wq_here, wkv_here, wo_here = wq[0, :, 0, :], wkv[0, :, 0, :], wo[0]
    cache_here = cache[0]

    prefix = cache_here[:, :, :PRE, :]
    own = lax.dynamic_index_in_dim(prefix, g, 1, False)
    give = lax.dynamic_index_in_dim(prefix, 1 - g, 1, False)
    got = lax.ppermute(give, "kvp", [(i, (i + RING) % N) for i in range(N)])
    held = lax.all_gather(jnp.stack([own, got]), "kvp", axis_index_groups=RINGS)

    wkv_t, held = lax.optimization_barrier((wkv_here.T, held))
    wkv_all = lax.all_gather(wkv_t, "kvp", axis_index_groups=RINGS).reshape(2 * HD, D)

    outputs, fresh_all = [], []
    x = entering[0]
    for moment in range(NCH):
        if moment:
            passed = lax.ppermute(outputs[-1], "section", [(i, i + 1) for i in range(15)])
            x = jnp.where(section_id == 0, feed[moment - 1], passed)
        mine = spread(jnp.broadcast_to(x[None], (N, ROWS, COLS)))
        other = swap(mine)
        scratch = [pltpu.VMEM((SPAN, D), BF16)]
        if moment == 0:
            q, kv = pl.pallas_call(
                project_first,
                out_shape=(shape(SPAN, HD), shape(N, 48, SPAN)),
                in_specs=[SMEM, SMEM] + [VMEM] * 5,
                out_specs=(VMEM, VMEM),
                scratch_shapes=scratch,
                compiler_params=PARAMS,
                name="project_first",
            )(place, filled[None], mine, other, gain, wq_here, wkv_here)
            first = spread(kv)
            extra = (first,)
            both = jnp.transpose(first[:, 0:32].reshape(2, 2, HD, SPAN), (1, 0, 3, 2))
        else:
            q, kv = pl.pallas_call(
                project_later,
                out_shape=(shape(SPAN, HD), shape(SPAN, 2 * HD)),
                in_specs=[SMEM] + [VMEM] * 5,
                out_specs=(VMEM, VMEM),
                scratch_shapes=scratch,
                compiler_params=PARAMS,
                name="project_later",
            )(place, mine, other, gain, wq_here, wkv_all)
            extra = (first, kv)
            pair = lax.ppermute(kv, "kvp", [(i, (i + RING) % N) for i in range(N)])
            heads = jnp.where(g == 0, jnp.stack([kv, pair]), jnp.stack([pair, kv]))
            both = jnp.transpose(heads.reshape(2, SPAN, 2, HD), (2, 0, 1, 3))
        fresh_all.append(both)
        att = pl.pallas_call(
            functools.partial(attend, later=moment > 0),
            out_shape=shape(N, SPAN, HD),
            in_specs=[SMEM] + [VMEM] * (2 + len(extra)),
            out_specs=VMEM,
            scratch_shapes=[pltpu.VMEM((SPAN, N * PRE), F32)],
            compiler_params=PARAMS,
            name="attend",
        )(place, q, held, *extra)
        att = spread(att)
        own_sum, other_sum = pl.pallas_call(
            mix,
            out_shape=(shape(ROWS, COLS, dtype=F32), shape(ROWS, COLS, dtype=F32)),
            in_specs=[SMEM] + [VMEM] * 3,
            out_specs=(VMEM, VMEM),
            compiler_params=PARAMS,
            name="mix",
        )(place, att, wo_here, x)
        outputs.append((own_sum + swap(other_sum)).astype(BF16))

    new_cache = cache_here
    for moment in range(NCH):
        is_owner = owner[moment, 0] == shard_id
        updated = lax.dynamic_update_slice(new_cache, fresh_all[moment], (0, 0, filled, 0))
        new_cache = jnp.where(is_owner, updated, new_cache)
        filled = filled + jnp.where(is_owner, SPAN, 0).astype(jnp.int32)
    return (jnp.stack(outputs)[:, None], new_cache[None])


def solution(mesh):
    in_specs = (
        P("section", "tp", "kvp"),
        P(None, "tp", "kvp"),
        P("section", None),
        P("section", None, "tp", "kvp"),
        P("section", None, "tp", "kvp"),
        P("section", "tp", "kvp"),
        P("section", None, "tp", "kvp", None),
        P("section", "kvp"),
        P(None, "section"),
    )
    out_specs = (P(None, "section", "tp", "kvp"), P("section", None, "tp", "kvp", None))
    return jax.shard_map(body, mesh=mesh, in_specs=in_specs, out_specs=out_specs, check_vma=False)
```

time: 764 us -> 194 us (0.25)
  waiting for transfers between devices: 366 us -> 42.2 us
  blocking collectives: 271 us -> 68.9 us
  other arithmetic: 69.6 us -> 1.6 us
  starting transfers between devices: 3.51 us -> 41.3 us
  matrix products: 13 us -> 0 us
  Pallas kernels: 0 us -> 10.8 us
  local copies, waits for them, and re-layouts: 19.4 us -> 11 us
    all_gather x4 -> x2, waiting for transfers between devices: 331 us -> 20.1 us  [the longest x1 20.1 us: body(): held = lax.all_gather(jnp.stack([own, got]), 'kvp', axis_index_groups=RINGS)]
    all_gather x10 -> x0, blocking collectives: 271 us -> none  [the longest x4 105 us: combined_all(): gathered = jax.tree.map(lambda a: lax.all_gather(a, axis), part)]
    all_to_all x0 -> x4, blocking collectives: none -> 68.9 us  [spread(): return lax.all_to_all(block, 'kvp', 0, 0, tiled=True)]
    add x62 -> x0, other arithmetic: 57.3 us -> none  [the longest x30 56.7 us: combine(): former_out * former_weight[..., None]]
    ppermute x1 -> x7, starting transfers between devices: 3.26 us -> 35.7 us  [the longest x4 26.7 us: swap(): return lax.ppermute(block, 'tp', [(0, 1), (1, 0)])]
    reduce_scatter x2 -> x0, waiting for transfers between devices: 29.7 us -> none  [body(): lax.psum_scatter(jnp.dot(attended, wo[0], preferred_element_type=jnp.floa...]
    ppermute x1 -> x7, waiting for transfers between devices: 4.98 us -> 19.5 us  [the longest x1 8.72 us: body(): lax.ppermute(outputs[-1], 'section', [(i, i + 1) for i in range(15)])]
    dot_general x10 -> x0, matrix products: 13 us -> none  [the longest x2 3.97 us: body(): jnp.dot(normed, wq[0, :, 0, :], preferred_element_type=jnp.float32)]
  transfers between devices with their start and end apart: 7 -> 10, of which waited for: 7 -> 8; matrix products, arithmetic and copies ran while one was open for 1% -> 2% of each run, Pallas kernels for 0% -> 3%
where the time goes in v1:
time: 194 us; the launch traced here: 192 us
  blocking collectives  68.9 us (36%)
  waiting for transfers between devices  42.2 us (22%)
  starting transfers between devices  41.3 us (21%)
  between operations  16.3 us (8%)
  local copies, waits for them, and re-layouts  11 us (6%)
  Pallas kernels  10.8 us (6%)
    all_to_all x4, blocking collectives, spread(): return lax.all_to_all(block, 'kvp', 0, 0, tiled=True)  68.9 us
    ppermute x4, starting transfers between devices, swap(): return lax.ppermute(block, 'tp', [(0, 1), (1, 0)])  26.7 us
    all_gather x1, waiting for transfers between devices, body(): held = lax.all_gather(jnp.stack([own, got]), 'kvp', axis_index_groups=RINGS)  20.1 us
    ppermute x1, waiting for transfers between devices, body(): lax.ppermute(outputs[-1], 'section', [(i, i + 1) for i in range(15)])  8.72 us
    unnamed x37, local copies, waits for them, and re-layouts  7.72 us
    all_to_all x1, starting transfers between devices, spread(): return lax.all_to_all(block, 'kvp', 0, 0, tiled=True)  5.5 us
    ppermute x1, waiting for transfers between devices, body(): pair = lax.ppermute(kv, 'kvp', [(i, (i + RING) % N) for i in range(N)])  5.15 us
    pallas_call x2, Pallas kernels, body(): pl.pallas_call(functools.partial(attend, later=moment > 0), out_shape=sha...  4.55 us
  transfers between devices with their start and end apart: 10, of which 8 were waited for; matrix products, arithmetic and copies ran while one was open for 2% of the time, Pallas kernels for 3%

profile of v1, /device:TPU:7, one launch (start us, length us, event | category | flops | bytes accessed | tf_op | source)
XLA Modules:
  0.0 192.2 jit_solution(10924406816090560867)
XLA Ops:
  7.2 1.0 copy.29
  8.4 2.6 %collective-permute-start.1 = (bf16[2,256,128]{2,1,0:T(8,128)(2,1)S(1)}, bf16[2,256,128]{2,1,0:T(8,128)(2,1)S(1)}, u32[]{:S(2)}, u32[]{:S(2)}) collective-permute-start(bf16[2,256,128]{2,1,0:T(8,128)(2,1)S(1)} %get-tuple-element.27), channel_id=1, source_target_pairs={{0,16},{2,18},{4,20},{6,22},{8,24},{10,26},{12,28},{14,30},{16,0},... | collective-permute-start | bytes 393224 | tf_op jit(solution)/shard_map/ppermute | solution.py:154
  11.0 3.8 %collective-permute-done.1 = bf16[2,256,128]{2,1,0:T(8,128)(2,1)S(1)} collective-permute-done((bf16[2,256,128]{2,1,0:T(8,128)(2,1)S(1)}, bf16[2,256,128]{2,1,0:T(8,128)(2,1)S(1)}, u32[]{:S(2)}, u32[]{:S(2)}) %collective-permute-start.1) | collective-permute-done | bytes 131104 | tf_op jit(solution)/shard_map/ppermute | solution.py:154
  15.6 19.9 %all_to_all.25.mine = bf16[16,64,256]{2,1,0:T(8,128)(2,1)} all-to-all(bf16[16,64,256]{2,1,0:T(8,128)(2,1)S(1)} %broadcast_in_dim.22), channel_id=1, replica_groups=mesh['section'=16,'kvp'=16,'tp'=2] {'kvp'}, dimensions={0} | all-to-all | bytes 1048576 | tf_op jit(solution)/shard_map/all_to_all | solution.py:131
  35.6 5.4 %collective-permute-start = (bf16[16,64,256]{2,1,0:T(8,128)(2,1)}, bf16[16,64,256]{2,1,0:T(8,128)(2,1)}, u32[]{:S(2)}, u32[]{:S(2)}) collective-permute-start(bf16[16,64,256]{2,1,0:T(8,128)(2,1)} %all_to_all.25.mine), channel_id=1, source_target_pairs={{0,1},{1,0},{2,3},{3,2},{4,5},{5,4},{6,7},{7,6},{8,9},{9,8},{10,11... | collective-permute-start | bytes 1572872 | tf_op jit(solution)/shard_map/ppermute | solution.py:135
  41.0 20.1 %all-gather.5.cloned.1.call-done = bf16[16,2,256,128]{3,2,1,0:T(8,128)(2,1)} async-done(((bf16[2,2,256,128]{3,2,1,0:T(8,128)(2,1)}), bf16[16,2,256,128]{3,2,1,0:T(8,128)(2,1)}) %all-gather.5.cloned.1.call-update) | async-done | bytes 2097168 | tf_op jit(solution)/shard_map/all_gather | solution.py:155
  61.8 1.4 copy.18.wkv
  63.2 1.3 copy-done.2
  64.6 2.3 %project_first.1 = (bf16[128,128]{1,0:T(8,128)(2,1)S(1)}, bf16[16,48,128]{2,1,0:T(8,128)(2,1)S(1)}) custom-call(s32[2]{0:T(128)S(1)} %pad_add_fusion.place, s32[1]{0:T(128)} %bitcast.42.lens, bf16[16,64,256]{2,1,0:T(8,128)(2,1)} %all_to_all.25.mine, bf16[16,64,256]{2,1,0:T(8,128)(2,1)} %collective-permute-done.other, f32[1,4096]{1,0:T(1,128)S(1)} %copy-done.11, ...), custom_call_target="tpu_custom_call" | custom-call | tf_op jit(solution)/shard_map/project_first/pallas_call | solution.py:170
  66.9 12.0 %all_to_all.26.first = bf16[16,48,128]{2,1,0:T(8,128)(2,1)S(1)} all-to-all(bf16[16,48,128]{2,1,0:T(8,128)(2,1)S(1)} %get-tuple-element.14), channel_id=1, replica_groups=mesh['section'=16,'kvp'=16,'tp'=2] {'kvp'}, dimensions={0} | all-to-all | bytes 393216 | tf_op jit(solution)/shard_map/all_to_all | solution.py:131
  78.9 1.9 attend.2
  80.8 20.1 %all_to_all.27.att = bf16[16,128,128]{2,1,0:T(8,128)(2,1)S(1)} all-to-all(bf16[16,128,128]{2,1,0:T(8,128)(2,1)S(1)} %attend.2), channel_id=1, replica_groups=mesh['section'=16,'kvp'=16,'tp'=2] {'kvp'}, dimensions={0} | all-to-all | bytes 1048576 | tf_op jit(solution)/shard_map/all_to_all | solution.py:131
  100.9 1.0 mix.2
  101.9 10.5 %collective-permute-start.2 = (f32[64,256]{1,0:T(8,128)S(1)}, f32[64,256]{1,0:T(8,128)S(1)}, u32[]{:S(2)}, u32[]{:S(2)}) collective-permute-start(f32[64,256]{1,0:T(8,128)S(1)} %get-tuple-element.16), channel_id=1, source_target_pairs={{0,1},{1,0},{2,3},{3,2},{4,5},{5,4},{6,7},{7,6},{8,9},{9,8},{10,11... | collective-permute-start | bytes 196616 | tf_op jit(solution)/shard_map/ppermute | solution.py:135
  112.4 0.9 collective-permute-done.2
  113.3 4.4 %collective-permute-start.3 = (bf16[64,256]{1,0:T(8,128)(2,1)S(1)}, bf16[64,256]{1,0:T(8,128)(2,1)S(1)}, u32[]{:S(2)}, u32[]{:S(2)}) collective-permute-start(bf16[64,256]{1,0:T(8,128)(2,1)S(1)} %add_convert_fusion.1), channel_id=1, source_target_pairs={{0,32},{32,64},{64,96},{96,128},{128,160},{160,192},{192,224},{224... | collective-permute-start | bytes 98312 | tf_op jit(solution)/shard_map/ppermute | solution.py:164
  117.7 8.7 %collective-permute-done.3 = bf16[64,256]{1,0:T(8,128)(2,1)S(1)} collective-permute-done((bf16[64,256]{1,0:T(8,128)(2,1)S(1)}, bf16[64,256]{1,0:T(8,128)(2,1)S(1)}, u32[]{:S(2)}, u32[]{:S(2)}) %collective-permute-start.3) | collective-permute-done | bytes 32800 | tf_op jit(solution)/shard_map/ppermute | solution.py:164
  126.5 16.9 %all_to_all.28.mine = bf16[16,64,256]{2,1,0:T(8,128)(2,1)S(1)} all-to-all(bf16[16,64,256]{2,1,0:T(8,128)(2,1)S(1)} %broadcast_in_dim.23), channel_id=1, replica_groups=mesh['section'=16,'kvp'=16,'tp'=2] {'kvp'}, dimensions={0} | all-to-all | bytes 1048576 | tf_op jit(solution)/shard_map/all_to_all | solution.py:131
  143.4 5.5 %collective-permute-start.4 = (bf16[16,64,256]{2,1,0:T(8,128)(2,1)S(1)}, bf16[16,64,256]{2,1,0:T(8,128)(2,1)S(1)}, u32[]{:S(2)}, u32[]{:S(2)}) collective-permute-start(bf16[16,64,256]{2,1,0:T(8,128)(2,1)S(1)} %all_to_all.28.mine), channel_id=1, source_target_pairs={{0,1},{1,0},{2,3},{3,2},{4,5},{5,4},{6,7},{7,6},{8,9},{9,8},{10,11... | collective-permute-start | bytes 1572872 | tf_op jit(solution)/shard_map/ppermute | solution.py:135
  148.9 0.8 copy-done.5
  150.4 0.8 copy-done.8
  151.2 1.0 copy-done.6
  152.2 1.6 copy-done.7
  153.8 1.0 copy-done.9
  154.9 2.0 %project_later.1 = (bf16[128,128]{1,0:T(8,128)(2,1)S(1)}, bf16[128,256]{1,0:T(8,128)(2,1)S(1)}) custom-call(s32[2]{0:T(128)S(1)} %pad_add_fusion.place, bf16[16,64,256]{2,1,0:T(8,128)(2,1)S(1)} %copy-done.6, bf16[16,64,256]{2,1,0:T(8,128)(2,1)S(1)} %copy-done.9, f32[1,4096]{1,0:T(1,128)S(1)} %copy-done.11, bf16[4096,128]{1,0:T(8,128)(2,1)S(1)} %bitcast.50, ...), custom_call_target="tpu_custom_call" | custom-call | tf_op jit(solution)/shard_map/project_later/pallas_call | solution.py:183
  156.9 2.7 %attend.3 = bf16[16,128,128]{2,1,0:T(8,128)(2,1)} custom-call(s32[2]{0:T(128)S(1)} %pad_add_fusion.place, bf16[128,128]{1,0:T(8,128)(2,1)S(1)} %get-tuple-element.18.q_ref, bf16[8,2,2,256,128]{4,3,2,1,0:T(8,128)(2,1)S(1)} %bitcast.48, bf16[16,48,128]{2,1,0:T(8,128)(2,1)S(1)} %all_to_all.26.first, bf16[128,256]{1,0:T(8,128)(2,1)S(1)} %get-tuple-element.19.rest_0_), custom_call_target="tpu_custom_call" | custom-call | tf_op jit(solution)/shard_map/attend/pallas_call | solution.py:197
  159.6 5.5 %all-to-all-start.4 = ((bf16[16,128,128]{2,1,0:T(8,128)(2,1)}), bf16[16,128,128]{2,1,0:T(8,128)(2,1)S(1)}, u32[]{:S(2)}, u32[]{:S(2)}) async-start(bf16[16,128,128]{2,1,0:T(8,128)(2,1)} %attend.3), calls=%async_computation.4 | async-start | bytes 1048576 | tf_op jit(solution)/shard_map/all_to_all | solution.py:131
  167.1 2.0 %collective-permute-start.6 = (bf16[128,256]{1,0:T(8,128)(2,1)S(1)}, bf16[128,256]{1,0:T(8,128)(2,1)S(1)}, u32[]{:S(2)}, u32[]{:S(2)}) collective-permute-start(bf16[128,256]{1,0:T(8,128)(2,1)S(1)} %get-tuple-element.19.rest_0_), channel_id=1, source_target_pairs={{0,16},{2,18},{4,20},{6,22},{8,24},{10,26},{12,28},{14,30},{16,0},... | collective-permute-start | bytes 196616 | tf_op jit(solution)/shard_map/ppermute | solution.py:193
  169.8 5.2 %collective-permute-done.6 = bf16[128,256]{1,0:T(8,128)(2,1)S(1)} collective-permute-done((bf16[128,256]{1,0:T(8,128)(2,1)S(1)}, bf16[128,256]{1,0:T(8,128)(2,1)S(1)}, u32[]{:S(2)}, u32[]{:S(2)}) %collective-permute-start.6) | collective-permute-done | bytes 65568 | tf_op jit(solution)/shard_map/ppermute | solution.py:193
  175.0 2.5 %all-to-all-done.4.att = bf16[16,128,128]{2,1,0:T(8,128)(2,1)S(1)} async-done(((bf16[16,128,128]{2,1,0:T(8,128)(2,1)}), bf16[16,128,128]{2,1,0:T(8,128)(2,1)S(1)}, u32[]{:S(2)}, u32[]{:S(2)}) %all-to-all-start.4) | async-done | bytes 524320 | tf_op jit(solution)/shard_map/all_to_all | solution.py:131
  177.5 1.0 mix.3
  178.4 5.3 %collective-permute-start.5 = (f32[64,256]{1,0:T(8,128)S(1)}, f32[64,256]{1,0:T(8,128)S(1)}, u32[]{:S(2)}, u32[]{:S(2)}) collective-permute-start(f32[64,256]{1,0:T(8,128)S(1)} %get-tuple-element.21), channel_id=1, source_target_pairs={{0,1},{1,0},{2,3},{3,2},{4,5},{5,4},{6,7},{7,6},{8,9},{9,8},{10,11... | collective-permute-start | bytes 196616 | tf_op jit(solution)/shard_map/ppermute | solution.py:135
  (59 shorter events, 4.7 us)
Async XLA Ops:
  7.2 8.4 %copy-start.10 = (bf16[1,64,256]{2,1,0:T(8,128)(2,1)S(1)}, bf16[1,64,256]{2,1,0:T(8,128)(2,1)}, u32[]{:S(2)}) copy-start(bf16[1,64,256]{2,1,0:T(8,128)(2,1)} %param.9) | copy-start | bytes 98308
  7.2 53.9 %all-gather.5.cloned.1.call-start = ((), (), s32[]{:S(2)}) async-start(), calls=%async_computation.5 | async-start | bytes 2359296 | tf_op jit(solution)/shard_map/all_gather | solution.py:155
  8.3 53.5 %copy-start.12 = (bf16[1,2,2,512,128]{4,3,2,1,0:T(8,128)(2,1)}, bf16[1,2,2,512,128]{4,3,2,1,0:T(8,128)(2,1)S(1)}, u32[]{:S(2)}) copy-start(bf16[1,2,2,512,128]{4,3,2,1,0:T(8,128)(2,1)S(1)} %copy.29) | copy-start | bytes 1572868
  8.3 53.5 %copy-start.15 = (bf16[1,4096,1,32]{1,3,2,0:T(8,128)(2,1)S(1)}, bf16[1,4096,1,32]{1,3,2,0:T(8,128)(2,1)}, u32[]{:S(2)}) copy-start(bf16[1,4096,1,32]{1,3,2,0:T(8,128)(2,1)} %param.13) | copy-start | bytes 786436
  8.3 54.9 %copy-start.1 = (bf16[1,4096,1,128]{3,1,2,0:T(8,128)(2,1)S(1)}, bf16[1,4096,1,128]{3,1,2,0:T(8,128)(2,1)}, u32[]{:S(2)}) copy-start(bf16[1,4096,1,128]{3,1,2,0:T(8,128)(2,1)} %param.12) | copy-start | bytes 3145732
  8.3 54.9 %copy-start.11 = (f32[1,4096]{1,0:T(1,128)S(1)}, f32[1,4096]{1,0:T(1,128)}, u32[]{:S(2)}) copy-start(f32[1,4096]{1,0:T(1,128)} %gain.3) | copy-start | bytes 49156
  8.4 6.4 %collective-permute-start.1 = (bf16[2,256,128]{2,1,0:T(8,128)(2,1)S(1)}, bf16[2,256,128]{2,1,0:T(8,128)(2,1)S(1)}, u32[]{:S(2)}, u32[]{:S(2)}) collective-permute-start(bf16[2,256,128]{2,1,0:T(8,128)(2,1)S(1)} %get-tuple-element.27), channel_id=1, source_target_pairs={{0,16},{2,18},{4,20},{6,22},{8,24},{10,26},{12,28},{14,30},{16,0},... | collective-permute-start | bytes 393224 | tf_op jit(solution)/shard_map/ppermute | solution.py:154
  15.5 135.7 %all-gather.7.cloned.1.call-start = ((), (), s32[]{:S(2)}) async-start(), calls=%async_computation.6 | async-start | bytes 2359296 | tf_op jit(solution)/shard_map/all_gather | solution.py:158
  35.6 27.7 %collective-permute-start = (bf16[16,64,256]{2,1,0:T(8,128)(2,1)}, bf16[16,64,256]{2,1,0:T(8,128)(2,1)}, u32[]{:S(2)}, u32[]{:S(2)}) collective-permute-start(bf16[16,64,256]{2,1,0:T(8,128)(2,1)} %all_to_all.25.mine), channel_id=1, source_target_pairs={{0,1},{1,0},{2,3},{3,2},{4,5},{5,4},{6,7},{7,6},{8,9},{9,8},{10,11... | collective-permute-start | bytes 1572872 | tf_op jit(solution)/shard_map/ppermute | solution.py:135
  63.1 15.8 %copy-start = (bf16[16,2,256,128]{3,2,1,0:T(8,128)(2,1)S(1)}, bf16[16,2,256,128]{3,2,1,0:T(8,128)(2,1)}, u32[]{:S(2)}) copy-start(bf16[16,2,256,128]{3,2,1,0:T(8,128)(2,1)} %all-gather.5.cloned.1.call-done) | copy-start | bytes 6291460
  63.2 1.4 copy-start.2
  66.9 34.0 %copy-start.3 = (bf16[1,2048,256]{2,1,0:T(8,128)(2,1)S(1)}, bf16[1,2048,256]{2,1,0:T(8,128)(2,1)}, u32[]{:S(2)}) copy-start(bf16[1,2048,256]{2,1,0:T(8,128)(2,1)} %param.14) | copy-start | bytes 3145732
  80.8 45.6 %copy-start.16 = (bf16[1,64,256]{2,1,0:T(8,128)(2,1)S(1)}, bf16[1,64,256]{2,1,0:T(8,128)(2,1)}, u32[]{:S(2)}) copy-start(bf16[1,64,256]{2,1,0:T(8,128)(2,1)} %param.10) | copy-start | bytes 98308
  101.9 11.4 %collective-permute-start.2 = (f32[64,256]{1,0:T(8,128)S(1)}, f32[64,256]{1,0:T(8,128)S(1)}, u32[]{:S(2)}, u32[]{:S(2)}) collective-permute-start(f32[64,256]{1,0:T(8,128)S(1)} %get-tuple-element.16), channel_id=1, source_target_pairs={{0,1},{1,0},{2,3},{3,2},{4,5},{5,4},{6,7},{7,6},{8,9},{9,8},{10,11... | collective-permute-start | bytes 196616 | tf_op jit(solution)/shard_map/ppermute | solution.py:135
  113.3 13.1 %collective-permute-start.3 = (bf16[64,256]{1,0:T(8,128)(2,1)S(1)}, bf16[64,256]{1,0:T(8,128)(2,1)S(1)}, u32[]{:S(2)}, u32[]{:S(2)}) collective-permute-start(bf16[64,256]{1,0:T(8,128)(2,1)S(1)} %add_convert_fusion.1), channel_id=1, source_target_pairs={{0,32},{32,64},{64,96},{96,128},{128,160},{160,192},{192,224},{224... | collective-permute-start | bytes 98312 | tf_op jit(solution)/shard_map/ppermute | solution.py:164
  143.4 7.0 %collective-permute-start.4 = (bf16[16,64,256]{2,1,0:T(8,128)(2,1)S(1)}, bf16[16,64,256]{2,1,0:T(8,128)(2,1)S(1)}, u32[]{:S(2)}, u32[]{:S(2)}) collective-permute-start(bf16[16,64,256]{2,1,0:T(8,128)(2,1)S(1)} %all_to_all.28.mine), channel_id=1, source_target_pairs={{0,1},{1,0},{2,3},{3,2},{4,5},{5,4},{6,7},{7,6},{8,9},{9,8},{10,11... | collective-permute-start | bytes 1572872 | tf_op jit(solution)/shard_map/ppermute | solution.py:135
  148.9 0.8 copy-start.5
  150.4 0.8 copy-start.8
  151.2 1.0 copy-start.6
  152.2 1.6 copy-start.7
  153.8 1.0 copy-start.9
  156.9 8.2 %copy-start.17 = (s32[2,1]{0,1:T(1,128)S(1)}, s32[2,1]{0,1:T(1,128)}, u32[]{:S(2)}) copy-start(s32[2,1]{0,1:T(1,128)} %param.17) | copy-start | bytes 28
  156.9 12.3 %copy-start.13 = (bf16[1,2,2,512,128]{4,3,2,1,0:T(8,128)(2,1)S(1)}, bf16[1,2,2,512,128]{4,3,2,1,0:T(8,128)(2,1)}, u32[]{:S(2)}) copy-start(bf16[1,2,2,512,128]{4,3,2,1,0:T(8,128)(2,1)} %copy-done.12) | copy-start | bytes 1572868
  159.6 17.9 %copy-start.4 = (bf16[1,2048,256]{2,1,0:T(8,128)(2,1)S(1)}, bf16[1,2048,256]{2,1,0:T(8,128)(2,1)}, u32[]{:S(2)}) copy-start(bf16[1,2048,256]{2,1,0:T(8,128)(2,1)} %param.14) | copy-start | bytes 3145732
  159.6 17.9 %all-to-all-start.4 = ((bf16[16,128,128]{2,1,0:T(8,128)(2,1)}), bf16[16,128,128]{2,1,0:T(8,128)(2,1)S(1)}, u32[]{:S(2)}, u32[]{:S(2)}) async-start(bf16[16,128,128]{2,1,0:T(8,128)(2,1)} %attend.3), calls=%async_computation.4 | async-start | bytes 1048576 | tf_op jit(solution)/shard_map/all_to_all | solution.py:131
  167.1 7.8 %collective-permute-start.6 = (bf16[128,256]{1,0:T(8,128)(2,1)S(1)}, bf16[128,256]{1,0:T(8,128)(2,1)S(1)}, u32[]{:S(2)}, u32[]{:S(2)}) collective-permute-start(bf16[128,256]{1,0:T(8,128)(2,1)S(1)} %get-tuple-element.19.rest_0_), channel_id=1, source_target_pairs={{0,16},{2,18},{4,20},{6,22},{8,24},{10,26},{12,28},{14,30},{16,0},... | collective-permute-start | bytes 196616 | tf_op jit(solution)/shard_map/ppermute | solution.py:193
  178.4 6.2 %collective-permute-start.5 = (f32[64,256]{1,0:T(8,128)S(1)}, f32[64,256]{1,0:T(8,128)S(1)}, u32[]{:S(2)}, u32[]{:S(2)}) collective-permute-start(f32[64,256]{1,0:T(8,128)S(1)} %get-tuple-element.21), channel_id=1, source_target_pairs={{0,1},{1,0},{2,3},{3,2},{4,5},{5,4},{6,7},{7,6},{8,9},{9,8},{10,11... | collective-permute-start | bytes 196616 | tf_op jit(solution)/shard_map/ppermute | solution.py:135
  184.4 0.9 copy-start.14
Sparse Core Ops, SparseCore 0:
  15.6 45.4 all-gather.4
  63.2 54.4 all-gather.6

commit v2 on v1

--- a/solution.py
+++ b/solution.py
@@ -53,16 +53,19 @@
 def project_first(place, lens, mine, other, gain, wq, wkv, q_out, kv_out, normed):
     normalise(place, mine, other, gain, normed)
     q_out[...] = dot(normed[...], wq[...]).astype(BF16)
-    kv = dot(normed[...], wkv[...]).T.astype(BF16)
+    kv = dot_t(wkv[...], normed[...]).astype(BF16)
     filled = jnp.full((16, SPAN), lens[0].astype(F32), F32).astype(BF16)
     for j in range(N):
         kv_out[j, 0:32] = kv
         kv_out[j, 32:48] = filled
 
 
-def project_later(place, mine, other, gain, wq, wkv, q_out, kv_out, normed):
+def project_later(place, mine, other, gain, wq, wkv_hbm, q_out, kv_out, normed, wkv, sem):
+    copy = pltpu.make_async_copy(wkv_hbm, wkv, sem)
+    copy.start()
     normalise(place, mine, other, gain, normed)
     q_out[...] = dot(normed[...], wq[...]).astype(BF16)
+    copy.wait()
     kv_out[...] = dot_t(normed[...], wkv[...]).astype(BF16)
 
 
@@ -135,6 +138,11 @@
     return lax.ppermute(block, "tp", [(0, 1), (1, 0)])
 
 
+def onward(block, cross):
+    route = [(i, (i ^ cross) + 2) for i in range(30)]
+    return lax.ppermute(block, ("section", "tp"), route)
+
+
 def shape(*dims, dtype=BF16):
     return jax.ShapeDtypeStruct(dims, dtype)
 
@@ -154,14 +162,13 @@
     got = lax.ppermute(give, "kvp", [(i, (i + RING) % N) for i in range(N)])
     held = lax.all_gather(jnp.stack([own, got]), "kvp", axis_index_groups=RINGS)
 
-    wkv_t, held = lax.optimization_barrier((wkv_here.T, held))
-    wkv_all = lax.all_gather(wkv_t, "kvp", axis_index_groups=RINGS).reshape(2 * HD, D)
-
-    outputs, fresh_all = [], []
+    wkv_t = wkv_here.T
+
+    sums, fresh_all = [], []
     x = entering[0]
     for moment in range(NCH):
         if moment:
-            passed = lax.ppermute(outputs[-1], "section", [(i, i + 1) for i in range(15)])
+            passed = (onward(own_sum, 0) + onward(other_sum, 1)).astype(BF16)
             x = jnp.where(section_id == 0, feed[moment - 1], passed)
         mine = spread(jnp.broadcast_to(x[None], (N, ROWS, COLS)))
         other = swap(mine)
@@ -175,21 +182,26 @@
                 scratch_shapes=scratch,
                 compiler_params=PARAMS,
                 name="project_first",
-            )(place, filled[None], mine, other, gain, wq_here, wkv_here)
+            )(place, filled[None], mine, other, gain, wq_here, wkv_t)
             first = spread(kv)
+            wkv_late, first = lax.optimization_barrier((wkv_t, first))
+            wkv_all = lax.all_gather(wkv_late, "kvp", axis_index_groups=RINGS)
+            wkv_all = wkv_all.reshape(2 * HD, D)
             extra = (first,)
             both = jnp.transpose(first[:, 0:32].reshape(2, 2, HD, SPAN), (1, 0, 3, 2))
         else:
             q, kv = pl.pallas_call(
                 project_later,
                 out_shape=(shape(SPAN, HD), shape(SPAN, 2 * HD)),
-                in_specs=[SMEM] + [VMEM] * 5,
+                in_specs=[SMEM] + [VMEM] * 4 + [pl.BlockSpec(memory_space=pl.ANY)],
                 out_specs=(VMEM, VMEM),
-                scratch_shapes=scratch,
+                scratch_shapes=scratch + [pltpu.VMEM((2 * HD, D), BF16), pltpu.SemaphoreType.DMA],
                 compiler_params=PARAMS,
                 name="project_later",
             )(place, mine, other, gain, wq_here, wkv_all)
             extra = (first, kv)
+            late, kv = lax.optimization_barrier((sums[0], kv))
+            sums[0] = late
             pair = lax.ppermute(kv, "kvp", [(i, (i + RING) % N) for i in range(N)])
             heads = jnp.where(g == 0, jnp.stack([kv, pair]), jnp.stack([pair, kv]))
             both = jnp.transpose(heads.reshape(2, SPAN, 2, HD), (2, 0, 1, 3))
@@ -212,8 +224,9 @@
             compiler_params=PARAMS,
             name="mix",
         )(place, att, wo_here, x)
-        outputs.append((own_sum + swap(other_sum)).astype(BF16))
-
+        sums.append((own_sum, other_sum))
+
+    outputs = [(own + swap(other)).astype(BF16) for own, other in sums]
     new_cache = cache_here
     for moment in range(NCH):
         is_owner = owner[moment, 0] == shard_id

time: 194 us -> 176 us (0.907)
  waiting for transfers between devices: 42.2 us -> 27.2 us
  local copies, waits for them, and re-layouts: 11 us -> 8.23 us
    all_gather x1, waiting for transfers between devices: 20.1 us -> 4.61 us  [body(): held = lax.all_gather(jnp.stack([own, got]), 'kvp', axis_index_groups=RINGS)]
    ppermute x4, starting transfers between devices: 26.7 us -> 15.7 us  [swap(): return lax.ppermute(block, 'tp', [(0, 1), (1, 0)])]
    ppermute x1 -> x2, starting transfers between devices: 4.4 us -> 14.1 us  [onward(): return lax.ppermute(block, ('section', 'tp'), route)]
    ppermute x1 -> x2, waiting for transfers between devices: 8.72 us -> 10.7 us  [onward(): return lax.ppermute(block, ('section', 'tp'), route)]
    unnamed x37 -> x35, local copies, waits for them, and re-layouts: 7.72 us -> 6.21 us
  transfers between devices with their start and end apart: 10 -> 11, of which waited for: 8 -> 9; matrix products, arithmetic and copies ran while one was open for 2% -> 2% of each run, Pallas kernels for 3% -> 3%
where the time goes in v2:
time: 176 us; the launch traced here: 175 us
  blocking collectives  69.5 us (39%)
  starting transfers between devices  39.9 us (23%)
  waiting for transfers between devices  27.2 us (15%)
  between operations  16.4 us (9%)
  Pallas kernels  11 us (6%)
  local copies, waits for them, and re-layouts  8.23 us (5%)
  other arithmetic  2.37 us (1%)
    all_to_all x4, blocking collectives, spread(): return lax.all_to_all(block, 'kvp', 0, 0, tiled=True)  69.5 us
    ppermute x4, starting transfers between devices, swap(): return lax.ppermute(block, 'tp', [(0, 1), (1, 0)])  15.7 us
    ppermute x2, starting transfers between devices, onward(): return lax.ppermute(block, ('section', 'tp'), route)  14.1 us
    ppermute x2, waiting for transfers between devices, onward(): return lax.ppermute(block, ('section', 'tp'), route)  10.7 us
    unnamed x35, local copies, waits for them, and re-layouts  6.21 us
    all_to_all x1, starting transfers between devices, spread(): return lax.all_to_all(block, 'kvp', 0, 0, tiled=True)  5.63 us
    all_gather x1, waiting for transfers between devices, body(): held = lax.all_gather(jnp.stack([own, got]), 'kvp', axis_index_groups=RINGS)  4.61 us
    pallas_call x2, Pallas kernels, body(): pl.pallas_call(functools.partial(attend, later=moment > 0), out_shape=sha...  4.57 us
  transfers between devices with their start and end apart: 11, of which 9 were waited for; matrix products, arithmetic and copies ran while one was open for 2% of the time, Pallas kernels for 3%

profile of v2, /device:TPU:7, one launch (start us, length us, event | category | flops | bytes accessed | tf_op | source)
XLA Modules:
  0.0 174.5 jit_solution(7929946741333504979)
XLA Ops:
  7.2 1.1 copy.27
  8.5 2.5 %collective-permute-start.1 = (bf16[2,256,128]{2,1,0:T(8,128)(2,1)S(1)}, bf16[2,256,128]{2,1,0:T(8,128)(2,1)S(1)}, u32[]{:S(2)}, u32[]{:S(2)}) collective-permute-start(bf16[2,256,128]{2,1,0:T(8,128)(2,1)S(1)} %get-tuple-element.33), channel_id=1, source_target_pairs={{0,16},{2,18},{4,20},{6,22},{8,24},{10,26},{12,28},{14,30},{16,0},... | collective-permute-start | bytes 393224 | tf_op jit(solution)/shard_map/ppermute | solution.py:162
  10.9 3.8 %collective-permute-done.1 = bf16[2,256,128]{2,1,0:T(8,128)(2,1)S(1)} collective-permute-done((bf16[2,256,128]{2,1,0:T(8,128)(2,1)S(1)}, bf16[2,256,128]{2,1,0:T(8,128)(2,1)S(1)}, u32[]{:S(2)}, u32[]{:S(2)}) %collective-permute-start.1) | collective-permute-done | bytes 131104 | tf_op jit(solution)/shard_map/ppermute | solution.py:162
  15.6 19.8 %all_to_all.25.mine = bf16[16,64,256]{2,1,0:T(8,128)(2,1)S(1)} all-to-all(bf16[16,64,256]{2,1,0:T(8,128)(2,1)S(1)} %broadcast_in_dim.22), channel_id=1, replica_groups=mesh['section'=16,'kvp'=16,'tp'=2] {'kvp'}, dimensions={0} | all-to-all | bytes 1048576 | tf_op jit(solution)/shard_map/all_to_all | solution.py:134
  35.4 5.4 %collective-permute-start = (bf16[16,64,256]{2,1,0:T(8,128)(2,1)S(1)}, bf16[16,64,256]{2,1,0:T(8,128)(2,1)S(1)}, u32[]{:S(2)}, u32[]{:S(2)}) collective-permute-start(bf16[16,64,256]{2,1,0:T(8,128)(2,1)S(1)} %all_to_all.25.mine), channel_id=1, source_target_pairs={{0,1},{1,0},{2,3},{3,2},{4,5},{5,4},{6,7},{7,6},{8,9},{9,8},{10,11... | collective-permute-start | bytes 1572872 | tf_op jit(solution)/shard_map/ppermute | solution.py:138
  41.6 0.8 collective-permute-done.other
  42.4 0.8 copy-done.7
  43.2 1.0 copy-done.8
  44.2 1.6 project_first.1
  45.8 14.9 %all_to_all.26.first = bf16[16,48,128]{2,1,0:T(8,128)(2,1)S(1)} all-to-all(bf16[16,48,128]{2,1,0:T(8,128)(2,1)S(1)} %get-tuple-element.16), channel_id=1, replica_groups=mesh['section'=16,'kvp'=16,'tp'=2] {'kvp'}, dimensions={0} | all-to-all | bytes 393216 | tf_op jit(solution)/shard_map/all_to_all | solution.py:134
  60.7 4.6 %all-gather.5.cloned.1.call-done = bf16[16,2,256,128]{3,2,1,0:T(8,128)(2,1)} async-done(((bf16[2,2,256,128]{3,2,1,0:T(8,128)(2,1)}), bf16[16,2,256,128]{3,2,1,0:T(8,128)(2,1)}) %all-gather.5.cloned.1.call-update) | async-done | bytes 2097168 | tf_op jit(solution)/shard_map/all_gather | solution.py:163
  65.3 1.6 copy-done
  66.9 1.9 %attend.2 = bf16[16,128,128]{2,1,0:T(8,128)(2,1)S(1)} custom-call(s32[2]{0:T(128)S(1)} %pad_add_fusion.place, bf16[128,128]{1,0:T(8,128)(2,1)S(1)} %get-tuple-element.15.q_ref, bf16[8,2,2,256,128]{4,3,2,1,0:T(8,128)(2,1)S(1)} %bitcast.48, bf16[16,48,128]{2,1,0:T(8,128)(2,1)S(1)} %all_to_all.26.first), custom_call_target="tpu_custom_call" | custom-call | tf_op jit(solution)/shard_map/attend/pallas_call | solution.py:209
  68.8 15.1 %all_to_all.27.att = bf16[16,128,128]{2,1,0:T(8,128)(2,1)S(1)} all-to-all(bf16[16,128,128]{2,1,0:T(8,128)(2,1)S(1)} %attend.2), channel_id=1, replica_groups=mesh['section'=16,'kvp'=16,'tp'=2] {'kvp'}, dimensions={0} | all-to-all | bytes 1048576 | tf_op jit(solution)/shard_map/all_to_all | solution.py:134
  83.8 1.0 mix.2
  84.8 2.9 %collective-permute-start.2 = (f32[64,256]{1,0:T(8,128)S(1)}, f32[64,256]{1,0:T(8,128)S(1)}, u32[]{:S(2)}, u32[]{:S(2)}) collective-permute-start(f32[64,256]{1,0:T(8,128)S(1)} %get-tuple-element.22), channel_id=1, source_target_pairs={{0,32},{1,33},{32,64},{33,65},{64,96},{65,97},{96,128},{97,129},{1... | collective-permute-start | bytes 196616 | tf_op jit(solution)/shard_map/ppermute | solution.py:143
  87.7 11.3 %collective-permute-start.3 = (f32[64,256]{1,0:T(8,128)S(1)}, f32[64,256]{1,0:T(8,128)S(1)}, u32[]{:S(2)}, u32[]{:S(2)}) collective-permute-start(f32[64,256]{1,0:T(8,128)S(1)} %get-tuple-element.23), channel_id=1, source_target_pairs={{0,33},{1,32},{32,65},{33,64},{64,97},{65,96},{96,129},{97,128},{1... | collective-permute-start | bytes 196616 | tf_op jit(solution)/shard_map/ppermute | solution.py:143
  99.3 10.3 %collective-permute-done.3 = f32[64,256]{1,0:T(8,128)S(1)} collective-permute-done((f32[64,256]{1,0:T(8,128)S(1)}, f32[64,256]{1,0:T(8,128)S(1)}, u32[]{:S(2)}, u32[]{:S(2)}) %collective-permute-start.3) | collective-permute-done | bytes 65568 | tf_op jit(solution)/shard_map/ppermute | solution.py:143
  109.7 0.8 fusion.3.x_ref
  110.5 19.7 %all_to_all.28.mine = bf16[16,64,256]{2,1,0:T(8,128)(2,1)} all-to-all(bf16[16,64,256]{2,1,0:T(8,128)(2,1)S(1)} %broadcast_in_dim.23), channel_id=1, replica_groups=mesh['section'=16,'kvp'=16,'tp'=2] {'kvp'}, dimensions={0} | all-to-all | bytes 1048576 | tf_op jit(solution)/shard_map/all_to_all | solution.py:134
  130.2 2.0 %collective-permute-start.4 = (bf16[16,64,256]{2,1,0:T(8,128)(2,1)}, bf16[16,64,256]{2,1,0:T(8,128)(2,1)}, u32[]{:S(2)}, u32[]{:S(2)}) collective-permute-start(bf16[16,64,256]{2,1,0:T(8,128)(2,1)} %all_to_all.28.mine), channel_id=1, source_target_pairs={{0,1},{1,0},{2,3},{3,2},{4,5},{5,4},{6,7},{7,6},{8,9},{9,8},{10,11... | collective-permute-start | bytes 1572872 | tf_op jit(solution)/shard_map/ppermute | solution.py:138
  132.3 2.2 %collective-permute-done.4.other = bf16[16,64,256]{2,1,0:T(8,128)(2,1)} collective-permute-done((bf16[16,64,256]{2,1,0:T(8,128)(2,1)}, bf16[16,64,256]{2,1,0:T(8,128)(2,1)}, u32[]{:S(2)}, u32[]{:S(2)}) %collective-permute-start.4) | collective-permute-done | bytes 524320 | tf_op jit(solution)/shard_map/ppermute | solution.py:138
  134.5 1.6 copy-done.5
  136.1 3.0 %project_later.1 = (bf16[128,128]{1,0:T(8,128)(2,1)S(1)}, bf16[128,256]{1,0:T(8,128)(2,1)S(1)}) custom-call(s32[2]{0:T(128)S(1)} %pad_add_fusion.place, bf16[16,64,256]{2,1,0:T(8,128)(2,1)} %all_to_all.28.mine, bf16[16,64,256]{2,1,0:T(8,128)(2,1)} %collective-permute-done.4.other, f32[1,4096]{1,0:T(1,128)S(1)} %copy-done.10, bf16[4096,128]{1,0:T(8,128)(2,1)S(1)} %bitcast.51, ...), custom_call_target="tpu_custom_call" | custom-call | tf_op jit(solution)/shard_map/project_later/pallas_call | solution.py:193
  139.1 2.7 %attend.3 = bf16[16,128,128]{2,1,0:T(8,128)(2,1)} custom-call(s32[2]{0:T(128)S(1)} %pad_add_fusion.place, bf16[128,128]{1,0:T(8,128)(2,1)S(1)} %get-tuple-element.24.q_ref, bf16[8,2,2,256,128]{4,3,2,1,0:T(8,128)(2,1)S(1)} %bitcast.49, bf16[16,48,128]{2,1,0:T(8,128)(2,1)S(1)} %all_to_all.26.first, bf16[128,256]{1,0:T(8,128)(2,1)S(1)} %get-tuple-element.27.rest_0_), custom_call_target="tpu_custom_call" | custom-call | tf_op jit(solution)/shard_map/attend/pallas_call | solution.py:209
  141.8 5.6 %all-to-all-start.4 = ((bf16[16,128,128]{2,1,0:T(8,128)(2,1)}), bf16[16,128,128]{2,1,0:T(8,128)(2,1)S(1)}, u32[]{:S(2)}, u32[]{:S(2)}) async-start(bf16[16,128,128]{2,1,0:T(8,128)(2,1)} %attend.3), calls=%async_computation.4 | async-start | bytes 1048576 | tf_op jit(solution)/shard_map/all_to_all | solution.py:134
  149.5 2.9 %collective-permute-start.5 = (f32[64,256]{1,0:T(8,128)S(1)}, f32[64,256]{1,0:T(8,128)S(1)}, u32[]{:S(2)}, u32[]{:S(2)}) collective-permute-start(f32[64,256]{1,0:T(8,128)S(1)} %copy-done.12), channel_id=1, source_target_pairs={{0,1},{1,0},{2,3},{3,2},{4,5},{5,4},{6,7},{7,6},{8,9},{9,8},{10,11... | collective-permute-start | bytes 196616 | tf_op jit(solution)/shard_map/ppermute | solution.py:138
  152.4 1.9 %collective-permute-start.7 = (bf16[128,256]{1,0:T(8,128)(2,1)S(1)}, bf16[128,256]{1,0:T(8,128)(2,1)S(1)}, u32[]{:S(2)}, u32[]{:S(2)}) collective-permute-start(bf16[128,256]{1,0:T(8,128)(2,1)S(1)} %get-tuple-element.27.rest_0_), channel_id=1, source_target_pairs={{0,16},{2,18},{4,20},{6,22},{8,24},{10,26},{12,28},{14,30},{16,0},... | collective-permute-start | bytes 196616 | tf_op jit(solution)/shard_map/ppermute | solution.py:205
  155.0 3.7 %collective-permute-done.7 = bf16[128,256]{1,0:T(8,128)(2,1)S(1)} collective-permute-done((bf16[128,256]{1,0:T(8,128)(2,1)S(1)}, bf16[128,256]{1,0:T(8,128)(2,1)S(1)}, u32[]{:S(2)}, u32[]{:S(2)}) %collective-permute-start.7) | collective-permute-done | bytes 65568 | tf_op jit(solution)/shard_map/ppermute | solution.py:205
  158.7 1.1 all-to-all-done.4.att
  159.8 1.0 mix.3
  160.8 5.4 %collective-permute-start.6 = (f32[64,256]{1,0:T(8,128)S(1)}, f32[64,256]{1,0:T(8,128)S(1)}, u32[]{:S(2)}, u32[]{:S(2)}) collective-permute-start(f32[64,256]{1,0:T(8,128)S(1)} %get-tuple-element.26), channel_id=1, source_target_pairs={{0,1},{1,0},{2,3},{3,2},{4,5},{5,4},{6,7},{7,6},{8,9},{9,8},{10,11... | collective-permute-start | bytes 196616 | tf_op jit(solution)/shard_map/ppermute | solution.py:138
  (58 shorter events, 4.5 us)
Async XLA Ops:
  7.2 8.4 %copy-start.9 = (bf16[1,64,256]{2,1,0:T(8,128)(2,1)S(1)}, bf16[1,64,256]{2,1,0:T(8,128)(2,1)}, u32[]{:S(2)}) copy-start(bf16[1,64,256]{2,1,0:T(8,128)(2,1)} %param.9) | copy-start | bytes 98308
  7.2 36.0 %copy-start.10 = (f32[1,4096]{1,0:T(1,128)S(1)}, f32[1,4096]{1,0:T(1,128)}, u32[]{:S(2)}) copy-start(f32[1,4096]{1,0:T(1,128)} %gain.3) | copy-start | bytes 49156
  7.2 36.0 %copy-start.2 = (bf16[1,4096,1,128]{3,1,2,0:T(8,128)(2,1)S(1)}, bf16[1,4096,1,128]{3,1,2,0:T(8,128)(2,1)}, u32[]{:S(2)}) copy-start(bf16[1,4096,1,128]{3,1,2,0:T(8,128)(2,1)} %param.12) | copy-start | bytes 3145732
  7.2 36.0 %copy-start.6 = (bf16[1,4096,1,32]{1,3,2,0:T(8,128)(2,1)S(1)}, bf16[1,4096,1,32]{1,3,2,0:T(8,128)(2,1)}, u32[]{:S(2)}) copy-start(bf16[1,4096,1,32]{1,3,2,0:T(8,128)(2,1)} %param.13) | copy-start | bytes 786436
  7.2 58.1 %all-gather.5.cloned.1.call-start = ((), (), s32[]{:S(2)}) async-start(), calls=%async_computation.5 | async-start | bytes 2359296 | tf_op jit(solution)/shard_map/all_gather | solution.py:163
  8.4 7.2 %copy-start.13 = (bf16[1,2,2,512,128]{4,3,2,1,0:T(8,128)(2,1)}, bf16[1,2,2,512,128]{4,3,2,1,0:T(8,128)(2,1)S(1)}, u32[]{:S(2)}) copy-start(bf16[1,2,2,512,128]{4,3,2,1,0:T(8,128)(2,1)S(1)} %copy.27) | copy-start | bytes 1572868
  8.5 6.3 %collective-permute-start.1 = (bf16[2,256,128]{2,1,0:T(8,128)(2,1)S(1)}, bf16[2,256,128]{2,1,0:T(8,128)(2,1)S(1)}, u32[]{:S(2)}, u32[]{:S(2)}) collective-permute-start(bf16[2,256,128]{2,1,0:T(8,128)(2,1)S(1)} %get-tuple-element.33), channel_id=1, source_target_pairs={{0,16},{2,18},{4,20},{6,22},{8,24},{10,26},{12,28},{14,30},{16,0},... | collective-permute-start | bytes 393224 | tf_op jit(solution)/shard_map/ppermute | solution.py:162
  15.5 116.8 %all-gather.7.cloned.1.call-start = ((), (), s32[]{:S(2)}) async-start(), calls=%async_computation.6 | async-start | bytes 2359296 | tf_op jit(solution)/shard_map/all_gather | solution.py:188
  35.4 6.9 %collective-permute-start = (bf16[16,64,256]{2,1,0:T(8,128)(2,1)S(1)}, bf16[16,64,256]{2,1,0:T(8,128)(2,1)S(1)}, u32[]{:S(2)}, u32[]{:S(2)}) collective-permute-start(bf16[16,64,256]{2,1,0:T(8,128)(2,1)S(1)} %all_to_all.25.mine), channel_id=1, source_target_pairs={{0,1},{1,0},{2,3},{3,2},{4,5},{5,4},{6,7},{7,6},{8,9},{9,8},{10,11... | collective-permute-start | bytes 1572872 | tf_op jit(solution)/shard_map/ppermute | solution.py:138
  42.4 0.8 copy-start.7
  43.2 1.0 copy-start.8
  44.2 39.6 %copy-start.3 = (bf16[1,2048,256]{2,1,0:T(8,128)(2,1)S(1)}, bf16[1,2048,256]{2,1,0:T(8,128)(2,1)}, u32[]{:S(2)}) copy-start(bf16[1,2048,256]{2,1,0:T(8,128)(2,1)} %param.14) | copy-start | bytes 3145732
  65.3 1.6 copy-start
  84.8 47.5 %copy-start.11 = (f32[64,256]{1,0:T(8,128)}, f32[64,256]{1,0:T(8,128)S(1)}, u32[]{:S(2)}) copy-start(f32[64,256]{1,0:T(8,128)S(1)} %get-tuple-element.23) | copy-start | bytes 196612
  84.8 14.5 %collective-permute-start.2 = (f32[64,256]{1,0:T(8,128)S(1)}, f32[64,256]{1,0:T(8,128)S(1)}, u32[]{:S(2)}, u32[]{:S(2)}) collective-permute-start(f32[64,256]{1,0:T(8,128)S(1)} %get-tuple-element.22), channel_id=1, source_target_pairs={{0,32},{1,33},{32,64},{33,65},{64,96},{65,97},{96,128},{97,129},{1... | collective-permute-start | bytes 196616 | tf_op jit(solution)/shard_map/ppermute | solution.py:143
  87.7 22.0 %collective-permute-start.3 = (f32[64,256]{1,0:T(8,128)S(1)}, f32[64,256]{1,0:T(8,128)S(1)}, u32[]{:S(2)}, u32[]{:S(2)}) collective-permute-start(f32[64,256]{1,0:T(8,128)S(1)} %get-tuple-element.23), channel_id=1, source_target_pairs={{0,33},{1,32},{32,65},{33,64},{64,97},{65,96},{96,129},{97,128},{1... | collective-permute-start | bytes 196616 | tf_op jit(solution)/shard_map/ppermute | solution.py:143
  130.2 8.9 %copy-start.1 = (bf16[16,2,256,128]{3,2,1,0:T(8,128)(2,1)S(1)}, bf16[16,2,256,128]{3,2,1,0:T(8,128)(2,1)}, u32[]{:S(2)}) copy-start(bf16[16,2,256,128]{3,2,1,0:T(8,128)(2,1)} %all-gather.5.cloned.1.call-done) | copy-start | bytes 6291460
  130.2 4.3 %collective-permute-start.4 = (bf16[16,64,256]{2,1,0:T(8,128)(2,1)}, bf16[16,64,256]{2,1,0:T(8,128)(2,1)}, u32[]{:S(2)}, u32[]{:S(2)}) collective-permute-start(bf16[16,64,256]{2,1,0:T(8,128)(2,1)} %all_to_all.28.mine), channel_id=1, source_target_pairs={{0,1},{1,0},{2,3},{3,2},{4,5},{5,4},{6,7},{7,6},{8,9},{9,8},{10,11... | collective-permute-start | bytes 1572872 | tf_op jit(solution)/shard_map/ppermute | solution.py:138
  134.5 1.6 copy-start.5
  139.1 8.4 %copy-start.16 = (s32[2,1]{0,1:T(1,128)S(1)}, s32[2,1]{0,1:T(1,128)}, u32[]{:S(2)}) copy-start(s32[2,1]{0,1:T(1,128)} %param.17) | copy-start | bytes 28
  139.1 10.5 %copy-start.12 = (f32[64,256]{1,0:T(8,128)S(1)}, f32[64,256]{1,0:T(8,128)}, u32[]{:S(2)}) copy-start(f32[64,256]{1,0:T(8,128)} %copy-done.11) | copy-start | bytes 196612
  139.1 15.2 %copy-start.14 = (bf16[1,2,2,512,128]{4,3,2,1,0:T(8,128)(2,1)S(1)}, bf16[1,2,2,512,128]{4,3,2,1,0:T(8,128)(2,1)}, u32[]{:S(2)}) copy-start(bf16[1,2,2,512,128]{4,3,2,1,0:T(8,128)(2,1)} %copy-done.13) | copy-start | bytes 1572868
  141.8 18.0 %copy-start.4 = (bf16[1,2048,256]{2,1,0:T(8,128)(2,1)S(1)}, bf16[1,2048,256]{2,1,0:T(8,128)(2,1)}, u32[]{:S(2)}) copy-start(bf16[1,2048,256]{2,1,0:T(8,128)(2,1)} %param.14) | copy-start | bytes 3145732
  141.8 18.0 %all-to-all-start.4 = ((bf16[16,128,128]{2,1,0:T(8,128)(2,1)}), bf16[16,128,128]{2,1,0:T(8,128)(2,1)S(1)}, u32[]{:S(2)}, u32[]{:S(2)}) async-start(bf16[16,128,128]{2,1,0:T(8,128)(2,1)} %attend.3), calls=%async_computation.4 | async-start | bytes 1048576 | tf_op jit(solution)/shard_map/all_to_all | solution.py:134
  149.5 9.2 %collective-permute-start.5 = (f32[64,256]{1,0:T(8,128)S(1)}, f32[64,256]{1,0:T(8,128)S(1)}, u32[]{:S(2)}, u32[]{:S(2)}) collective-permute-start(f32[64,256]{1,0:T(8,128)S(1)} %copy-done.12), channel_id=1, source_target_pairs={{0,1},{1,0},{2,3},{3,2},{4,5},{5,4},{6,7},{7,6},{8,9},{9,8},{10,11... | collective-permute-start | bytes 196616 | tf_op jit(solution)/shard_map/ppermute | solution.py:138
  152.4 6.3 %collective-permute-start.7 = (bf16[128,256]{1,0:T(8,128)(2,1)S(1)}, bf16[128,256]{1,0:T(8,128)(2,1)S(1)}, u32[]{:S(2)}, u32[]{:S(2)}) collective-permute-start(bf16[128,256]{1,0:T(8,128)(2,1)S(1)} %get-tuple-element.27.rest_0_), channel_id=1, source_target_pairs={{0,16},{2,18},{4,20},{6,22},{8,24},{10,26},{12,28},{14,30},{16,0},... | collective-permute-start | bytes 196616 | tf_op jit(solution)/shard_map/ppermute | solution.py:205
  160.8 6.3 %collective-permute-start.6 = (f32[64,256]{1,0:T(8,128)S(1)}, f32[64,256]{1,0:T(8,128)S(1)}, u32[]{:S(2)}, u32[]{:S(2)}) collective-permute-start(f32[64,256]{1,0:T(8,128)S(1)} %get-tuple-element.26), channel_id=1, source_target_pairs={{0,1},{1,0},{2,3},{3,2},{4,5},{5,4},{6,7},{7,6},{8,9},{9,8},{10,11... | collective-permute-start | bytes 196616 | tf_op jit(solution)/shard_map/ppermute | solution.py:138
  166.7 0.9 copy-start.15
Sparse Core Ops, SparseCore 0:
  15.6 49.6 all-gather.4
  67.4 44.2 all-gather.6

commit v3 on v2

v3 whole, which is shorter than its diff:
```python
import functools
import math

import jax
import jax.numpy as jnp
from jax import lax
from jax.experimental import pallas as pl
from jax.experimental.pallas import tpu as pltpu
from jax.sharding import PartitionSpec as P

HD = 128
NCH = 2
EPS = 1e-05
N = 16
RING = 8
ROWS = 64
SPAN = 128
PRE = 256
D = 4096
COLS = 256
SCALE = 1.0 / math.sqrt(HD)
LOW = -1e30
F32 = jnp.float32
BF16 = jnp.bfloat16
RINGS = [list(range(RING)), list(range(RING, N))]
VMEM = pl.BlockSpec(memory_space=pltpu.VMEM)
SMEM = pl.BlockSpec(memory_space=pltpu.SMEM)
PARAMS = pltpu.CompilerParams(vmem_limit_bytes=24 * 1024 * 1024)


def dot(a, b):
    return jnp.dot(a, b, preferred_element_type=F32)


def dot_t(a, b):
    return lax.dot_general(a, b, (((1,), (1,)), ((), ())), preferred_element_type=F32)


def normalise(ref, gain, normed, rows):
    total = jnp.zeros((ROWS, COLS), F32)
    for j in range(N):
        part = ref[j].astype(F32)
        total = total + part * part
    inverse = lax.rsqrt(jnp.sum(total, axis=1, keepdims=True) / D + EPS)
    for j in range(N):
        cols = slice(j * COLS, (j + 1) * COLS)
        normed[rows, cols] = (ref[j].astype(F32) * inverse * gain[:, cols]).astype(BF16)


def half_rows(half):
    return pl.ds(pl.multiple_of(half * ROWS, ROWS), ROWS)


def project_first(place, lens, mine, other, gain, wq, wkv, q_out, kv_out, normed):
    t = place[0]
    normalise(mine, gain, normed, half_rows(t))
    normalise(other, gain, normed, half_rows(1 - t))
    q_out[...] = dot(normed[...], wq[...]).astype(BF16)
    kv = dot_t(wkv[...], normed[...]).astype(BF16)
    filled = jnp.full((16, SPAN), lens[0].astype(F32), F32).astype(BF16)
    for j in range(N):
        kv_out[j, 0:32] = kv
        kv_out[j, 32:48] = filled


def over_prefixes(g, q, held, first, scores):
    count = q.shape[0]
    slot = lax.broadcasted_iota(jnp.int32, (1, PRE), 1).astype(F32)
    top = jnp.full((count, PRE), LOW, F32)
    for k in range(RING):
        for o in range(2):
            shard = (g if o == 0 else 1 - g) * RING + k
            filled = first[shard, 32:48][0:1].astype(F32)
            filled = jnp.concatenate([filled, filled], axis=1)
            s = dot_t(q, held[k, o, 0]) * SCALE
            s = jnp.where(slot < filled, s, LOW)
            b = (k * 2 + o) * PRE
            scores[:, b : b + PRE] = s
            top = jnp.maximum(top, s)
    top = jnp.max(top, axis=1, keepdims=True)
    total = jnp.zeros((count, PRE), F32)
    acc = jnp.zeros((count, HD), F32)
    for k in range(RING):
        for o in range(2):
            b = (k * 2 + o) * PRE
            e = jnp.exp(scores[:, b : b + PRE] - top)
            total = total + e
            acc = acc + dot(e.astype(BF16), held[k, o, 1])
    return top, jnp.sum(total, axis=1, keepdims=True), acc


def with_spans(start, top, total, acc, spans):
    count = acc.shape[0]
    row = lax.broadcasted_iota(jnp.int32, (count, SPAN), 0) + start
    col = lax.broadcasted_iota(jnp.int32, (count, SPAN), 1)
    spans = list(spans)
    spans[-1] = (jnp.where(col <= row, spans[-1][0], LOW), spans[-1][1])
    peak = top
    for s, _ in spans:
        peak = jnp.maximum(peak, jnp.max(s, axis=1, keepdims=True))
    weight = jnp.exp(top - peak)
    total = total * weight
    acc = acc * weight
    for s, product in spans:
        e = jnp.exp(s - peak)
        total = total + jnp.sum(e, axis=1, keepdims=True)
        acc = acc + product(e.astype(BF16))
    return (acc / total).astype(BF16)


def first_span(g, q, first):
    keys = jnp.concatenate([first[g * RING + i, 0:32] for i in range(4)], axis=0)
    values = jnp.concatenate([first[g * RING + 4 + i, 0:32] for i in range(4)], axis=0)
    return dot(q, keys) * SCALE, lambda e: dot_t(e, values)


def attend_first(place, q_ref, held, first, out, scores):
    g = place[1]
    q = q_ref[...]
    top, total, acc = over_prefixes(g, q, held, first, scores)
    result = with_spans(0, top, total, acc, [first_span(g, q, first)])
    for j in range(N):
        out[j] = result


def own_rows(place, x, gain, wq, held, first, normed, q_out, top_out, sum_out, acc_out, scores):
    normalise(x, gain, normed, slice(0, ROWS))
    q = dot(normed[...], wq[...]).astype(BF16)
    q_out[...] = q
    top, total, acc = over_prefixes(place[1], q, held, first, scores)
    top_out[...] = jnp.broadcast_to(top, (ROWS, HD))
    sum_out[...] = jnp.broadcast_to(total, (ROWS, HD))
    acc_out[...] = acc


def other_rows(
    place, x, gain, wq, wkv, held, first, normed_own, q_own, top_own, sum_own, acc_own, out, kv, normed, scores
):
    t, g = place[0], place[1]
    normalise(x, gain, normed, slice(0, ROWS))
    q = dot(normed[...], wq[...]).astype(BF16)
    kv[half_rows(1 - t), :] = dot_t(normed[...], wkv[...]).astype(BF16)
    kv[half_rows(t), :] = dot_t(normed_own[...], wkv[...]).astype(BF16)
    top, total, acc = over_prefixes(g, q, held, first, scores)
    keys, values = kv[:, 0:HD], kv[:, HD : 2 * HD]
    parts = (
        (t, q_own[...], top_own[:, 0:1], sum_own[:, 0:1], acc_own[...]),
        (1 - t, q, top, total, acc),
    )
    for half, q, top, total, acc in parts:
        spans = [first_span(g, q, first), (dot_t(q, keys) * SCALE, lambda e: dot(e, values))]
        result = with_spans(half * ROWS, top, total, acc, spans)
        for j in range(N):
            out[j, half_rows(half), :] = result


def mix(place, att, wo, x_ref, mine, other):
    t = place[0]
    acc = jnp.zeros((SPAN, COLS), F32)
    for j in range(N):
        acc = acc + dot(att[j], wo[j * HD : (j + 1) * HD, :])
    top, bottom = acc[0:ROWS], acc[ROWS:SPAN]
    mine[...] = x_ref[...].astype(F32) + jnp.where(t == 0, top, bottom)
    other[...] = jnp.where(t == 0, bottom, top)


def spread(block):
    return lax.all_to_all(block, "kvp", 0, 0, tiled=True)


def swap(block):
    return lax.ppermute(block, "tp", [(0, 1), (1, 0)])


def onward(block, cross):
    route = [(i, (i ^ cross) + 2) for i in range(30)]
    return lax.ppermute(block, ("section", "tp"), route)


def shape(*dims, dtype=BF16):
    return jax.ShapeDtypeStruct(dims, dtype)


def body(entering, feed, gain, wq, wkv, wo, cache, prefix_len, owner):
    shard_id = lax.axis_index("kvp")
    section_id = lax.axis_index("section")
    g = shard_id // RING
    place = jnp.stack([lax.axis_index("tp"), g]).astype(jnp.int32)
    filled = prefix_len[0, 0]
    wq_here, wkv_here, wo_here = wq[0, :, 0, :], wkv[0, :, 0, :], wo[0]
    cache_here = cache[0]

    prefix = cache_here[:, :, :PRE, :]
    own = lax.dynamic_index_in_dim(prefix, g, 1, False)
    give = lax.dynamic_index_in_dim(prefix, 1 - g, 1, False)
    got = lax.ppermute(give, "kvp", [(i, (i + RING) % N) for i in range(N)])
    held = lax.all_gather(jnp.stack([own, got]), "kvp", axis_index_groups=RINGS)

    wkv_t = wkv_here.T

    def updated(cache_now, fresh, moment):
        start = filled
        for u in range(moment):
            start = start + jnp.where(owner[u, 0] == shard_id, SPAN, 0).astype(jnp.int32)
        changed = lax.dynamic_update_slice(cache_now, fresh, (0, 0, start, 0))
        return jnp.where(owner[moment, 0] == shard_id, changed, cache_now)

    sums, fresh_all = [], []
    x = entering[0]
    for moment in range(NCH):
        if moment:
            passed = (onward(own_sum, 0) + onward(other_sum, 1)).astype(BF16)
            x = jnp.where(section_id == 0, feed[moment - 1], passed)
        mine = spread(jnp.broadcast_to(x[None], (N, ROWS, COLS)))
        other = swap(mine)
        if moment == 0:
            q, kv = pl.pallas_call(
                project_first,
                out_shape=(shape(SPAN, HD), shape(N, 48, SPAN)),
                in_specs=[SMEM, SMEM] + [VMEM] * 5,
                out_specs=(VMEM, VMEM),
                scratch_shapes=[pltpu.VMEM((SPAN, D), BF16)],
                compiler_params=PARAMS,
                name="project_first",
            )(place, filled[None], mine, other, gain, wq_here, wkv_t)
            first = spread(kv)
            wkv_late, first = lax.optimization_barrier((wkv_t, first))
            wkv_all = lax.all_gather(wkv_late, "kvp", axis_index_groups=RINGS)
            wkv_all = wkv_all.reshape(2 * HD, D)
            both = jnp.transpose(first[:, 0:32].reshape(2, 2, HD, SPAN), (1, 0, 3, 2))
            fresh_all.append(both)
            att = pl.pallas_call(
                attend_first,
                out_shape=shape(N, SPAN, HD),
                in_specs=[SMEM] + [VMEM] * 3,
                out_specs=VMEM,
                scratch_shapes=[pltpu.VMEM((SPAN, N * PRE), F32)],
                compiler_params=PARAMS,
                name="attend_first",
            )(place, q, held, first)
        else:
            mine, wkv_all = lax.optimization_barrier((mine, wkv_all))
            own_state = pl.pallas_call(
                own_rows,
                out_shape=(shape(ROWS, D), shape(ROWS, HD)) + (shape(ROWS, HD, dtype=F32),) * 3,
                in_specs=[SMEM] + [VMEM] * 5,
                out_specs=(VMEM,) * 5,
                scratch_shapes=[pltpu.VMEM((ROWS, N * PRE), F32)],
                compiler_params=PARAMS,
                name="own_rows",
            )(place, mine, gain, wq_here, held, first)
            att, kv = pl.pallas_call(
                other_rows,
                out_shape=(shape(N, SPAN, HD), shape(SPAN, 2 * HD)),
                in_specs=[SMEM] + [VMEM] * 11,
                out_specs=(VMEM, VMEM),
                scratch_shapes=[pltpu.VMEM((ROWS, D), BF16), pltpu.VMEM((ROWS, N * PRE), F32)],
                compiler_params=PARAMS,
                name="other_rows",
            )(place, other, gain, wq_here, wkv_all, held, first, *own_state)
            late, kv = lax.optimization_barrier((sums[0], kv))
            sums[0] = late
            pair = lax.ppermute(kv, "kvp", [(i, (i + RING) % N) for i in range(N)])
            heads = jnp.where(g == 0, jnp.stack([kv, pair]), jnp.stack([pair, kv]))
            both = jnp.transpose(heads.reshape(2, SPAN, 2, HD), (2, 0, 1, 3))
            fresh_all.append(both)
        att = spread(att)
        if moment:
            new_cache = cache_here
            for u in range(NCH):
                new_cache = updated(new_cache, fresh_all[u], u)
            new_cache, att = lax.optimization_barrier((new_cache, att))
        own_sum, other_sum = pl.pallas_call(
            mix,
            out_shape=(shape(ROWS, COLS, dtype=F32), shape(ROWS, COLS, dtype=F32)),
            in_specs=[SMEM] + [VMEM] * 3,
            out_specs=(VMEM, VMEM),
            compiler_params=PARAMS,
            name="mix",
        )(place, att, wo_here, x)
        sums.append((own_sum, other_sum))
    outputs = [(mine + swap(other)).astype(BF16) for mine, other in sums]
    return (jnp.stack(outputs)[:, None], new_cache[None])


def solution(mesh):
    in_specs = (
        P("section", "tp", "kvp"),
        P(None, "tp", "kvp"),
        P("section", None),
        P("section", None, "tp", "kvp"),
        P("section", None, "tp", "kvp"),
        P("section", "tp", "kvp"),
        P("section", None, "tp", "kvp", None),
        P("section", "kvp"),
        P(None, "section"),
    )
    out_specs = (P(None, "section", "tp", "kvp"), P("section", None, "tp", "kvp", None))
    return jax.shard_map(body, mesh=mesh, in_specs=in_specs, out_specs=out_specs, check_vma=False)
```

time: 176 us -> 174 us (0.989)
  blocking collectives: 69.5 us -> 67.1 us
  other arithmetic: 2.37 us -> 4.33 us
    ppermute x1, waiting for transfers between devices: 3.69 us -> 0.32 us  [body(): pair = lax.ppermute(kv, 'kvp', [(i, (i + RING) % N) for i in range(N)])]
    all_gather x1, waiting for transfers between devices: 4.61 us -> 7.56 us  [body(): held = lax.all_gather(jnp.stack([own, got]), 'kvp', axis_index_groups=RINGS)]
    unnamed x35 -> x29, local copies, waits for them, and re-layouts: 6.21 us -> 3.57 us
    select_n x2, local copies, waits for them, and re-layouts: 1.01 us -> 3.65 us  [updated(): return jnp.where(owner[moment, 0] == shard_id, changed, cache_now)]
    all_to_all x4, blocking collectives: 69.5 us -> 67.1 us  [spread(): return lax.all_to_all(block, 'kvp', 0, 0, tiled=True)]
    select_n x1 -> x2, other arithmetic: 0.06 us -> 1.96 us  [updated(): return jnp.where(owner[moment, 0] == shard_id, changed, cache_now)]
  transfers between devices with their start and end apart: 11 -> 11, of which waited for: 9 -> 8; matrix products, arithmetic and copies ran while one was open for 2% -> 4% of each run, Pallas kernels for 3% -> 5%
where the time goes in v3:
time: 174 us; the launch traced here: 172 us
  blocking collectives  67.1 us (39%)
  starting transfers between devices  39 us (22%)
  waiting for transfers between devices  25.8 us (15%)
  between operations  16.4 us (9%)
  Pallas kernels  11.6 us (7%)
  local copies, waits for them, and re-layouts  8.22 us (5%)
  other arithmetic  4.33 us (2%)
    all_to_all x4, blocking collectives, spread(): return lax.all_to_all(block, 'kvp', 0, 0, tiled=True)  67.1 us
    ppermute x2, starting transfers between devices, onward(): return lax.ppermute(block, ('section', 'tp'), route)  14.4 us
    ppermute x4, starting transfers between devices, swap(): return lax.ppermute(block, 'tp', [(0, 1), (1, 0)])  14.1 us
    ppermute x2, waiting for transfers between devices, onward(): return lax.ppermute(block, ('section', 'tp'), route)  11.8 us
    all_gather x1, waiting for transfers between devices, body(): held = lax.all_gather(jnp.stack([own, got]), 'kvp', axis_index_groups=RINGS)  7.56 us
    all_to_all x1, starting transfers between devices, spread(): return lax.all_to_all(block, 'kvp', 0, 0, tiled=True)  6.04 us
    pallas_call x1, Pallas kernels, body(): pl.pallas_call(other_rows, out_shape=(shape(N, SPAN, HD), shape(SPAN, 2 *...  3.8 us
    ppermute x1, waiting for transfers between devices, body(): got = lax.ppermute(give, 'kvp', [(i, (i + RING) % N) for i in range(N)])  3.79 us
  transfers between devices with their start and end apart: 11, of which 8 were waited for; matrix products, arithmetic and copies ran while one was open for 4% of the time, Pallas kernels for 5%

profile of v3, /device:TPU:7, one launch (start us, length us, event | category | flops | bytes accessed | tf_op | source)
XLA Modules:
  0.0 172.4 jit_solution(2891321595538717950)
XLA Ops:
  7.2 1.1 copy.27
  8.5 2.5 %collective-permute-start.1 = (bf16[2,256,128]{2,1,0:T(8,128)(2,1)S(1)}, bf16[2,256,128]{2,1,0:T(8,128)(2,1)S(1)}, u32[]{:S(2)}, u32[]{:S(2)}) collective-permute-start(bf16[2,256,128]{2,1,0:T(8,128)(2,1)S(1)} %get-tuple-element.51), channel_id=1, source_target_pairs={{0,16},{2,18},{4,20},{6,22},{8,24},{10,26},{12,28},{14,30},{16,0},... | collective-permute-start | bytes 393224 | tf_op jit(solution)/shard_map/ppermute | solution.py:196
  10.9 3.8 %collective-permute-done.1 = bf16[2,256,128]{2,1,0:T(8,128)(2,1)S(1)} collective-permute-done((bf16[2,256,128]{2,1,0:T(8,128)(2,1)S(1)}, bf16[2,256,128]{2,1,0:T(8,128)(2,1)S(1)}, u32[]{:S(2)}, u32[]{:S(2)}) %collective-permute-start.1) | collective-permute-done | bytes 131104 | tf_op jit(solution)/shard_map/ppermute | solution.py:196
  15.6 19.8 %all_to_all.25.mine = bf16[16,64,256]{2,1,0:T(8,128)(2,1)S(1)} all-to-all(bf16[16,64,256]{2,1,0:T(8,128)(2,1)S(1)} %broadcast_in_dim.20), channel_id=1, replica_groups=mesh['section'=16,'kvp'=16,'tp'=2] {'kvp'}, dimensions={0} | all-to-all | bytes 1048576 | tf_op jit(solution)/shard_map/all_to_all | solution.py:168
  35.4 5.4 %collective-permute-start = (bf16[16,64,256]{2,1,0:T(8,128)(2,1)S(1)}, bf16[16,64,256]{2,1,0:T(8,128)(2,1)S(1)}, u32[]{:S(2)}, u32[]{:S(2)}) collective-permute-start(bf16[16,64,256]{2,1,0:T(8,128)(2,1)S(1)} %all_to_all.25.mine), channel_id=1, source_target_pairs={{0,1},{1,0},{2,3},{3,2},{4,5},{5,4},{6,7},{7,6},{8,9},{9,8},{10,11... | collective-permute-start | bytes 1572872 | tf_op jit(solution)/shard_map/ppermute | solution.py:172
  42.4 1.6 project_first.1
  44.0 14.0 %all_to_all.26.first = bf16[16,48,128]{2,1,0:T(8,128)(2,1)S(1)} all-to-all(bf16[16,48,128]{2,1,0:T(8,128)(2,1)S(1)} %get-tuple-element.25), channel_id=1, replica_groups=mesh['section'=16,'kvp'=16,'tp'=2] {'kvp'}, dimensions={0} | all-to-all | bytes 393216 | tf_op jit(solution)/shard_map/all_to_all | solution.py:168
  57.9 7.6 %all-gather.5.cloned.1.call-done = bf16[16,2,256,128]{3,2,1,0:T(8,128)(2,1)} async-done(((bf16[2,2,256,128]{3,2,1,0:T(8,128)(2,1)}), bf16[16,2,256,128]{3,2,1,0:T(8,128)(2,1)}) %all-gather.5.cloned.1.call-update) | async-done | bytes 2097168 | tf_op jit(solution)/shard_map/all_gather | solution.py:197
  65.5 1.6 copy-done
  67.1 1.8 %attend_first.1 = bf16[16,128,128]{2,1,0:T(8,128)(2,1)S(1)} custom-call(s32[2]{0:T(128)S(1)} %pad_add_fusion.place, bf16[128,128]{1,0:T(8,128)(2,1)S(1)} %get-tuple-element.24.q_ref, bf16[8,2,2,256,128]{4,3,2,1,0:T(8,128)(2,1)S(1)} %bitcast.44, bf16[16,48,128]{2,1,0:T(8,128)(2,1)S(1)} %all_to_all.26.first), custom_call_target="tpu_custom_call" | custom-call | tf_op jit(solution)/shard_map/attend_first/pallas_call | solution.py:232
  68.9 14.2 %all_to_all.27.att = bf16[16,128,128]{2,1,0:T(8,128)(2,1)S(1)} all-to-all(bf16[16,128,128]{2,1,0:T(8,128)(2,1)S(1)} %attend_first.1), channel_id=1, replica_groups=mesh['section'=16,'kvp'=16,'tp'=2] {'kvp'}, dimensions={0} | all-to-all | bytes 1048576 | tf_op jit(solution)/shard_map/all_to_all | solution.py:168
  83.0 1.0 mix.2
  84.0 4.0 %collective-permute-start.2 = (f32[64,256]{1,0:T(8,128)S(1)}, f32[64,256]{1,0:T(8,128)}, u32[]{:S(2)}, u32[]{:S(2)}) collective-permute-start(f32[64,256]{1,0:T(8,128)S(1)} %get-tuple-element.38), channel_id=1, source_target_pairs={{0,32},{1,33},{32,64},{33,65},{64,96},{65,97},{96,128},{97,129},{1... | collective-permute-start | bytes 196616 | tf_op jit(solution)/shard_map/ppermute | solution.py:177
  88.0 10.4 %collective-permute-start.3 = (f32[64,256]{1,0:T(8,128)S(1)}, f32[64,256]{1,0:T(8,128)}, u32[]{:S(2)}, u32[]{:S(2)}) collective-permute-start(f32[64,256]{1,0:T(8,128)S(1)} %get-tuple-element.39), channel_id=1, source_target_pairs={{0,33},{1,32},{32,65},{33,64},{64,97},{65,96},{96,129},{97,128},{1... | collective-permute-start | bytes 196616 | tf_op jit(solution)/shard_map/ppermute | solution.py:177
  98.4 1.2 collective-permute-done.2
  99.6 10.6 %collective-permute-done.3 = f32[64,256]{1,0:T(8,128)} collective-permute-done((f32[64,256]{1,0:T(8,128)S(1)}, f32[64,256]{1,0:T(8,128)}, u32[]{:S(2)}, u32[]{:S(2)}) %collective-permute-start.3) | collective-permute-done | bytes 65568 | tf_op jit(solution)/shard_map/ppermute | solution.py:177
  110.2 0.9 fusion.2.x_ref
  111.1 19.1 %all_to_all.28.x = bf16[16,64,256]{2,1,0:T(8,128)(2,1)} all-to-all(bf16[16,64,256]{2,1,0:T(8,128)(2,1)S(1)} %broadcast_in_dim.21), channel_id=1, replica_groups=mesh['section'=16,'kvp'=16,'tp'=2] {'kvp'}, dimensions={0} | all-to-all | bytes 1048576 | tf_op jit(solution)/shard_map/all_to_all | solution.py:168
  130.3 1.9 %collective-permute-start.4 = (bf16[16,64,256]{2,1,0:T(8,128)(2,1)}, bf16[16,64,256]{2,1,0:T(8,128)(2,1)}, u32[]{:S(2)}, u32[]{:S(2)}) collective-permute-start(bf16[16,64,256]{2,1,0:T(8,128)(2,1)} %all_to_all.28.x), channel_id=1, source_target_pairs={{0,1},{1,0},{2,3},{3,2},{4,5},{5,4},{6,7},{7,6},{8,9},{9,8},{10,11... | collective-permute-start | bytes 1572872 | tf_op jit(solution)/shard_map/ppermute | solution.py:172
  132.2 2.5 %own_rows.1 = (bf16[64,4096]{1,0:T(8,128)(2,1)S(1)}, bf16[64,128]{1,0:T(8,128)(2,1)S(1)}, f32[64,128]{1,0:T(8,128)S(1)}, f32[64,128]{1,0:T(8,128)S(1)}, f32[64,128]{1,0:T(8,128)S(1)}) custom-call(s32[2]{0:T(128)S(1)} %pad_add_fusion.place, bf16[16,64,256]{2,1,0:T(8,128)(2,1)} %all_to_all.28.x, f32[1,4096]{1,0:T(1,128)S(1)} %copy-done.8, ...), custom_call_target="tpu_custom_call" | custom-call | tf_op jit(solution)/shard_map/own_rows/pallas_call | solution.py:243
  134.8 3.8 %other_rows.1 = (bf16[16,128,128]{2,1,0:T(8,128)(2,1)S(1)}, bf16[128,256]{1,0:T(8,128)(2,1)S(1)}) custom-call(s32[2]{0:T(128)S(1)} %pad_add_fusion.place, bf16[16,64,256]{2,1,0:T(8,128)(2,1)} %collective-permute-done.4.x, f32[1,4096]{1,0:T(1,128)S(1)} %copy-done.8, bf16[4096,128]{1,0:T(8,128)(2,1)S(1)} %bitcast.49, bf16[256,4096]{1,0:T(8,128)(2,1)S(1)} %copy-done.5, ...), custom_call_target="tpu_custom_call" | custom-call | tf_op jit(solution)/shard_map/other_rows/pallas_call | solution.py:252
  138.6 0.8 copy-done.7
  139.4 6.0 %all-to-all-start.4 = ((bf16[16,128,128]{2,1,0:T(8,128)(2,1)}), bf16[16,128,128]{2,1,0:T(8,128)(2,1)S(1)}, u32[]{:S(2)}, u32[]{:S(2)}) async-start(bf16[16,128,128]{2,1,0:T(8,128)(2,1)} %copy-done.7), calls=%async_computation.4 | async-start | bytes 1048576 | tf_op jit(solution)/shard_map/all_to_all | solution.py:168
  147.6 2.0 %collective-permute-start.6 = (bf16[128,256]{1,0:T(8,128)(2,1)S(1)}, bf16[128,256]{1,0:T(8,128)(2,1)S(1)}, u32[]{:S(2)}, u32[]{:S(2)}) collective-permute-start(bf16[128,256]{1,0:T(8,128)(2,1)S(1)} %get-tuple-element.40), channel_id=1, source_target_pairs={{0,16},{2,18},{4,20},{6,22},{8,24},{10,26},{12,28},{14,30},{16,0},... | collective-permute-start | bytes 196616 | tf_op jit(solution)/shard_map/ppermute | solution.py:263
  149.6 1.0 bitcast_select_fusion
  150.6 1.8 %select_n.73 = bf16[2,2,512,128]{3,2,1,0:T(8,128)(2,1)} dynamic-update-slice(bf16[2,2,512,128]{3,2,1,0:T(8,128)(2,1)} %bitcast.57, bf16[2,2,128,128]{3,2,1,0:T(8,128)(2,1)S(1)} %bitcast_select_fusion, s32[]{:T(128)} %constant.35.clone.1, s32[]{:T(128)} %constant.35.clone.1, s32[]{:T(128)S(6)} %select_n.69, s32[]{:T(128)} %constant.35.clone.1) | dynamic-update-slice | bytes 262148 | tf_op jit(solution)/shard_map/jit(_where)/select_n | solution.py:206
  152.5 2.5 %collective-permute-start.5 = (f32[64,256]{1,0:T(8,128)S(1)}, f32[64,256]{1,0:T(8,128)S(1)}, u32[]{:S(2)}, u32[]{:S(2)}) collective-permute-start(f32[64,256]{1,0:T(8,128)S(1)} %copy-done.11), channel_id=1, source_target_pairs={{0,1},{1,0},{2,3},{3,2},{4,5},{5,4},{6,7},{7,6},{8,9},{9,8},{10,11... | collective-permute-start | bytes 196616 | tf_op jit(solution)/shard_map/ppermute | solution.py:172
  155.4 1.0 fusion.1
  156.4 1.8 %select_n.81 = bf16[2,2,512,128]{3,2,1,0:T(8,128)(2,1)} dynamic-update-slice(bf16[2,2,512,128]{3,2,1,0:T(8,128)(2,1)} %select_n.73, bf16[2,2,128,128]{3,2,1,0:T(8,128)(2,1)S(1)} %fusion.1, s32[]{:T(128)} %constant.35.clone.1, s32[]{:T(128)} %constant.35.clone.1, s32[]{:T(128)S(6)} %select_n.78, s32[]{:T(128)} %constant.35.clone.1) | dynamic-update-slice | bytes 262148 | tf_op jit(solution)/shard_map/jit(_where)/select_n | solution.py:206
  158.8 1.0 mix.3
  159.8 4.2 %collective-permute-start.7 = (f32[64,256]{1,0:T(8,128)S(1)}, f32[64,256]{1,0:T(8,128)S(1)}, u32[]{:S(2)}, u32[]{:S(2)}) collective-permute-start(f32[64,256]{1,0:T(8,128)S(1)} %get-tuple-element.44), channel_id=1, source_target_pairs={{0,1},{1,0},{2,3},{3,2},{4,5},{5,4},{6,7},{7,6},{8,9},{9,8},{10,11... | collective-permute-start | bytes 196616 | tf_op jit(solution)/shard_map/ppermute | solution.py:172
  164.0 0.9 collective-permute-done.7
  (52 shorter events, 4.4 us)
Async XLA Ops:
  7.2 8.4 %copy-start.9 = (bf16[1,64,256]{2,1,0:T(8,128)(2,1)S(1)}, bf16[1,64,256]{2,1,0:T(8,128)(2,1)}, u32[]{:S(2)}) copy-start(bf16[1,64,256]{2,1,0:T(8,128)(2,1)} %param.9) | copy-start | bytes 98308
  7.2 35.2 %copy-start.8 = (f32[1,4096]{1,0:T(1,128)S(1)}, f32[1,4096]{1,0:T(1,128)}, u32[]{:S(2)}) copy-start(f32[1,4096]{1,0:T(1,128)} %gain.5) | copy-start | bytes 49156
  7.2 35.2 %copy-start.2 = (bf16[1,4096,1,128]{3,1,2,0:T(8,128)(2,1)S(1)}, bf16[1,4096,1,128]{3,1,2,0:T(8,128)(2,1)}, u32[]{:S(2)}) copy-start(bf16[1,4096,1,128]{3,1,2,0:T(8,128)(2,1)} %param.12) | copy-start | bytes 3145732
  7.2 35.2 %copy-start.6 = (bf16[1,4096,1,32]{1,3,2,0:T(8,128)(2,1)S(1)}, bf16[1,4096,1,32]{1,3,2,0:T(8,128)(2,1)}, u32[]{:S(2)}) copy-start(bf16[1,4096,1,32]{1,3,2,0:T(8,128)(2,1)} %param.13) | copy-start | bytes 786436
  7.2 58.3 %all-gather.5.cloned.1.call-start = ((), (), s32[]{:S(2)}) async-start(), calls=%async_computation.5 | async-start | bytes 2359296 | tf_op jit(solution)/shard_map/all_gather | solution.py:197
  8.4 7.1 %copy-start.12 = (bf16[1,2,2,512,128]{4,3,2,1,0:T(8,128)(2,1)}, bf16[1,2,2,512,128]{4,3,2,1,0:T(8,128)(2,1)S(1)}, u32[]{:S(2)}) copy-start(bf16[1,2,2,512,128]{4,3,2,1,0:T(8,128)(2,1)S(1)} %copy.27) | copy-start | bytes 1572868
  8.5 6.3 %collective-permute-start.1 = (bf16[2,256,128]{2,1,0:T(8,128)(2,1)S(1)}, bf16[2,256,128]{2,1,0:T(8,128)(2,1)S(1)}, u32[]{:S(2)}, u32[]{:S(2)}) collective-permute-start(bf16[2,256,128]{2,1,0:T(8,128)(2,1)S(1)} %get-tuple-element.51), channel_id=1, source_target_pairs={{0,16},{2,18},{4,20},{6,22},{8,24},{10,26},{12,28},{14,30},{16,0},... | collective-permute-start | bytes 393224 | tf_op jit(solution)/shard_map/ppermute | solution.py:196
  15.5 116.7 %all-gather.7.cloned.1.call-start = ((), (), s32[]{:S(2)}) async-start(), calls=%async_computation.6 | async-start | bytes 2359296 | tf_op jit(solution)/shard_map/all_gather | solution.py:228
  35.4 6.9 %collective-permute-start = (bf16[16,64,256]{2,1,0:T(8,128)(2,1)S(1)}, bf16[16,64,256]{2,1,0:T(8,128)(2,1)S(1)}, u32[]{:S(2)}, u32[]{:S(2)}) collective-permute-start(bf16[16,64,256]{2,1,0:T(8,128)(2,1)S(1)} %all_to_all.25.mine), channel_id=1, source_target_pairs={{0,1},{1,0},{2,3},{3,2},{4,5},{5,4},{6,7},{7,6},{8,9},{9,8},{10,11... | collective-permute-start | bytes 1572872 | tf_op jit(solution)/shard_map/ppermute | solution.py:172
  65.5 1.6 copy-start
  67.1 15.9 %copy-start.3 = (bf16[1,2048,256]{2,1,0:T(8,128)(2,1)S(1)}, bf16[1,2048,256]{2,1,0:T(8,128)(2,1)}, u32[]{:S(2)}) copy-start(bf16[1,2048,256]{2,1,0:T(8,128)(2,1)} %param.14) | copy-start | bytes 3145732
  68.9 63.3 %copy-start.1 = (bf16[16,2,256,128]{3,2,1,0:T(8,128)(2,1)S(1)}, bf16[16,2,256,128]{3,2,1,0:T(8,128)(2,1)}, u32[]{:S(2)}) copy-start(bf16[16,2,256,128]{3,2,1,0:T(8,128)(2,1)} %all-gather.5.cloned.1.call-done) | copy-start | bytes 6291460
  84.0 50.8 %copy-start.10 = (f32[64,256]{1,0:T(8,128)}, f32[64,256]{1,0:T(8,128)S(1)}, u32[]{:S(2)}) copy-start(f32[64,256]{1,0:T(8,128)S(1)} %get-tuple-element.39) | copy-start | bytes 196612
  84.0 15.6 %collective-permute-start.2 = (f32[64,256]{1,0:T(8,128)S(1)}, f32[64,256]{1,0:T(8,128)}, u32[]{:S(2)}, u32[]{:S(2)}) collective-permute-start(f32[64,256]{1,0:T(8,128)S(1)} %get-tuple-element.38), channel_id=1, source_target_pairs={{0,32},{1,33},{32,64},{33,65},{64,96},{65,97},{96,128},{97,129},{1... | collective-permute-start | bytes 196616 | tf_op jit(solution)/shard_map/ppermute | solution.py:177
  88.0 22.2 %collective-permute-start.3 = (f32[64,256]{1,0:T(8,128)S(1)}, f32[64,256]{1,0:T(8,128)}, u32[]{:S(2)}, u32[]{:S(2)}) collective-permute-start(f32[64,256]{1,0:T(8,128)S(1)} %get-tuple-element.39), channel_id=1, source_target_pairs={{0,33},{1,32},{32,65},{33,64},{64,97},{65,96},{96,129},{97,128},{1... | collective-permute-start | bytes 196616 | tf_op jit(solution)/shard_map/ppermute | solution.py:177
  130.3 4.5 %collective-permute-start.4 = (bf16[16,64,256]{2,1,0:T(8,128)(2,1)}, bf16[16,64,256]{2,1,0:T(8,128)(2,1)}, u32[]{:S(2)}, u32[]{:S(2)}) collective-permute-start(bf16[16,64,256]{2,1,0:T(8,128)(2,1)} %all_to_all.28.x), channel_id=1, source_target_pairs={{0,1},{1,0},{2,3},{3,2},{4,5},{5,4},{6,7},{7,6},{8,9},{9,8},{10,11... | collective-permute-start | bytes 1572872 | tf_op jit(solution)/shard_map/ppermute | solution.py:172
  132.2 2.6 %copy-start.5 = (bf16[256,4096]{1,0:T(8,128)(2,1)S(1)}, bf16[256,4096]{1,0:T(8,128)(2,1)}, u32[]{:S(2)}) copy-start(bf16[256,4096]{1,0:T(8,128)(2,1)} %all-gather.7.cloned.1.call-done.wkv) | copy-start | bytes 6291460
  134.8 10.7 %copy-start.13 = (s32[2,1]{0,1:T(1,128)S(1)}, s32[2,1]{0,1:T(1,128)}, u32[]{:S(2)}) copy-start(s32[2,1]{0,1:T(1,128)} %param.17) | copy-start | bytes 28
  138.6 0.8 copy-start.7
  139.4 13.1 %copy-start.11 = (f32[64,256]{1,0:T(8,128)S(1)}, f32[64,256]{1,0:T(8,128)}, u32[]{:S(2)}) copy-start(f32[64,256]{1,0:T(8,128)} %copy-done.10) | copy-start | bytes 196612
  139.4 19.4 %copy-start.4 = (bf16[1,2048,256]{2,1,0:T(8,128)(2,1)S(1)}, bf16[1,2048,256]{2,1,0:T(8,128)(2,1)}, u32[]{:S(2)}) copy-start(bf16[1,2048,256]{2,1,0:T(8,128)(2,1)} %param.14) | copy-start | bytes 3145732
  139.4 19.4 %all-to-all-start.4 = ((bf16[16,128,128]{2,1,0:T(8,128)(2,1)}), bf16[16,128,128]{2,1,0:T(8,128)(2,1)S(1)}, u32[]{:S(2)}, u32[]{:S(2)}) async-start(bf16[16,128,128]{2,1,0:T(8,128)(2,1)} %copy-done.7), calls=%async_computation.4 | async-start | bytes 1048576 | tf_op jit(solution)/shard_map/all_to_all | solution.py:168
  147.6 7.8 %collective-permute-start.6 = (bf16[128,256]{1,0:T(8,128)(2,1)S(1)}, bf16[128,256]{1,0:T(8,128)(2,1)S(1)}, u32[]{:S(2)}, u32[]{:S(2)}) collective-permute-start(bf16[128,256]{1,0:T(8,128)(2,1)S(1)} %get-tuple-element.40), channel_id=1, source_target_pairs={{0,16},{2,18},{4,20},{6,22},{8,24},{10,26},{12,28},{14,30},{16,0},... | collective-permute-start | bytes 196616 | tf_op jit(solution)/shard_map/ppermute | solution.py:263
  152.5 11.5 %collective-permute-start.5 = (f32[64,256]{1,0:T(8,128)S(1)}, f32[64,256]{1,0:T(8,128)S(1)}, u32[]{:S(2)}, u32[]{:S(2)}) collective-permute-start(f32[64,256]{1,0:T(8,128)S(1)} %copy-done.11), channel_id=1, source_target_pairs={{0,1},{1,0},{2,3},{3,2},{4,5},{5,4},{6,7},{7,6},{8,9},{9,8},{10,11... | collective-permute-start | bytes 196616 | tf_op jit(solution)/shard_map/ppermute | solution.py:172
  159.8 5.1 %collective-permute-start.7 = (f32[64,256]{1,0:T(8,128)S(1)}, f32[64,256]{1,0:T(8,128)S(1)}, u32[]{:S(2)}, u32[]{:S(2)}) collective-permute-start(f32[64,256]{1,0:T(8,128)S(1)} %get-tuple-element.44), channel_id=1, source_target_pairs={{0,1},{1,0},{2,3},{3,2},{4,5},{5,4},{6,7},{7,6},{8,9},{9,8},{10,11... | collective-permute-start | bytes 196616 | tf_op jit(solution)/shard_map/ppermute | solution.py:172
Sparse Core Ops, SparseCore 0:
  15.6 49.8 all-gather.4
  67.6 44.0 all-gather.6

commit v4 on v3

--- a/solution.py
+++ b/solution.py
@@ -25,7 +25,7 @@
 RINGS = [list(range(RING)), list(range(RING, N))]
 VMEM = pl.BlockSpec(memory_space=pltpu.VMEM)
 SMEM = pl.BlockSpec(memory_space=pltpu.SMEM)
-PARAMS = pltpu.CompilerParams(vmem_limit_bytes=24 * 1024 * 1024)
+PARAMS = pltpu.CompilerParams(vmem_limit_bytes=40 * 1024 * 1024)
 
 
 def dot(a, b):
@@ -139,8 +139,10 @@
     t, g = place[0], place[1]
     normalise(x, gain, normed, slice(0, ROWS))
     q = dot(normed[...], wq[...]).astype(BF16)
-    kv[half_rows(1 - t), :] = dot_t(normed[...], wkv[...]).astype(BF16)
-    kv[half_rows(t), :] = dot_t(normed_own[...], wkv[...]).astype(BF16)
+    both = jnp.concatenate([normed_own[...], normed[...]], axis=0)
+    both = dot_t(both, wkv[...]).astype(BF16)
+    kv[half_rows(t), :] = both[0:ROWS]
+    kv[half_rows(1 - t), :] = both[ROWS:SPAN]
     top, total, acc = over_prefixes(g, q, held, first, scores)
     keys, values = kv[:, 0:HD], kv[:, HD : 2 * HD]
     parts = (

time: 174 us -> 174 us (level)
  no operation moved by 1% of the time
where the time goes in v4:
time: 174 us; the launch traced here: 172 us
  blocking collectives  67.1 us (39%)
  starting transfers between devices  39.6 us (23%)
  waiting for transfers between devices  25.2 us (14%)
  between operations  16.4 us (9%)
  Pallas kernels  11.2 us (6%)
  local copies, waits for them, and re-layouts  8.22 us (5%)
  other arithmetic  4.33 us (2%)
    all_to_all x4, blocking collectives, spread(): return lax.all_to_all(block, 'kvp', 0, 0, tiled=True)  67.1 us
    ppermute x4, starting transfers between devices, swap(): return lax.ppermute(block, 'tp', [(0, 1), (1, 0)])  14.6 us
    ppermute x2, starting transfers between devices, onward(): return lax.ppermute(block, ('section', 'tp'), route)  14.4 us
    ppermute x2, waiting for transfers between devices, onward(): return lax.ppermute(block, ('section', 'tp'), route)  11.8 us
    all_gather x1, waiting for transfers between devices, body(): held = lax.all_gather(jnp.stack([own, got]), 'kvp', axis_index_groups=RINGS)  7.56 us
    all_to_all x1, starting transfers between devices, spread(): return lax.all_to_all(block, 'kvp', 0, 0, tiled=True)  6 us
    ppermute x1, waiting for transfers between devices, body(): got = lax.ppermute(give, 'kvp', [(i, (i + RING) % N) for i in range(N)])  3.79 us
    select_n x2, local copies, waits for them, and re-layouts, updated(): return jnp.where(owner[moment, 0] == shard_id, changed, cache_now)  3.65 us
  transfers between devices with their start and end apart: 11, of which 8 were waited for; matrix products, arithmetic and copies ran while one was open for 4% of the time, Pallas kernels for 5%

profile of v4, /device:TPU:7, one launch (start us, length us, event | category | flops | bytes accessed | tf_op | source)
XLA Modules:
  0.0 172.0 jit_solution(9513249635000165428)
XLA Ops:
  7.2 1.1 copy.27
  8.5 2.5 %collective-permute-start.1 = (bf16[2,256,128]{2,1,0:T(8,128)(2,1)S(1)}, bf16[2,256,128]{2,1,0:T(8,128)(2,1)S(1)}, u32[]{:S(2)}, u32[]{:S(2)}) collective-permute-start(bf16[2,256,128]{2,1,0:T(8,128)(2,1)S(1)} %get-tuple-element.51), channel_id=1, source_target_pairs={{0,16},{2,18},{4,20},{6,22},{8,24},{10,26},{12,28},{14,30},{16,0},... | collective-permute-start | bytes 393224 | tf_op jit(solution)/shard_map/ppermute | solution.py:198
  10.9 3.8 %collective-permute-done.1 = bf16[2,256,128]{2,1,0:T(8,128)(2,1)S(1)} collective-permute-done((bf16[2,256,128]{2,1,0:T(8,128)(2,1)S(1)}, bf16[2,256,128]{2,1,0:T(8,128)(2,1)S(1)}, u32[]{:S(2)}, u32[]{:S(2)}) %collective-permute-start.1) | collective-permute-done | bytes 131104 | tf_op jit(solution)/shard_map/ppermute | solution.py:198
  15.6 19.8 %all_to_all.25.mine = bf16[16,64,256]{2,1,0:T(8,128)(2,1)S(1)} all-to-all(bf16[16,64,256]{2,1,0:T(8,128)(2,1)S(1)} %broadcast_in_dim.20), channel_id=1, replica_groups=mesh['section'=16,'kvp'=16,'tp'=2] {'kvp'}, dimensions={0} | all-to-all | bytes 1048576 | tf_op jit(solution)/shard_map/all_to_all | solution.py:170
  35.4 5.4 %collective-permute-start = (bf16[16,64,256]{2,1,0:T(8,128)(2,1)S(1)}, bf16[16,64,256]{2,1,0:T(8,128)(2,1)S(1)}, u32[]{:S(2)}, u32[]{:S(2)}) collective-permute-start(bf16[16,64,256]{2,1,0:T(8,128)(2,1)S(1)} %all_to_all.25.mine), channel_id=1, source_target_pairs={{0,1},{1,0},{2,3},{3,2},{4,5},{5,4},{6,7},{7,6},{8,9},{9,8},{10,11... | collective-permute-start | bytes 1572872 | tf_op jit(solution)/shard_map/ppermute | solution.py:174
  42.4 1.6 project_first.1
  44.0 14.0 %all_to_all.26.first = bf16[16,48,128]{2,1,0:T(8,128)(2,1)S(1)} all-to-all(bf16[16,48,128]{2,1,0:T(8,128)(2,1)S(1)} %get-tuple-element.25), channel_id=1, replica_groups=mesh['section'=16,'kvp'=16,'tp'=2] {'kvp'}, dimensions={0} | all-to-all | bytes 393216 | tf_op jit(solution)/shard_map/all_to_all | solution.py:170
  57.9 7.6 %all-gather.5.cloned.1.call-done = bf16[16,2,256,128]{3,2,1,0:T(8,128)(2,1)} async-done(((bf16[2,2,256,128]{3,2,1,0:T(8,128)(2,1)}), bf16[16,2,256,128]{3,2,1,0:T(8,128)(2,1)}) %all-gather.5.cloned.1.call-update) | async-done | bytes 2097168 | tf_op jit(solution)/shard_map/all_gather | solution.py:199
  65.5 1.6 copy-done
  67.1 1.8 %attend_first.1 = bf16[16,128,128]{2,1,0:T(8,128)(2,1)S(1)} custom-call(s32[2]{0:T(128)S(1)} %pad_add_fusion.place, bf16[128,128]{1,0:T(8,128)(2,1)S(1)} %get-tuple-element.24.q_ref, bf16[8,2,2,256,128]{4,3,2,1,0:T(8,128)(2,1)S(1)} %bitcast.44, bf16[16,48,128]{2,1,0:T(8,128)(2,1)S(1)} %all_to_all.26.first), custom_call_target="tpu_custom_call" | custom-call | tf_op jit(solution)/shard_map/attend_first/pallas_call | solution.py:234
  68.9 14.2 %all_to_all.27.att = bf16[16,128,128]{2,1,0:T(8,128)(2,1)S(1)} all-to-all(bf16[16,128,128]{2,1,0:T(8,128)(2,1)S(1)} %attend_first.1), channel_id=1, replica_groups=mesh['section'=16,'kvp'=16,'tp'=2] {'kvp'}, dimensions={0} | all-to-all | bytes 1048576 | tf_op jit(solution)/shard_map/all_to_all | solution.py:170
  83.0 1.0 mix.2
  84.0 4.0 %collective-permute-start.2 = (f32[64,256]{1,0:T(8,128)S(1)}, f32[64,256]{1,0:T(8,128)}, u32[]{:S(2)}, u32[]{:S(2)}) collective-permute-start(f32[64,256]{1,0:T(8,128)S(1)} %get-tuple-element.38), channel_id=1, source_target_pairs={{0,32},{1,33},{32,64},{33,65},{64,96},{65,97},{96,128},{97,129},{1... | collective-permute-start | bytes 196616 | tf_op jit(solution)/shard_map/ppermute | solution.py:179
  88.0 10.4 %collective-permute-start.3 = (f32[64,256]{1,0:T(8,128)S(1)}, f32[64,256]{1,0:T(8,128)}, u32[]{:S(2)}, u32[]{:S(2)}) collective-permute-start(f32[64,256]{1,0:T(8,128)S(1)} %get-tuple-element.39), channel_id=1, source_target_pairs={{0,33},{1,32},{32,65},{33,64},{64,97},{65,96},{96,129},{97,128},{1... | collective-permute-start | bytes 196616 | tf_op jit(solution)/shard_map/ppermute | solution.py:179
  98.4 1.2 collective-permute-done.2
  99.6 10.6 %collective-permute-done.3 = f32[64,256]{1,0:T(8,128)} collective-permute-done((f32[64,256]{1,0:T(8,128)S(1)}, f32[64,256]{1,0:T(8,128)}, u32[]{:S(2)}, u32[]{:S(2)}) %collective-permute-start.3) | collective-permute-done | bytes 65568 | tf_op jit(solution)/shard_map/ppermute | solution.py:179
  110.2 0.9 fusion.2.x_ref
  111.1 19.1 %all_to_all.28.x = bf16[16,64,256]{2,1,0:T(8,128)(2,1)} all-to-all(bf16[16,64,256]{2,1,0:T(8,128)(2,1)S(1)} %broadcast_in_dim.21), channel_id=1, replica_groups=mesh['section'=16,'kvp'=16,'tp'=2] {'kvp'}, dimensions={0} | all-to-all | bytes 1048576 | tf_op jit(solution)/shard_map/all_to_all | solution.py:170
  130.3 1.9 %collective-permute-start.4 = (bf16[16,64,256]{2,1,0:T(8,128)(2,1)}, bf16[16,64,256]{2,1,0:T(8,128)(2,1)}, u32[]{:S(2)}, u32[]{:S(2)}) collective-permute-start(bf16[16,64,256]{2,1,0:T(8,128)(2,1)} %all_to_all.28.x), channel_id=1, source_target_pairs={{0,1},{1,0},{2,3},{3,2},{4,5},{5,4},{6,7},{7,6},{8,9},{9,8},{10,11... | collective-permute-start | bytes 1572872 | tf_op jit(solution)/shard_map/ppermute | solution.py:174
  132.2 2.5 %own_rows.1 = (bf16[64,4096]{1,0:T(8,128)(2,1)S(1)}, bf16[64,128]{1,0:T(8,128)(2,1)S(1)}, f32[64,128]{1,0:T(8,128)S(1)}, f32[64,128]{1,0:T(8,128)S(1)}, f32[64,128]{1,0:T(8,128)S(1)}) custom-call(s32[2]{0:T(128)S(1)} %pad_add_fusion.place, bf16[16,64,256]{2,1,0:T(8,128)(2,1)} %all_to_all.28.x, f32[1,4096]{1,0:T(1,128)S(1)} %copy-done.8, ...), custom_call_target="tpu_custom_call" | custom-call | tf_op jit(solution)/shard_map/own_rows/pallas_call | solution.py:245
  134.8 3.4 %other_rows.1 = (bf16[16,128,128]{2,1,0:T(8,128)(2,1)S(1)}, bf16[128,256]{1,0:T(8,128)(2,1)S(1)}) custom-call(s32[2]{0:T(128)S(1)} %pad_add_fusion.place, bf16[16,64,256]{2,1,0:T(8,128)(2,1)} %collective-permute-done.4.x, f32[1,4096]{1,0:T(1,128)S(1)} %copy-done.8, bf16[4096,128]{1,0:T(8,128)(2,1)S(1)} %bitcast.49, bf16[256,4096]{1,0:T(8,128)(2,1)S(1)} %copy-done.5, ...), custom_call_target="tpu_custom_call" | custom-call | tf_op jit(solution)/shard_map/other_rows/pallas_call | solution.py:254
  138.3 0.8 copy-done.7
  139.1 6.0 %all-to-all-start.4 = ((bf16[16,128,128]{2,1,0:T(8,128)(2,1)}), bf16[16,128,128]{2,1,0:T(8,128)(2,1)S(1)}, u32[]{:S(2)}, u32[]{:S(2)}) async-start(bf16[16,128,128]{2,1,0:T(8,128)(2,1)} %copy-done.7), calls=%async_computation.4 | async-start | bytes 1048576 | tf_op jit(solution)/shard_map/all_to_all | solution.py:170
  147.2 2.0 %collective-permute-start.6 = (bf16[128,256]{1,0:T(8,128)(2,1)S(1)}, bf16[128,256]{1,0:T(8,128)(2,1)S(1)}, u32[]{:S(2)}, u32[]{:S(2)}) collective-permute-start(bf16[128,256]{1,0:T(8,128)(2,1)S(1)} %get-tuple-element.40), channel_id=1, source_target_pairs={{0,16},{2,18},{4,20},{6,22},{8,24},{10,26},{12,28},{14,30},{16,0},... | collective-permute-start | bytes 196616 | tf_op jit(solution)/shard_map/ppermute | solution.py:265
  149.2 1.0 bitcast_select_fusion
  150.2 1.8 %select_n.73 = bf16[2,2,512,128]{3,2,1,0:T(8,128)(2,1)} dynamic-update-slice(bf16[2,2,512,128]{3,2,1,0:T(8,128)(2,1)} %bitcast.57, bf16[2,2,128,128]{3,2,1,0:T(8,128)(2,1)S(1)} %bitcast_select_fusion, s32[]{:T(128)} %constant.35.clone.1, s32[]{:T(128)} %constant.35.clone.1, s32[]{:T(128)S(6)} %select_n.69, s32[]{:T(128)} %constant.35.clone.1) | dynamic-update-slice | bytes 262148 | tf_op jit(solution)/shard_map/jit(_where)/select_n | solution.py:208
  152.1 2.6 %collective-permute-start.5 = (f32[64,256]{1,0:T(8,128)S(1)}, f32[64,256]{1,0:T(8,128)S(1)}, u32[]{:S(2)}, u32[]{:S(2)}) collective-permute-start(f32[64,256]{1,0:T(8,128)S(1)} %copy-done.11), channel_id=1, source_target_pairs={{0,1},{1,0},{2,3},{3,2},{4,5},{5,4},{6,7},{7,6},{8,9},{9,8},{10,11... | collective-permute-start | bytes 196616 | tf_op jit(solution)/shard_map/ppermute | solution.py:174
  154.8 1.0 fusion.1
  155.8 1.8 %select_n.81 = bf16[2,2,512,128]{3,2,1,0:T(8,128)(2,1)} dynamic-update-slice(bf16[2,2,512,128]{3,2,1,0:T(8,128)(2,1)} %select_n.73, bf16[2,2,128,128]{3,2,1,0:T(8,128)(2,1)S(1)} %fusion.1, s32[]{:T(128)} %constant.35.clone.1, s32[]{:T(128)} %constant.35.clone.1, s32[]{:T(128)S(6)} %select_n.78, s32[]{:T(128)} %constant.35.clone.1) | dynamic-update-slice | bytes 262148 | tf_op jit(solution)/shard_map/jit(_where)/select_n | solution.py:208
  158.0 1.0 mix.3
  158.9 4.7 %collective-permute-start.7 = (f32[64,256]{1,0:T(8,128)S(1)}, f32[64,256]{1,0:T(8,128)S(1)}, u32[]{:S(2)}, u32[]{:S(2)}) collective-permute-start(f32[64,256]{1,0:T(8,128)S(1)} %get-tuple-element.44), channel_id=1, source_target_pairs={{0,1},{1,0},{2,3},{3,2},{4,5},{5,4},{6,7},{7,6},{8,9},{9,8},{10,11... | collective-permute-start | bytes 196616 | tf_op jit(solution)/shard_map/ppermute | solution.py:174
  163.7 0.9 collective-permute-done.7
  (52 shorter events, 3.8 us)
Async XLA Ops:
  7.2 8.4 %copy-start.9 = (bf16[1,64,256]{2,1,0:T(8,128)(2,1)S(1)}, bf16[1,64,256]{2,1,0:T(8,128)(2,1)}, u32[]{:S(2)}) copy-start(bf16[1,64,256]{2,1,0:T(8,128)(2,1)} %param.9) | copy-start | bytes 98308
  7.2 35.2 %copy-start.8 = (f32[1,4096]{1,0:T(1,128)S(1)}, f32[1,4096]{1,0:T(1,128)}, u32[]{:S(2)}) copy-start(f32[1,4096]{1,0:T(1,128)} %gain.5) | copy-start | bytes 49156
  7.2 35.2 %copy-start.2 = (bf16[1,4096,1,128]{3,1,2,0:T(8,128)(2,1)S(1)}, bf16[1,4096,1,128]{3,1,2,0:T(8,128)(2,1)}, u32[]{:S(2)}) copy-start(bf16[1,4096,1,128]{3,1,2,0:T(8,128)(2,1)} %param.12) | copy-start | bytes 3145732
  7.2 35.2 %copy-start.6 = (bf16[1,4096,1,32]{1,3,2,0:T(8,128)(2,1)S(1)}, bf16[1,4096,1,32]{1,3,2,0:T(8,128)(2,1)}, u32[]{:S(2)}) copy-start(bf16[1,4096,1,32]{1,3,2,0:T(8,128)(2,1)} %param.13) | copy-start | bytes 786436
  7.2 58.3 %all-gather.5.cloned.1.call-start = ((), (), s32[]{:S(2)}) async-start(), calls=%async_computation.5 | async-start | bytes 2359296 | tf_op jit(solution)/shard_map/all_gather | solution.py:199
  8.4 7.1 %copy-start.12 = (bf16[1,2,2,512,128]{4,3,2,1,0:T(8,128)(2,1)}, bf16[1,2,2,512,128]{4,3,2,1,0:T(8,128)(2,1)S(1)}, u32[]{:S(2)}) copy-start(bf16[1,2,2,512,128]{4,3,2,1,0:T(8,128)(2,1)S(1)} %copy.27) | copy-start | bytes 1572868
  8.5 6.3 %collective-permute-start.1 = (bf16[2,256,128]{2,1,0:T(8,128)(2,1)S(1)}, bf16[2,256,128]{2,1,0:T(8,128)(2,1)S(1)}, u32[]{:S(2)}, u32[]{:S(2)}) collective-permute-start(bf16[2,256,128]{2,1,0:T(8,128)(2,1)S(1)} %get-tuple-element.51), channel_id=1, source_target_pairs={{0,16},{2,18},{4,20},{6,22},{8,24},{10,26},{12,28},{14,30},{16,0},... | collective-permute-start | bytes 393224 | tf_op jit(solution)/shard_map/ppermute | solution.py:198
  15.5 116.7 %all-gather.7.cloned.1.call-start = ((), (), s32[]{:S(2)}) async-start(), calls=%async_computation.6 | async-start | bytes 2359296 | tf_op jit(solution)/shard_map/all_gather | solution.py:230
  35.4 6.9 %collective-permute-start = (bf16[16,64,256]{2,1,0:T(8,128)(2,1)S(1)}, bf16[16,64,256]{2,1,0:T(8,128)(2,1)S(1)}, u32[]{:S(2)}, u32[]{:S(2)}) collective-permute-start(bf16[16,64,256]{2,1,0:T(8,128)(2,1)S(1)} %all_to_all.25.mine), channel_id=1, source_target_pairs={{0,1},{1,0},{2,3},{3,2},{4,5},{5,4},{6,7},{7,6},{8,9},{9,8},{10,11... | collective-permute-start | bytes 1572872 | tf_op jit(solution)/shard_map/ppermute | solution.py:174
  65.5 1.6 copy-start
  67.1 15.9 %copy-start.3 = (bf16[1,2048,256]{2,1,0:T(8,128)(2,1)S(1)}, bf16[1,2048,256]{2,1,0:T(8,128)(2,1)}, u32[]{:S(2)}) copy-start(bf16[1,2048,256]{2,1,0:T(8,128)(2,1)} %param.14) | copy-start | bytes 3145732
  68.9 63.3 %copy-start.1 = (bf16[16,2,256,128]{3,2,1,0:T(8,128)(2,1)S(1)}, bf16[16,2,256,128]{3,2,1,0:T(8,128)(2,1)}, u32[]{:S(2)}) copy-start(bf16[16,2,256,128]{3,2,1,0:T(8,128)(2,1)} %all-gather.5.cloned.1.call-done) | copy-start | bytes 6291460
  84.0 50.8 %copy-start.10 = (f32[64,256]{1,0:T(8,128)}, f32[64,256]{1,0:T(8,128)S(1)}, u32[]{:S(2)}) copy-start(f32[64,256]{1,0:T(8,128)S(1)} %get-tuple-element.39) | copy-start | bytes 196612
  84.0 15.6 %collective-permute-start.2 = (f32[64,256]{1,0:T(8,128)S(1)}, f32[64,256]{1,0:T(8,128)}, u32[]{:S(2)}, u32[]{:S(2)}) collective-permute-start(f32[64,256]{1,0:T(8,128)S(1)} %get-tuple-element.38), channel_id=1, source_target_pairs={{0,32},{1,33},{32,64},{33,65},{64,96},{65,97},{96,128},{97,129},{1... | collective-permute-start | bytes 196616 | tf_op jit(solution)/shard_map/ppermute | solution.py:179
  88.0 22.2 %collective-permute-start.3 = (f32[64,256]{1,0:T(8,128)S(1)}, f32[64,256]{1,0:T(8,128)}, u32[]{:S(2)}, u32[]{:S(2)}) collective-permute-start(f32[64,256]{1,0:T(8,128)S(1)} %get-tuple-element.39), channel_id=1, source_target_pairs={{0,33},{1,32},{32,65},{33,64},{64,97},{65,96},{96,129},{97,128},{1... | collective-permute-start | bytes 196616 | tf_op jit(solution)/shard_map/ppermute | solution.py:179
  130.3 4.5 %collective-permute-start.4 = (bf16[16,64,256]{2,1,0:T(8,128)(2,1)}, bf16[16,64,256]{2,1,0:T(8,128)(2,1)}, u32[]{:S(2)}, u32[]{:S(2)}) collective-permute-start(bf16[16,64,256]{2,1,0:T(8,128)(2,1)} %all_to_all.28.x), channel_id=1, source_target_pairs={{0,1},{1,0},{2,3},{3,2},{4,5},{5,4},{6,7},{7,6},{8,9},{9,8},{10,11... | collective-permute-start | bytes 1572872 | tf_op jit(solution)/shard_map/ppermute | solution.py:174
  132.2 2.6 %copy-start.5 = (bf16[256,4096]{1,0:T(8,128)(2,1)S(1)}, bf16[256,4096]{1,0:T(8,128)(2,1)}, u32[]{:S(2)}) copy-start(bf16[256,4096]{1,0:T(8,128)(2,1)} %all-gather.7.cloned.1.call-done.wkv) | copy-start | bytes 6291460
  134.8 10.3 %copy-start.13 = (s32[2,1]{0,1:T(1,128)S(1)}, s32[2,1]{0,1:T(1,128)}, u32[]{:S(2)}) copy-start(s32[2,1]{0,1:T(1,128)} %param.17) | copy-start | bytes 28
  138.3 0.8 copy-start.7
  139.1 13.0 %copy-start.11 = (f32[64,256]{1,0:T(8,128)S(1)}, f32[64,256]{1,0:T(8,128)}, u32[]{:S(2)}) copy-start(f32[64,256]{1,0:T(8,128)} %copy-done.10) | copy-start | bytes 196612
  139.1 18.9 %copy-start.4 = (bf16[1,2048,256]{2,1,0:T(8,128)(2,1)S(1)}, bf16[1,2048,256]{2,1,0:T(8,128)(2,1)}, u32[]{:S(2)}) copy-start(bf16[1,2048,256]{2,1,0:T(8,128)(2,1)} %param.14) | copy-start | bytes 3145732
  139.1 18.9 %all-to-all-start.4 = ((bf16[16,128,128]{2,1,0:T(8,128)(2,1)}), bf16[16,128,128]{2,1,0:T(8,128)(2,1)S(1)}, u32[]{:S(2)}, u32[]{:S(2)}) async-start(bf16[16,128,128]{2,1,0:T(8,128)(2,1)} %copy-done.7), calls=%async_computation.4 | async-start | bytes 1048576 | tf_op jit(solution)/shard_map/all_to_all | solution.py:170
  147.2 7.6 %collective-permute-start.6 = (bf16[128,256]{1,0:T(8,128)(2,1)S(1)}, bf16[128,256]{1,0:T(8,128)(2,1)S(1)}, u32[]{:S(2)}, u32[]{:S(2)}) collective-permute-start(bf16[128,256]{1,0:T(8,128)(2,1)S(1)} %get-tuple-element.40), channel_id=1, source_target_pairs={{0,16},{2,18},{4,20},{6,22},{8,24},{10,26},{12,28},{14,30},{16,0},... | collective-permute-start | bytes 196616 | tf_op jit(solution)/shard_map/ppermute | solution.py:265
  152.1 11.6 %collective-permute-start.5 = (f32[64,256]{1,0:T(8,128)S(1)}, f32[64,256]{1,0:T(8,128)S(1)}, u32[]{:S(2)}, u32[]{:S(2)}) collective-permute-start(f32[64,256]{1,0:T(8,128)S(1)} %copy-done.11), channel_id=1, source_target_pairs={{0,1},{1,0},{2,3},{3,2},{4,5},{5,4},{6,7},{7,6},{8,9},{9,8},{10,11... | collective-permute-start | bytes 196616 | tf_op jit(solution)/shard_map/ppermute | solution.py:174
  158.9 5.6 %collective-permute-start.7 = (f32[64,256]{1,0:T(8,128)S(1)}, f32[64,256]{1,0:T(8,128)S(1)}, u32[]{:S(2)}, u32[]{:S(2)}) collective-permute-start(f32[64,256]{1,0:T(8,128)S(1)} %get-tuple-element.44), channel_id=1, source_target_pairs={{0,1},{1,0},{2,3},{3,2},{4,5},{5,4},{6,7},{7,6},{8,9},{9,8},{10,11... | collective-permute-start | bytes 196616 | tf_op jit(solution)/shard_map/ppermute | solution.py:174
Sparse Core Ops, SparseCore 0:
  15.6 49.8 all-gather.4
  67.6 44.0 all-gather.6

commit v5 on v4

--- a/solution.py
+++ b/solution.py
@@ -20,6 +20,7 @@
 COLS = 256
 SCALE = 1.0 / math.sqrt(HD)
 LOW = -1e30
+MARK = 1024.0
 F32 = jnp.float32
 BF16 = jnp.bfloat16
 RINGS = [list(range(RING)), list(range(RING, N))]
@@ -51,26 +52,24 @@
     return pl.ds(pl.multiple_of(half * ROWS, ROWS), ROWS)
 
 
-def project_first(place, lens, mine, other, gain, wq, wkv, q_out, kv_out, normed):
+def project_first(place, mine, other, gain, wq, wkv, q_out, kv_out, normed):
     t = place[0]
     normalise(mine, gain, normed, half_rows(t))
     normalise(other, gain, normed, half_rows(1 - t))
     q_out[...] = dot(normed[...], wq[...]).astype(BF16)
     kv = dot_t(wkv[...], normed[...]).astype(BF16)
-    filled = jnp.full((16, SPAN), lens[0].astype(F32), F32).astype(BF16)
-    for j in range(N):
-        kv_out[j, 0:32] = kv
-        kv_out[j, 32:48] = filled
-
-
-def over_prefixes(g, q, held, first, scores):
+    for j in range(RING):
+        kv_out[j] = kv
+
+
+def over_prefixes(q, held, scores):
     count = q.shape[0]
     slot = lax.broadcasted_iota(jnp.int32, (1, PRE), 1).astype(F32)
     top = jnp.full((count, PRE), LOW, F32)
     for k in range(RING):
         for o in range(2):
-            shard = (g if o == 0 else 1 - g) * RING + k
-            filled = first[shard, 32:48][0:1].astype(F32)
+            mark = held[k, o, 0, PRE - 16 : PRE][15:16].astype(F32)
+            filled = jnp.where(mark > MARK / 2, mark / MARK, float(PRE))
             filled = jnp.concatenate([filled, filled], axis=1)
             s = dot_t(q, held[k, o, 0]) * SCALE
             s = jnp.where(slot < filled, s, LOW)
@@ -108,17 +107,17 @@
     return (acc / total).astype(BF16)
 
 
-def first_span(g, q, first):
-    keys = jnp.concatenate([first[g * RING + i, 0:32] for i in range(4)], axis=0)
-    values = jnp.concatenate([first[g * RING + 4 + i, 0:32] for i in range(4)], axis=0)
+def first_span(q, first):
+    keys = jnp.concatenate([first[i] for i in range(4)], axis=0)
+    values = jnp.concatenate([first[4 + i] for i in range(4)], axis=0)
     return dot(q, keys) * SCALE, lambda e: dot_t(e, values)
 
 
 def attend_first(place, q_ref, held, first, out, scores):
     g = place[1]
     q = q_ref[...]
-    top, total, acc = over_prefixes(g, q, held, first, scores)
-    result = with_spans(0, top, total, acc, [first_span(g, q, first)])
+    top, total, acc = over_prefixes(q, held, scores)
+    result = with_spans(0, top, total, acc, [first_span(q, first)])
     for j in range(N):
         out[j] = result
 
@@ -127,7 +126,7 @@
     normalise(x, gain, normed, slice(0, ROWS))
     q = dot(normed[...], wq[...]).astype(BF16)
     q_out[...] = q
-    top, total, acc = over_prefixes(place[1], q, held, first, scores)
+    top, total, acc = over_prefixes(q, held, scores)
     top_out[...] = jnp.broadcast_to(top, (ROWS, HD))
     sum_out[...] = jnp.broadcast_to(total, (ROWS, HD))
     acc_out[...] = acc
@@ -143,14 +142,14 @@
     both = dot_t(both, wkv[...]).astype(BF16)
     kv[half_rows(t), :] = both[0:ROWS]
     kv[half_rows(1 - t), :] = both[ROWS:SPAN]
-    top, total, acc = over_prefixes(g, q, held, first, scores)
+    top, total, acc = over_prefixes(q, held, scores)
     keys, values = kv[:, 0:HD], kv[:, HD : 2 * HD]
     parts = (
         (t, q_own[...], top_own[:, 0:1], sum_own[:, 0:1], acc_own[...]),
         (1 - t, q, top, total, acc),
     )
     for half, q, top, total, acc in parts:
-        spans = [first_span(g, q, first), (dot_t(q, keys) * SCALE, lambda e: dot(e, values))]
+        spans = [first_span(q, first), (dot_t(q, keys) * SCALE, lambda e: dot(e, values))]
         result = with_spans(half * ROWS, top, total, acc, spans)
         for j in range(N):
             out[j, half_rows(half), :] = result
@@ -193,6 +192,9 @@
     cache_here = cache[0]
 
     prefix = cache_here[:, :, :PRE, :]
+    last = prefix[0:1, :, PRE - 1 : PRE]
+    last = jnp.where(filled < PRE, (filled.astype(F32) * MARK).astype(BF16), last)
+    prefix = lax.dynamic_update_slice(prefix, last, (0, 0, PRE - 1, 0))
     own = lax.dynamic_index_in_dim(prefix, g, 1, False)
     give = lax.dynamic_index_in_dim(prefix, 1 - g, 1, False)
     got = lax.ppermute(give, "kvp", [(i, (i + RING) % N) for i in range(N)])
@@ -200,14 +202,14 @@
 
     wkv_t = wkv_here.T
 
-    def updated(cache_now, fresh, moment):
+    def updated(cache_now, fresh, moment, owner):
         start = filled
         for u in range(moment):
             start = start + jnp.where(owner[u, 0] == shard_id, SPAN, 0).astype(jnp.int32)
         changed = lax.dynamic_update_slice(cache_now, fresh, (0, 0, start, 0))
         return jnp.where(owner[moment, 0] == shard_id, changed, cache_now)
 
-    sums, fresh_all = [], []
+    sums = []
     x = entering[0]
     for moment in range(NCH):
         if moment:
@@ -218,19 +220,18 @@
         if moment == 0:
             q, kv = pl.pallas_call(
                 project_first,
-                out_shape=(shape(SPAN, HD), shape(N, 48, SPAN)),
-                in_specs=[SMEM, SMEM] + [VMEM] * 5,
+                out_shape=(shape(SPAN, HD), shape(RING, 32, SPAN)),
+                in_specs=[SMEM] + [VMEM] * 5,
                 out_specs=(VMEM, VMEM),
                 scratch_shapes=[pltpu.VMEM((SPAN, D), BF16)],
                 compiler_params=PARAMS,
                 name="project_first",
-            )(place, filled[None], mine, other, gain, wq_here, wkv_t)
-            first = spread(kv)
+            )(place, mine, other, gain, wq_here, wkv_t)
+            first = lax.all_to_all(kv, "kvp", 0, 0, tiled=True, axis_index_groups=RINGS)
             wkv_late, first = lax.optimization_barrier((wkv_t, first))
             wkv_all = lax.all_gather(wkv_late, "kvp", axis_index_groups=RINGS)
             wkv_all = wkv_all.reshape(2 * HD, D)
-            both = jnp.transpose(first[:, 0:32].reshape(2, 2, HD, SPAN), (1, 0, 3, 2))
-            fresh_all.append(both)
+            kv_first = first.reshape(2 * HD, SPAN).T
             att = pl.pallas_call(
                 attend_first,
                 out_shape=shape(N, SPAN, HD),
@@ -260,17 +261,18 @@
                 compiler_params=PARAMS,
                 name="other_rows",
             )(place, other, gain, wq_here, wkv_all, held, first, *own_state)
-            late, kv = lax.optimization_barrier((sums[0], kv))
+            late, kv_first, kv = lax.optimization_barrier((sums[0], kv_first, kv))
             sums[0] = late
-            pair = lax.ppermute(kv, "kvp", [(i, (i + RING) % N) for i in range(N)])
-            heads = jnp.where(g == 0, jnp.stack([kv, pair]), jnp.stack([pair, kv]))
-            both = jnp.transpose(heads.reshape(2, SPAN, 2, HD), (2, 0, 1, 3))
-            fresh_all.append(both)
+            both = []
+            for here in (kv_first, kv):
+                pair = lax.ppermute(here, "kvp", [(i, (i + RING) % N) for i in range(N)])
+                heads = jnp.where(g == 0, jnp.stack([here, pair]), jnp.stack([pair, here]))
+                both.append(jnp.transpose(heads.reshape(2, SPAN, 2, HD), (2, 0, 1, 3)))
         att = spread(att)
         if moment:
             new_cache = cache_here
             for u in range(NCH):
-                new_cache = updated(new_cache, fresh_all[u], u)
+                new_cache = updated(new_cache, both[u], u, owner)
             new_cache, att = lax.optimization_barrier((new_cache, att))
         own_sum, other_sum = pl.pallas_call(
             mix,

time: 174 us -> 173 us (level)
  waiting for transfers between devices: 25.2 us -> 22.2 us
  local copies, waits for them, and re-layouts: 8.22 us -> 10.4 us
    all_to_all x4 -> x3, blocking collectives: 67.1 us -> 54.6 us  [spread(): return lax.all_to_all(block, 'kvp', 0, 0, tiled=True)]
    all_to_all x0 -> x1, blocking collectives: none -> 12.1 us  [body(): first = lax.all_to_all(kv, 'kvp', 0, 0, tiled=True, axis_index_groups=RINGS)]
    ppermute x1 -> x2, starting transfers between devices: 2.01 us -> 5.27 us  [body(): pair = lax.ppermute(here, 'kvp', [(i, (i + RING) % N) for i in range(N)])]
    ppermute x4, starting transfers between devices: 14.6 us -> 12.3 us  [swap(): return lax.ppermute(block, 'tp', [(0, 1), (1, 0)])]
    unnamed x29 -> x28, local copies, waits for them, and re-layouts: 3.57 us -> 5.65 us
  transfers between devices with their start and end apart: 11 -> 12, of which waited for: 8 -> 5; matrix products, arithmetic and copies ran while one was open for 4% -> 5% of each run, Pallas kernels for 5% -> 5%
where the time goes in v5:
time: 173 us; the launch traced here: 172 us
  blocking collectives  66.7 us (39%)
  starting transfers between devices  40.8 us (24%)
  waiting for transfers between devices  22.2 us (13%)
  between operations  16.4 us (9%)
  Pallas kernels  11.2 us (6%)
  local copies, waits for them, and re-layouts  10.4 us (6%)
  other arithmetic  4.21 us (2%)
    all_to_all x3, blocking collectives, spread(): return lax.all_to_all(block, 'kvp', 0, 0, tiled=True)  54.6 us
    ppermute x2, starting transfers between devices, onward(): return lax.ppermute(block, ('section', 'tp'), route)  14.6 us
    ppermute x4, starting transfers between devices, swap(): return lax.ppermute(block, 'tp', [(0, 1), (1, 0)])  12.3 us
    all_to_all x1, blocking collectives, body(): first = lax.all_to_all(kv, 'kvp', 0, 0, tiled=True, axis_index_groups=RINGS)  12.1 us
    ppermute x2, waiting for transfers between devices, onward(): return lax.ppermute(block, ('section', 'tp'), route)  10.6 us
    all_to_all x1, starting transfers between devices, spread(): return lax.all_to_all(block, 'kvp', 0, 0, tiled=True)  6.05 us
    all_gather x1, waiting for transfers between devices, body(): held = lax.all_gather(jnp.stack([own, got]), 'kvp', axis_index_groups=RINGS)  5.94 us
    unnamed x28, local copies, waits for them, and re-layouts  5.65 us
  transfers between devices with their start and end apart: 12, of which 5 were waited for; matrix products, arithmetic and copies ran while one was open for 5% of the time, Pallas kernels for 5%

profile of v5, /device:TPU:7, one launch (start us, length us, event | category | flops | bytes accessed | tf_op | source)
XLA Modules:
  0.0 171.9 jit_solution(15758502110271943481)
XLA Ops:
  7.9 1.2 copy.50
  9.2 2.5 %collective-permute-start.1 = (bf16[2,256,128]{2,1,0:T(8,128)(2,1)S(1)}, bf16[2,256,128]{2,1,0:T(8,128)(2,1)S(1)}, u32[]{:S(2)}, u32[]{:S(2)}) collective-permute-start(bf16[2,256,128]{2,1,0:T(8,128)(2,1)S(1)} %get-tuple-element.57), channel_id=1, source_target_pairs={{0,16},{2,18},{4,20},{6,22},{8,24},{10,26},{12,28},{14,30},{16,0},... | collective-permute-start | bytes 393224 | tf_op jit(solution)/shard_map/ppermute | solution.py:200
  11.7 3.8 %collective-permute-done.1 = bf16[2,256,128]{2,1,0:T(8,128)(2,1)S(1)} collective-permute-done((bf16[2,256,128]{2,1,0:T(8,128)(2,1)S(1)}, bf16[2,256,128]{2,1,0:T(8,128)(2,1)S(1)}, u32[]{:S(2)}, u32[]{:S(2)}) %collective-permute-start.1) | collective-permute-done | bytes 131104 | tf_op jit(solution)/shard_map/ppermute | solution.py:200
  16.4 19.8 %all_to_all.25.mine = bf16[16,64,256]{2,1,0:T(8,128)(2,1)S(1)} all-to-all(bf16[16,64,256]{2,1,0:T(8,128)(2,1)S(1)} %broadcast_in_dim.24), channel_id=1, replica_groups=mesh['section'=16,'kvp'=16,'tp'=2] {'kvp'}, dimensions={0} | all-to-all | bytes 1048576 | tf_op jit(solution)/shard_map/all_to_all | solution.py:169
  36.2 5.4 %collective-permute-start = (bf16[16,64,256]{2,1,0:T(8,128)(2,1)S(1)}, bf16[16,64,256]{2,1,0:T(8,128)(2,1)S(1)}, u32[]{:S(2)}, u32[]{:S(2)}) collective-permute-start(bf16[16,64,256]{2,1,0:T(8,128)(2,1)S(1)} %all_to_all.25.mine), channel_id=1, source_target_pairs={{0,1},{1,0},{2,3},{3,2},{4,5},{5,4},{6,7},{7,6},{8,9},{9,8},{10,11... | collective-permute-start | bytes 1572872 | tf_op jit(solution)/shard_map/ppermute | solution.py:173
  41.7 1.4 collective-permute-done.other
  43.1 1.6 project_first.1
  44.7 12.1 %all_to_all.26.first = bf16[8,32,128]{2,1,0:T(8,128)(2,1)S(1)} all-to-all(bf16[8,32,128]{2,1,0:T(8,128)(2,1)S(1)} %get-tuple-element.26), channel_id=1, replica_groups={{0,2,4,6,8,10,12,14},{16,18,20,22,24,26,28,30},{1,3,5,7,9,11,13,15},{17..., dimensions={0} | all-to-all | bytes 131072 | tf_op jit(solution)/shard_map/all_to_all | solution.py:230
  56.8 5.9 %all-gather.5.cloned.1.call-done = bf16[16,2,256,128]{3,2,1,0:T(8,128)(2,1)} async-done(((bf16[2,2,256,128]{3,2,1,0:T(8,128)(2,1)}), bf16[16,2,256,128]{3,2,1,0:T(8,128)(2,1)}) %all-gather.5.cloned.1.call-update) | async-done | bytes 2097168 | tf_op jit(solution)/shard_map/all_gather | solution.py:201
  62.8 1.6 copy-done
  64.4 1.8 %attend_first.1 = bf16[16,128,128]{2,1,0:T(8,128)(2,1)S(1)} custom-call(s32[2]{0:T(128)S(1)} %pad_add_fusion.place, bf16[128,128]{1,0:T(8,128)(2,1)S(1)} %get-tuple-element.25.q_ref, bf16[8,2,2,256,128]{4,3,2,1,0:T(8,128)(2,1)S(1)} %bitcast.52, bf16[8,32,128]{2,1,0:T(8,128)(2,1)S(1)} %all_to_all.26.first), custom_call_target="tpu_custom_call" | custom-call | tf_op jit(solution)/shard_map/attend_first/pallas_call | solution.py:235
  66.1 15.0 %all_to_all.27.att = bf16[16,128,128]{2,1,0:T(8,128)(2,1)S(1)} all-to-all(bf16[16,128,128]{2,1,0:T(8,128)(2,1)S(1)} %attend_first.1), channel_id=1, replica_groups=mesh['section'=16,'kvp'=16,'tp'=2] {'kvp'}, dimensions={0} | all-to-all | bytes 1048576 | tf_op jit(solution)/shard_map/all_to_all | solution.py:169
  81.2 1.2 copy-done.3
  82.4 1.0 mix.2
  83.4 4.5 %collective-permute-start.2 = (f32[64,256]{1,0:T(8,128)S(1)}, f32[64,256]{1,0:T(8,128)S(1)}, u32[]{:S(2)}, u32[]{:S(2)}) collective-permute-start(f32[64,256]{1,0:T(8,128)S(1)} %get-tuple-element.39), channel_id=1, source_target_pairs={{0,32},{1,33},{32,64},{33,65},{64,96},{65,97},{96,128},{97,129},{1... | collective-permute-start | bytes 196616 | tf_op jit(solution)/shard_map/ppermute | solution.py:178
  87.8 10.2 %collective-permute-start.3 = (f32[64,256]{1,0:T(8,128)S(1)}, f32[64,256]{1,0:T(8,128)S(1)}, u32[]{:S(2)}, u32[]{:S(2)}) collective-permute-start(f32[64,256]{1,0:T(8,128)S(1)} %get-tuple-element.40), channel_id=1, source_target_pairs={{0,33},{1,32},{32,65},{33,64},{64,97},{65,96},{96,129},{97,128},{1... | collective-permute-start | bytes 196616 | tf_op jit(solution)/shard_map/ppermute | solution.py:178
  98.0 10.6 %collective-permute-done.3 = f32[64,256]{1,0:T(8,128)S(1)} collective-permute-done((f32[64,256]{1,0:T(8,128)S(1)}, f32[64,256]{1,0:T(8,128)S(1)}, u32[]{:S(2)}, u32[]{:S(2)}) %collective-permute-start.3) | collective-permute-done | bytes 65568 | tf_op jit(solution)/shard_map/ppermute | solution.py:178
  109.4 19.8 %all_to_all.28.x = bf16[16,64,256]{2,1,0:T(8,128)(2,1)} all-to-all(bf16[16,64,256]{2,1,0:T(8,128)(2,1)S(1)} %broadcast_in_dim.26), channel_id=1, replica_groups=mesh['section'=16,'kvp'=16,'tp'=2] {'kvp'}, dimensions={0} | all-to-all | bytes 1048576 | tf_op jit(solution)/shard_map/all_to_all | solution.py:169
  129.2 1.9 %collective-permute-start.4 = (bf16[16,64,256]{2,1,0:T(8,128)(2,1)}, bf16[16,64,256]{2,1,0:T(8,128)(2,1)}, u32[]{:S(2)}, u32[]{:S(2)}) collective-permute-start(bf16[16,64,256]{2,1,0:T(8,128)(2,1)} %all_to_all.28.x), channel_id=1, source_target_pairs={{0,1},{1,0},{2,3},{3,2},{4,5},{5,4},{6,7},{7,6},{8,9},{9,8},{10,11... | collective-permute-start | bytes 1572872 | tf_op jit(solution)/shard_map/ppermute | solution.py:173
  131.2 2.5 %own_rows.1 = (bf16[64,4096]{1,0:T(8,128)(2,1)S(1)}, bf16[64,128]{1,0:T(8,128)(2,1)S(1)}, f32[64,128]{1,0:T(8,128)S(1)}, f32[64,128]{1,0:T(8,128)S(1)}, f32[64,128]{1,0:T(8,128)S(1)}) custom-call(s32[2]{0:T(128)S(1)} %pad_add_fusion.place, bf16[16,64,256]{2,1,0:T(8,128)(2,1)} %all_to_all.28.x, f32[1,4096]{1,0:T(1,128)S(1)} %copy-done.8, ...), custom_call_target="tpu_custom_call" | custom-call | tf_op jit(solution)/shard_map/own_rows/pallas_call | solution.py:246
  133.7 3.4 %other_rows.1 = (bf16[16,128,128]{2,1,0:T(8,128)(2,1)S(1)}, bf16[128,256]{1,0:T(8,128)(2,1)S(1)}) custom-call(s32[2]{0:T(128)S(1)} %pad_add_fusion.place, bf16[16,64,256]{2,1,0:T(8,128)(2,1)} %collective-permute-done.4.x, f32[1,4096]{1,0:T(1,128)S(1)} %copy-done.8, bf16[4096,128]{1,0:T(8,128)(2,1)S(1)} %bitcast.57, bf16[256,4096]{1,0:T(8,128)(2,1)S(1)} %copy-done.5, ...), custom_call_target="tpu_custom_call" | custom-call | tf_op jit(solution)/shard_map/other_rows/pallas_call | solution.py:255
  138.0 6.0 %all-to-all-start.4 = ((bf16[16,128,128]{2,1,0:T(8,128)(2,1)}), bf16[16,128,128]{2,1,0:T(8,128)(2,1)S(1)}, u32[]{:S(2)}, u32[]{:S(2)}) async-start(bf16[16,128,128]{2,1,0:T(8,128)(2,1)} %copy-done.7), calls=%async_computation.4 | async-start | bytes 1048576 | tf_op jit(solution)/shard_map/all_to_all | solution.py:169
  144.0 2.0 %collective-permute-start.6 = (bf16[128,256]{0,1:T(8,128)(2,1)S(1)}, bf16[128,256]{0,1:T(8,128)(2,1)S(1)}, u32[]{:S(2)}, u32[]{:S(2)}) collective-permute-start(bf16[128,256]{0,1:T(8,128)(2,1)S(1)} %bitcast.60), channel_id=1, source_target_pairs={{0,16},{2,18},{4,20},{6,22},{8,24},{10,26},{12,28},{14,30},{16,0},... | collective-permute-start | bytes 196616 | tf_op jit(solution)/shard_map/ppermute | solution.py:268
  147.9 3.3 %collective-permute-start.7 = (bf16[128,256]{1,0:T(8,128)(2,1)S(1)}, bf16[128,256]{1,0:T(8,128)(2,1)S(1)}, u32[]{:S(2)}, u32[]{:S(2)}) collective-permute-start(bf16[128,256]{1,0:T(8,128)(2,1)S(1)} %get-tuple-element.42), channel_id=1, source_target_pairs={{0,16},{2,18},{4,20},{6,22},{8,24},{10,26},{12,28},{14,30},{16,0},... | collective-permute-start | bytes 196616 | tf_op jit(solution)/shard_map/ppermute | solution.py:268
  151.4 3.1 %collective-permute-start.5 = (f32[64,256]{1,0:T(8,128)S(1)}, f32[64,256]{1,0:T(8,128)S(1)}, u32[]{:S(2)}, u32[]{:S(2)}) collective-permute-start(f32[64,256]{1,0:T(8,128)S(1)} %get-tuple-element.40), channel_id=1, source_target_pairs={{0,1},{1,0},{2,3},{3,2},{4,5},{5,4},{6,7},{7,6},{8,9},{9,8},{10,11... | collective-permute-start | bytes 196616 | tf_op jit(solution)/shard_map/ppermute | solution.py:173
  154.6 1.0 fusion.1
  155.6 1.8 %select_n.90 = bf16[2,2,512,128]{3,2,0,1:T(8,128)(2,1)} dynamic-update-slice(bf16[2,2,512,128]{3,2,0,1:T(8,128)(2,1)} %bitcast.68, bf16[2,2,128,128]{3,2,0,1:T(8,128)(2,1)S(1)} %fusion.1, s32[]{:T(128)} %constant.38.clone.1, s32[]{:T(128)} %constant.38.clone.1, s32[]{:T(128)S(6)} %select_n.86, s32[]{:T(128)} %constant.38.clone.1) | dynamic-update-slice | bytes 262148 | tf_op jit(solution)/shard_map/jit(_where)/select_n | solution.py:210
  157.5 1.0 fusion.3
  158.5 1.8 %select_n.97 = bf16[2,2,512,128]{3,2,0,1:T(8,128)(2,1)} dynamic-update-slice(bf16[2,2,512,128]{3,2,0,1:T(8,128)(2,1)} %select_n.90, bf16[2,2,128,128]{3,2,0,1:T(8,128)(2,1)S(1)} %fusion.3, s32[]{:T(128)} %constant.38.clone.1, s32[]{:T(128)} %constant.38.clone.1, s32[]{:T(128)S(6)} %select_n.94, s32[]{:T(128)} %constant.38.clone.1) | dynamic-update-slice | bytes 262148 | tf_op jit(solution)/shard_map/jit(_where)/select_n | solution.py:210
  160.3 1.0 mix.3
  161.3 1.9 %collective-permute-start.8 = (f32[64,256]{1,0:T(8,128)S(1)}, f32[64,256]{1,0:T(8,128)S(1)}, u32[]{:S(2)}, u32[]{:S(2)}) collective-permute-start(f32[64,256]{1,0:T(8,128)S(1)} %get-tuple-element.46), channel_id=1, source_target_pairs={{0,1},{1,0},{2,3},{3,2},{4,5},{5,4},{6,7},{7,6},{8,9},{9,8},{10,11... | collective-permute-start | bytes 196616 | tf_op jit(solution)/shard_map/ppermute | solution.py:173
  163.2 0.8 copy.47
  (55 shorter events, 4.6 us)
Async XLA Ops:
  7.2 9.2 %copy-start.9 = (bf16[1,64,256]{2,1,0:T(8,128)(2,1)S(1)}, bf16[1,64,256]{2,1,0:T(8,128)(2,1)}, u32[]{:S(2)}) copy-start(bf16[1,64,256]{2,1,0:T(8,128)(2,1)} %param.9) | copy-start | bytes 98308
  7.2 55.6 %all-gather.5.cloned.1.call-start = ((), (), s32[]{:S(2)}) async-start(), calls=%async_computation.5 | async-start | bytes 2359296 | tf_op jit(solution)/shard_map/all_gather | solution.py:201
  7.9 35.3 %copy-start.2 = (bf16[1,4096,1,128]{3,1,2,0:T(8,128)(2,1)S(1)}, bf16[1,4096,1,128]{3,1,2,0:T(8,128)(2,1)}, u32[]{:S(2)}) copy-start(bf16[1,4096,1,128]{3,1,2,0:T(8,128)(2,1)} %param.12) | copy-start | bytes 3145732
  7.9 35.2 %copy-start.6 = (bf16[1,4096,1,32]{1,3,2,0:T(8,128)(2,1)S(1)}, bf16[1,4096,1,32]{1,3,2,0:T(8,128)(2,1)}, u32[]{:S(2)}) copy-start(bf16[1,4096,1,32]{1,3,2,0:T(8,128)(2,1)} %param.13) | copy-start | bytes 786436
  7.9 35.2 %copy-start.8 = (f32[1,4096]{1,0:T(1,128)S(1)}, f32[1,4096]{1,0:T(1,128)}, u32[]{:S(2)}) copy-start(f32[1,4096]{1,0:T(1,128)} %gain.5) | copy-start | bytes 49156
  9.1 7.2 %copy-start.10 = (bf16[1,2,2,512,128]{4,3,1,2,0:T(8,128)(2,1)}, bf16[1,2,2,512,128]{4,3,1,2,0:T(8,128)(2,1)S(1)}, u32[]{:S(2)}) copy-start(bf16[1,2,2,512,128]{4,3,1,2,0:T(8,128)(2,1)S(1)} %copy.50) | copy-start | bytes 1572868
  9.2 6.3 %collective-permute-start.1 = (bf16[2,256,128]{2,1,0:T(8,128)(2,1)S(1)}, bf16[2,256,128]{2,1,0:T(8,128)(2,1)S(1)}, u32[]{:S(2)}, u32[]{:S(2)}) collective-permute-start(bf16[2,256,128]{2,1,0:T(8,128)(2,1)S(1)} %get-tuple-element.57), channel_id=1, source_target_pairs={{0,16},{2,18},{4,20},{6,22},{8,24},{10,26},{12,28},{14,30},{16,0},... | collective-permute-start | bytes 393224 | tf_op jit(solution)/shard_map/ppermute | solution.py:200
  16.3 114.9 %all-gather.7.cloned.1.call-start = ((), (), s32[]{:S(2)}) async-start(), calls=%async_computation.6 | async-start | bytes 2359296 | tf_op jit(solution)/shard_map/all_gather | solution.py:232
  36.2 6.9 %collective-permute-start = (bf16[16,64,256]{2,1,0:T(8,128)(2,1)S(1)}, bf16[16,64,256]{2,1,0:T(8,128)(2,1)S(1)}, u32[]{:S(2)}, u32[]{:S(2)}) collective-permute-start(bf16[16,64,256]{2,1,0:T(8,128)(2,1)S(1)} %all_to_all.25.mine), channel_id=1, source_target_pairs={{0,1},{1,0},{2,3},{3,2},{4,5},{5,4},{6,7},{7,6},{8,9},{9,8},{10,11... | collective-permute-start | bytes 1572872 | tf_op jit(solution)/shard_map/ppermute | solution.py:173
  62.8 1.6 copy-start
  66.1 65.0 %copy-start.1 = (bf16[16,2,256,128]{3,2,1,0:T(8,128)(2,1)S(1)}, bf16[16,2,256,128]{3,2,1,0:T(8,128)(2,1)}, u32[]{:S(2)}) copy-start(bf16[16,2,256,128]{3,2,1,0:T(8,128)(2,1)} %all-gather.5.cloned.1.call-done) | copy-start | bytes 6291460
  81.2 1.2 copy-start.3
  83.4 14.7 %collective-permute-start.2 = (f32[64,256]{1,0:T(8,128)S(1)}, f32[64,256]{1,0:T(8,128)S(1)}, u32[]{:S(2)}, u32[]{:S(2)}) collective-permute-start(f32[64,256]{1,0:T(8,128)S(1)} %get-tuple-element.39), channel_id=1, source_target_pairs={{0,32},{1,33},{32,64},{33,65},{64,96},{65,97},{96,128},{97,129},{1... | collective-permute-start | bytes 196616 | tf_op jit(solution)/shard_map/ppermute | solution.py:178
  87.8 20.8 %collective-permute-start.3 = (f32[64,256]{1,0:T(8,128)S(1)}, f32[64,256]{1,0:T(8,128)S(1)}, u32[]{:S(2)}, u32[]{:S(2)}) collective-permute-start(f32[64,256]{1,0:T(8,128)S(1)} %get-tuple-element.40), channel_id=1, source_target_pairs={{0,33},{1,32},{32,65},{33,64},{64,97},{65,96},{96,129},{97,128},{1... | collective-permute-start | bytes 196616 | tf_op jit(solution)/shard_map/ppermute | solution.py:178
  129.2 4.5 %collective-permute-start.4 = (bf16[16,64,256]{2,1,0:T(8,128)(2,1)}, bf16[16,64,256]{2,1,0:T(8,128)(2,1)}, u32[]{:S(2)}, u32[]{:S(2)}) collective-permute-start(bf16[16,64,256]{2,1,0:T(8,128)(2,1)} %all_to_all.28.x), channel_id=1, source_target_pairs={{0,1},{1,0},{2,3},{3,2},{4,5},{5,4},{6,7},{7,6},{8,9},{9,8},{10,11... | collective-permute-start | bytes 1572872 | tf_op jit(solution)/shard_map/ppermute | solution.py:173
  131.1 2.6 %copy-start.5 = (bf16[256,4096]{1,0:T(8,128)(2,1)S(1)}, bf16[256,4096]{1,0:T(8,128)(2,1)}, u32[]{:S(2)}) copy-start(bf16[256,4096]{1,0:T(8,128)(2,1)} %all-gather.7.cloned.1.call-done.wkv) | copy-start | bytes 6291460
  133.7 12.3 %copy-start.12 = (s32[2,1]{0,1:T(1,128)S(1)}, s32[2,1]{0,1:T(1,128)}, u32[]{:S(2)}) copy-start(s32[2,1]{0,1:T(1,128)} %param.17) | copy-start | bytes 28
  137.2 0.8 copy-start.7
  138.0 22.3 %copy-start.4 = (bf16[1,2048,256]{2,1,0:T(8,128)(2,1)S(1)}, bf16[1,2048,256]{2,1,0:T(8,128)(2,1)}, u32[]{:S(2)}) copy-start(bf16[1,2048,256]{2,1,0:T(8,128)(2,1)} %param.14) | copy-start | bytes 3145732
  138.0 22.3 %all-to-all-start.4 = ((bf16[16,128,128]{2,1,0:T(8,128)(2,1)}), bf16[16,128,128]{2,1,0:T(8,128)(2,1)S(1)}, u32[]{:S(2)}, u32[]{:S(2)}) async-start(bf16[16,128,128]{2,1,0:T(8,128)(2,1)} %copy-done.7), calls=%async_computation.4 | async-start | bytes 1048576 | tf_op jit(solution)/shard_map/all_to_all | solution.py:169
  144.0 10.5 %collective-permute-start.6 = (bf16[128,256]{0,1:T(8,128)(2,1)S(1)}, bf16[128,256]{0,1:T(8,128)(2,1)S(1)}, u32[]{:S(2)}, u32[]{:S(2)}) collective-permute-start(bf16[128,256]{0,1:T(8,128)(2,1)S(1)} %bitcast.60), channel_id=1, source_target_pairs={{0,16},{2,18},{4,20},{6,22},{8,24},{10,26},{12,28},{14,30},{16,0},... | collective-permute-start | bytes 196616 | tf_op jit(solution)/shard_map/ppermute | solution.py:268
  147.9 9.5 %collective-permute-start.7 = (bf16[128,256]{1,0:T(8,128)(2,1)S(1)}, bf16[128,256]{1,0:T(8,128)(2,1)S(1)}, u32[]{:S(2)}, u32[]{:S(2)}) collective-permute-start(bf16[128,256]{1,0:T(8,128)(2,1)S(1)} %get-tuple-element.42), channel_id=1, source_target_pairs={{0,16},{2,18},{4,20},{6,22},{8,24},{10,26},{12,28},{14,30},{16,0},... | collective-permute-start | bytes 196616 | tf_op jit(solution)/shard_map/ppermute | solution.py:268
  151.4 11.8 %collective-permute-start.5 = (f32[64,256]{1,0:T(8,128)S(1)}, f32[64,256]{1,0:T(8,128)S(1)}, u32[]{:S(2)}, u32[]{:S(2)}) collective-permute-start(f32[64,256]{1,0:T(8,128)S(1)} %get-tuple-element.40), channel_id=1, source_target_pairs={{0,1},{1,0},{2,3},{3,2},{4,5},{5,4},{6,7},{7,6},{8,9},{9,8},{10,11... | collective-permute-start | bytes 196616 | tf_op jit(solution)/shard_map/ppermute | solution.py:173
  160.3 2.9 %copy-start.11 = (bf16[2,2,512,128]{3,2,0,1:T(8,128)(2,1)S(1)}, bf16[2,2,512,128]{3,2,0,1:T(8,128)(2,1)}, u32[]{:S(2)}) copy-start(bf16[2,2,512,128]{3,2,0,1:T(8,128)(2,1)} %select_n.97) | copy-start | bytes 1572868
  161.3 3.1 %collective-permute-start.8 = (f32[64,256]{1,0:T(8,128)S(1)}, f32[64,256]{1,0:T(8,128)S(1)}, u32[]{:S(2)}, u32[]{:S(2)}) collective-permute-start(f32[64,256]{1,0:T(8,128)S(1)} %get-tuple-element.46), channel_id=1, source_target_pairs={{0,1},{1,0},{2,3},{3,2},{4,5},{5,4},{6,7},{7,6},{8,9},{9,8},{10,11... | collective-permute-start | bytes 196616 | tf_op jit(solution)/shard_map/ppermute | solution.py:173
Sparse Core Ops, SparseCore 0:
  16.4 46.3 all-gather.4
  64.8 45.2 all-gather.6

commit v6 on v5

--- a/solution.py
+++ b/solution.py
@@ -113,7 +113,7 @@
     return dot(q, keys) * SCALE, lambda e: dot_t(e, values)
 
 
-def attend_first(place, q_ref, held, first, out, scores):
+def attend_first(place, q_ref, held, first, wo, out, scores):
     g = place[1]
     q = q_ref[...]
     top, total, acc = over_prefixes(q, held, scores)
@@ -235,12 +235,12 @@
             att = pl.pallas_call(
                 attend_first,
                 out_shape=shape(N, SPAN, HD),
-                in_specs=[SMEM] + [VMEM] * 3,
+                in_specs=[SMEM] + [VMEM] * 4,
                 out_specs=VMEM,
                 scratch_shapes=[pltpu.VMEM((SPAN, N * PRE), F32)],
                 compiler_params=PARAMS,
                 name="attend_first",
-            )(place, q, held, first)
+            )(place, q, held, first, wo_here)
         else:
             mine, wkv_all = lax.optimization_barrier((mine, wkv_all))
             own_state = pl.pallas_call(

time: 173 us -> 172 us (level)
    unnamed x28 -> x34, local copies, waits for them, and re-layouts: 5.65 us -> 4.45 us
where the time goes in v6:
time: 172 us; the launch traced here: 171 us
  blocking collectives  65.6 us (38%)
  starting transfers between devices  40.8 us (24%)
  waiting for transfers between devices  23.7 us (14%)
  between operations  16.4 us (10%)
  Pallas kernels  11.2 us (7%)
  local copies, waits for them, and re-layouts  9.18 us (5%)
  other arithmetic  4.29 us (2%)
    all_to_all x3, blocking collectives, spread(): return lax.all_to_all(block, 'kvp', 0, 0, tiled=True)  53.9 us
    ppermute x2, starting transfers between devices, onward(): return lax.ppermute(block, ('section', 'tp'), route)  14.6 us
    ppermute x4, starting transfers between devices, swap(): return lax.ppermute(block, 'tp', [(0, 1), (1, 0)])  12.3 us
    all_to_all x1, blocking collectives, body(): first = lax.all_to_all(kv, 'kvp', 0, 0, tiled=True, axis_index_groups=RINGS)  11.7 us
    ppermute x2, waiting for transfers between devices, onward(): return lax.ppermute(block, ('section', 'tp'), route)  10.9 us
    all_gather x1, waiting for transfers between devices, body(): held = lax.all_gather(jnp.stack([own, got]), 'kvp', axis_index_groups=RINGS)  7.19 us
    all_to_all x1, starting transfers between devices, spread(): return lax.all_to_all(block, 'kvp', 0, 0, tiled=True)  6.05 us
    ppermute x2, starting transfers between devices, body(): pair = lax.ppermute(here, 'kvp', [(i, (i + RING) % N) for i in range(N)])  5.27 us
  transfers between devices with their start and end apart: 12, of which 5 were waited for; matrix products, arithmetic and copies ran while one was open for 5% of the time, Pallas kernels for 5%

profile of v6, /device:TPU:7, one launch (start us, length us, event | category | flops | bytes accessed | tf_op | source)
XLA Modules:
  0.0 171.2 jit_solution(1935352039394672011)
XLA Ops:
  7.9 1.2 copy.50
  9.2 2.5 %collective-permute-start.1 = (bf16[2,256,128]{2,1,0:T(8,128)(2,1)S(1)}, bf16[2,256,128]{2,1,0:T(8,128)(2,1)S(1)}, u32[]{:S(2)}, u32[]{:S(2)}) collective-permute-start(bf16[2,256,128]{2,1,0:T(8,128)(2,1)S(1)} %get-tuple-element.57), channel_id=1, source_target_pairs={{0,16},{2,18},{4,20},{6,22},{8,24},{10,26},{12,28},{14,30},{16,0},... | collective-permute-start | bytes 393224 | tf_op jit(solution)/shard_map/ppermute | solution.py:200
  11.7 3.8 %collective-permute-done.1 = bf16[2,256,128]{2,1,0:T(8,128)(2,1)S(1)} collective-permute-done((bf16[2,256,128]{2,1,0:T(8,128)(2,1)S(1)}, bf16[2,256,128]{2,1,0:T(8,128)(2,1)S(1)}, u32[]{:S(2)}, u32[]{:S(2)}) %collective-permute-start.1) | collective-permute-done | bytes 131104 | tf_op jit(solution)/shard_map/ppermute | solution.py:200
  16.4 20.0 %all_to_all.25.mine = bf16[16,64,256]{2,1,0:T(8,128)(2,1)S(1)} all-to-all(bf16[16,64,256]{2,1,0:T(8,128)(2,1)S(1)} %broadcast_in_dim.24), channel_id=1, replica_groups=mesh['section'=16,'kvp'=16,'tp'=2] {'kvp'}, dimensions={0} | all-to-all | bytes 1048576 | tf_op jit(solution)/shard_map/all_to_all | solution.py:169
  36.4 5.4 %collective-permute-start = (bf16[16,64,256]{2,1,0:T(8,128)(2,1)S(1)}, bf16[16,64,256]{2,1,0:T(8,128)(2,1)S(1)}, u32[]{:S(2)}, u32[]{:S(2)}) collective-permute-start(bf16[16,64,256]{2,1,0:T(8,128)(2,1)S(1)} %all_to_all.25.mine), channel_id=1, source_target_pairs={{0,1},{1,0},{2,3},{3,2},{4,5},{5,4},{6,7},{7,6},{8,9},{9,8},{10,11... | collective-permute-start | bytes 1572872 | tf_op jit(solution)/shard_map/ppermute | solution.py:173
  41.9 1.4 collective-permute-done.other
  43.3 1.6 project_first.1
  44.9 11.7 %all_to_all.26.first = bf16[8,32,128]{2,1,0:T(8,128)(2,1)S(1)} all-to-all(bf16[8,32,128]{2,1,0:T(8,128)(2,1)S(1)} %get-tuple-element.26), channel_id=1, replica_groups={{0,2,4,6,8,10,12,14},{16,18,20,22,24,26,28,30},{1,3,5,7,9,11,13,15},{17..., dimensions={0} | all-to-all | bytes 131072 | tf_op jit(solution)/shard_map/all_to_all | solution.py:230
  56.6 7.2 %all-gather.5.cloned.1.call-done = bf16[16,2,256,128]{3,2,1,0:T(8,128)(2,1)} async-done(((bf16[2,2,256,128]{3,2,1,0:T(8,128)(2,1)}), bf16[16,2,256,128]{3,2,1,0:T(8,128)(2,1)}) %all-gather.5.cloned.1.call-update) | async-done | bytes 2097168 | tf_op jit(solution)/shard_map/all_gather | solution.py:201
  63.8 1.6 copy-done
  65.4 1.8 %attend_first.1 = bf16[16,128,128]{2,1,0:T(8,128)(2,1)S(1)} custom-call(s32[2]{0:T(128)S(1)} %pad_add_fusion.place, bf16[128,128]{1,0:T(8,128)(2,1)S(1)} %get-tuple-element.25.q_ref, bf16[8,2,2,256,128]{4,3,2,1,0:T(8,128)(2,1)S(1)} %bitcast.52, bf16[8,32,128]{2,1,0:T(8,128)(2,1)S(1)} %all_to_all.26.first, bf16[2048,256]{1,0:T(8,128)(2,1)S(1)} %bitcast.58), custom_call_target="tpu_custom_call" | custom-call | tf_op jit(solution)/shard_map/attend_first/pallas_call | solution.py:235
  67.2 14.2 %all_to_all.27.att = bf16[16,128,128]{2,1,0:T(8,128)(2,1)S(1)} all-to-all(bf16[16,128,128]{2,1,0:T(8,128)(2,1)S(1)} %attend_first.1), channel_id=1, replica_groups=mesh['section'=16,'kvp'=16,'tp'=2] {'kvp'}, dimensions={0} | all-to-all | bytes 1048576 | tf_op jit(solution)/shard_map/all_to_all | solution.py:169
  81.4 1.0 mix.2
  82.4 3.5 %collective-permute-start.2 = (f32[64,256]{1,0:T(8,128)S(1)}, f32[64,256]{1,0:T(8,128)S(1)}, u32[]{:S(2)}, u32[]{:S(2)}) collective-permute-start(f32[64,256]{1,0:T(8,128)S(1)} %get-tuple-element.39), channel_id=1, source_target_pairs={{0,32},{1,33},{32,64},{33,65},{64,96},{65,97},{96,128},{97,129},{1... | collective-permute-start | bytes 196616 | tf_op jit(solution)/shard_map/ppermute | solution.py:178
  85.9 11.1 %collective-permute-start.3 = (f32[64,256]{1,0:T(8,128)S(1)}, f32[64,256]{1,0:T(8,128)}, u32[]{:S(2)}, u32[]{:S(2)}) collective-permute-start(f32[64,256]{1,0:T(8,128)S(1)} %get-tuple-element.40), channel_id=1, source_target_pairs={{0,33},{1,32},{32,65},{33,64},{64,97},{65,96},{96,129},{97,128},{1... | collective-permute-start | bytes 196616 | tf_op jit(solution)/shard_map/ppermute | solution.py:178
  97.0 10.9 %collective-permute-done.3 = f32[64,256]{1,0:T(8,128)} collective-permute-done((f32[64,256]{1,0:T(8,128)S(1)}, f32[64,256]{1,0:T(8,128)}, u32[]{:S(2)}, u32[]{:S(2)}) %collective-permute-start.3) | collective-permute-done | bytes 65568 | tf_op jit(solution)/shard_map/ppermute | solution.py:178
  107.9 0.9 fusion.4.x_ref
  108.8 19.7 %all_to_all.28.x = bf16[16,64,256]{2,1,0:T(8,128)(2,1)} all-to-all(bf16[16,64,256]{2,1,0:T(8,128)(2,1)S(1)} %broadcast_in_dim.26), channel_id=1, replica_groups=mesh['section'=16,'kvp'=16,'tp'=2] {'kvp'}, dimensions={0} | all-to-all | bytes 1048576 | tf_op jit(solution)/shard_map/all_to_all | solution.py:169
  128.5 1.9 %collective-permute-start.4 = (bf16[16,64,256]{2,1,0:T(8,128)(2,1)}, bf16[16,64,256]{2,1,0:T(8,128)(2,1)}, u32[]{:S(2)}, u32[]{:S(2)}) collective-permute-start(bf16[16,64,256]{2,1,0:T(8,128)(2,1)} %all_to_all.28.x), channel_id=1, source_target_pairs={{0,1},{1,0},{2,3},{3,2},{4,5},{5,4},{6,7},{7,6},{8,9},{9,8},{10,11... | collective-permute-start | bytes 1572872 | tf_op jit(solution)/shard_map/ppermute | solution.py:173
  130.4 2.5 %own_rows.1 = (bf16[64,4096]{1,0:T(8,128)(2,1)S(1)}, bf16[64,128]{1,0:T(8,128)(2,1)S(1)}, f32[64,128]{1,0:T(8,128)S(1)}, f32[64,128]{1,0:T(8,128)S(1)}, f32[64,128]{1,0:T(8,128)S(1)}) custom-call(s32[2]{0:T(128)S(1)} %pad_add_fusion.place, bf16[16,64,256]{2,1,0:T(8,128)(2,1)} %all_to_all.28.x, f32[1,4096]{1,0:T(1,128)S(1)} %copy-done.9, ...), custom_call_target="tpu_custom_call" | custom-call | tf_op jit(solution)/shard_map/own_rows/pallas_call | solution.py:246
  133.0 3.4 %other_rows.1 = (bf16[16,128,128]{2,1,0:T(8,128)(2,1)S(1)}, bf16[128,256]{1,0:T(8,128)(2,1)S(1)}) custom-call(s32[2]{0:T(128)S(1)} %pad_add_fusion.place, bf16[16,64,256]{2,1,0:T(8,128)(2,1)} %collective-permute-done.4.x, f32[1,4096]{1,0:T(1,128)S(1)} %copy-done.9, bf16[4096,128]{1,0:T(8,128)(2,1)S(1)} %bitcast.57, bf16[256,4096]{1,0:T(8,128)(2,1)S(1)} %copy-done.6, ...), custom_call_target="tpu_custom_call" | custom-call | tf_op jit(solution)/shard_map/other_rows/pallas_call | solution.py:255
  137.3 6.0 %all-to-all-start.4 = ((bf16[16,128,128]{2,1,0:T(8,128)(2,1)}), bf16[16,128,128]{2,1,0:T(8,128)(2,1)S(1)}, u32[]{:S(2)}, u32[]{:S(2)}) async-start(bf16[16,128,128]{2,1,0:T(8,128)(2,1)} %copy-done.8), calls=%async_computation.4 | async-start | bytes 1048576 | tf_op jit(solution)/shard_map/all_to_all | solution.py:169
  143.3 2.0 %collective-permute-start.6 = (bf16[128,256]{0,1:T(8,128)(2,1)S(1)}, bf16[128,256]{0,1:T(8,128)(2,1)S(1)}, u32[]{:S(2)}, u32[]{:S(2)}) collective-permute-start(bf16[128,256]{0,1:T(8,128)(2,1)S(1)} %bitcast.61), channel_id=1, source_target_pairs={{0,16},{2,18},{4,20},{6,22},{8,24},{10,26},{12,28},{14,30},{16,0},... | collective-permute-start | bytes 196616 | tf_op jit(solution)/shard_map/ppermute | solution.py:268
  147.2 3.3 %collective-permute-start.7 = (bf16[128,256]{1,0:T(8,128)(2,1)S(1)}, bf16[128,256]{1,0:T(8,128)(2,1)S(1)}, u32[]{:S(2)}, u32[]{:S(2)}) collective-permute-start(bf16[128,256]{1,0:T(8,128)(2,1)S(1)} %get-tuple-element.42), channel_id=1, source_target_pairs={{0,16},{2,18},{4,20},{6,22},{8,24},{10,26},{12,28},{14,30},{16,0},... | collective-permute-start | bytes 196616 | tf_op jit(solution)/shard_map/ppermute | solution.py:268
  150.7 3.1 %collective-permute-start.5 = (f32[64,256]{1,0:T(8,128)}, f32[64,256]{1,0:T(8,128)S(1)}, u32[]{:S(2)}, u32[]{:S(2)}) collective-permute-start(f32[64,256]{1,0:T(8,128)} %copy-done.11), channel_id=1, source_target_pairs={{0,1},{1,0},{2,3},{3,2},{4,5},{5,4},{6,7},{7,6},{8,9},{9,8},{10,11... | collective-permute-start | bytes 196616 | tf_op jit(solution)/shard_map/ppermute | solution.py:173
  153.9 1.0 fusion.1
  154.9 1.8 %select_n.90 = bf16[2,2,512,128]{3,2,0,1:T(8,128)(2,1)} dynamic-update-slice(bf16[2,2,512,128]{3,2,0,1:T(8,128)(2,1)} %bitcast.69, bf16[2,2,128,128]{3,2,0,1:T(8,128)(2,1)S(1)} %fusion.1, s32[]{:T(128)} %constant.38.clone.1, s32[]{:T(128)} %constant.38.clone.1, s32[]{:T(128)S(6)} %select_n.86, s32[]{:T(128)} %constant.38.clone.1) | dynamic-update-slice | bytes 262148 | tf_op jit(solution)/shard_map/jit(_where)/select_n | solution.py:210
  156.8 1.0 fusion.3
  157.8 1.8 %select_n.97 = bf16[2,2,512,128]{3,2,0,1:T(8,128)(2,1)} dynamic-update-slice(bf16[2,2,512,128]{3,2,0,1:T(8,128)(2,1)} %select_n.90, bf16[2,2,128,128]{3,2,0,1:T(8,128)(2,1)S(1)} %fusion.3, s32[]{:T(128)} %constant.38.clone.1, s32[]{:T(128)} %constant.38.clone.1, s32[]{:T(128)S(6)} %select_n.94, s32[]{:T(128)} %constant.38.clone.1) | dynamic-update-slice | bytes 262148 | tf_op jit(solution)/shard_map/jit(_where)/select_n | solution.py:210
  159.6 1.0 mix.3
  160.6 1.9 %collective-permute-start.8 = (f32[64,256]{1,0:T(8,128)S(1)}, f32[64,256]{1,0:T(8,128)S(1)}, u32[]{:S(2)}, u32[]{:S(2)}) collective-permute-start(f32[64,256]{1,0:T(8,128)S(1)} %get-tuple-element.46), channel_id=1, source_target_pairs={{0,1},{1,0},{2,3},{3,2},{4,5},{5,4},{6,7},{7,6},{8,9},{9,8},{10,11... | collective-permute-start | bytes 196616 | tf_op jit(solution)/shard_map/ppermute | solution.py:173
  162.6 0.8 copy.47
  (61 shorter events, 3.9 us)
Async XLA Ops:
  7.2 9.2 %copy-start.10 = (bf16[1,64,256]{2,1,0:T(8,128)(2,1)S(1)}, bf16[1,64,256]{2,1,0:T(8,128)(2,1)}, u32[]{:S(2)}) copy-start(bf16[1,64,256]{2,1,0:T(8,128)(2,1)} %param.9) | copy-start | bytes 98308
  7.2 56.6 %all-gather.5.cloned.1.call-start = ((), (), s32[]{:S(2)}) async-start(), calls=%async_computation.5 | async-start | bytes 2359296 | tf_op jit(solution)/shard_map/all_gather | solution.py:201
  7.9 35.4 %copy-start.2 = (bf16[1,4096,1,128]{3,1,2,0:T(8,128)(2,1)S(1)}, bf16[1,4096,1,128]{3,1,2,0:T(8,128)(2,1)}, u32[]{:S(2)}) copy-start(bf16[1,4096,1,128]{3,1,2,0:T(8,128)(2,1)} %param.12) | copy-start | bytes 3145732
  7.9 35.4 %copy-start.7 = (bf16[1,4096,1,32]{1,3,2,0:T(8,128)(2,1)S(1)}, bf16[1,4096,1,32]{1,3,2,0:T(8,128)(2,1)}, u32[]{:S(2)}) copy-start(bf16[1,4096,1,32]{1,3,2,0:T(8,128)(2,1)} %param.13) | copy-start | bytes 786436
  7.9 35.4 %copy-start.9 = (f32[1,4096]{1,0:T(1,128)S(1)}, f32[1,4096]{1,0:T(1,128)}, u32[]{:S(2)}) copy-start(f32[1,4096]{1,0:T(1,128)} %gain.5) | copy-start | bytes 49156
  9.1 7.2 %copy-start.12 = (bf16[1,2,2,512,128]{4,3,1,2,0:T(8,128)(2,1)}, bf16[1,2,2,512,128]{4,3,1,2,0:T(8,128)(2,1)S(1)}, u32[]{:S(2)}) copy-start(bf16[1,2,2,512,128]{4,3,1,2,0:T(8,128)(2,1)S(1)} %copy.50) | copy-start | bytes 1572868
  9.2 6.3 %collective-permute-start.1 = (bf16[2,256,128]{2,1,0:T(8,128)(2,1)S(1)}, bf16[2,256,128]{2,1,0:T(8,128)(2,1)S(1)}, u32[]{:S(2)}, u32[]{:S(2)}) collective-permute-start(bf16[2,256,128]{2,1,0:T(8,128)(2,1)S(1)} %get-tuple-element.57), channel_id=1, source_target_pairs={{0,16},{2,18},{4,20},{6,22},{8,24},{10,26},{12,28},{14,30},{16,0},... | collective-permute-start | bytes 393224 | tf_op jit(solution)/shard_map/ppermute | solution.py:200
  16.3 114.2 %all-gather.7.cloned.1.call-start = ((), (), s32[]{:S(2)}) async-start(), calls=%async_computation.6 | async-start | bytes 2359296 | tf_op jit(solution)/shard_map/all_gather | solution.py:232
  16.3 47.5 %copy-start.3 = (bf16[1,2048,256]{2,1,0:T(8,128)(2,1)S(1)}, bf16[1,2048,256]{2,1,0:T(8,128)(2,1)}, u32[]{:S(2)}) copy-start(bf16[1,2048,256]{2,1,0:T(8,128)(2,1)} %param.14) | copy-start | bytes 3145732
  36.4 6.9 %collective-permute-start = (bf16[16,64,256]{2,1,0:T(8,128)(2,1)S(1)}, bf16[16,64,256]{2,1,0:T(8,128)(2,1)S(1)}, u32[]{:S(2)}, u32[]{:S(2)}) collective-permute-start(bf16[16,64,256]{2,1,0:T(8,128)(2,1)S(1)} %all_to_all.25.mine), channel_id=1, source_target_pairs={{0,1},{1,0},{2,3},{3,2},{4,5},{5,4},{6,7},{7,6},{8,9},{9,8},{10,11... | collective-permute-start | bytes 1572872 | tf_op jit(solution)/shard_map/ppermute | solution.py:173
  63.8 1.6 copy-start
  65.4 16.0 %copy-start.4 = (bf16[1,2048,256]{2,1,0:T(8,128)(2,1)S(1)}, bf16[1,2048,256]{2,1,0:T(8,128)(2,1)}, u32[]{:S(2)}) copy-start(bf16[1,2048,256]{2,1,0:T(8,128)(2,1)} %param.14) | copy-start | bytes 3145732
  67.2 40.7 %copy-start.14 = (bf16[1,64,256]{2,1,0:T(8,128)(2,1)S(1)}, bf16[1,64,256]{2,1,0:T(8,128)(2,1)}, u32[]{:S(2)}) copy-start(bf16[1,64,256]{2,1,0:T(8,128)(2,1)} %param.10) | copy-start | bytes 98308
  67.2 63.3 %copy-start.1 = (bf16[16,2,256,128]{3,2,1,0:T(8,128)(2,1)S(1)}, bf16[16,2,256,128]{3,2,1,0:T(8,128)(2,1)}, u32[]{:S(2)}) copy-start(bf16[16,2,256,128]{3,2,1,0:T(8,128)(2,1)} %all-gather.5.cloned.1.call-done) | copy-start | bytes 6291460
  82.4 50.6 %copy-start.11 = (f32[64,256]{1,0:T(8,128)}, f32[64,256]{1,0:T(8,128)S(1)}, u32[]{:S(2)}) copy-start(f32[64,256]{1,0:T(8,128)S(1)} %get-tuple-element.40) | copy-start | bytes 196612
  82.4 14.6 %collective-permute-start.2 = (f32[64,256]{1,0:T(8,128)S(1)}, f32[64,256]{1,0:T(8,128)S(1)}, u32[]{:S(2)}, u32[]{:S(2)}) collective-permute-start(f32[64,256]{1,0:T(8,128)S(1)} %get-tuple-element.39), channel_id=1, source_target_pairs={{0,32},{1,33},{32,64},{33,65},{64,96},{65,97},{96,128},{97,129},{1... | collective-permute-start | bytes 196616 | tf_op jit(solution)/shard_map/ppermute | solution.py:178
  85.9 22.0 %collective-permute-start.3 = (f32[64,256]{1,0:T(8,128)S(1)}, f32[64,256]{1,0:T(8,128)}, u32[]{:S(2)}, u32[]{:S(2)}) collective-permute-start(f32[64,256]{1,0:T(8,128)S(1)} %get-tuple-element.40), channel_id=1, source_target_pairs={{0,33},{1,32},{32,65},{33,64},{64,97},{65,96},{96,129},{97,128},{1... | collective-permute-start | bytes 196616 | tf_op jit(solution)/shard_map/ppermute | solution.py:178
  128.5 4.5 %collective-permute-start.4 = (bf16[16,64,256]{2,1,0:T(8,128)(2,1)}, bf16[16,64,256]{2,1,0:T(8,128)(2,1)}, u32[]{:S(2)}, u32[]{:S(2)}) collective-permute-start(bf16[16,64,256]{2,1,0:T(8,128)(2,1)} %all_to_all.28.x), channel_id=1, source_target_pairs={{0,1},{1,0},{2,3},{3,2},{4,5},{5,4},{6,7},{7,6},{8,9},{9,8},{10,11... | collective-permute-start | bytes 1572872 | tf_op jit(solution)/shard_map/ppermute | solution.py:173
  130.4 2.6 %copy-start.6 = (bf16[256,4096]{1,0:T(8,128)(2,1)S(1)}, bf16[256,4096]{1,0:T(8,128)(2,1)}, u32[]{:S(2)}) copy-start(bf16[256,4096]{1,0:T(8,128)(2,1)} %all-gather.7.cloned.1.call-done.wkv) | copy-start | bytes 6291460
  133.0 12.3 %copy-start.15 = (s32[2,1]{0,1:T(1,128)S(1)}, s32[2,1]{0,1:T(1,128)}, u32[]{:S(2)}) copy-start(s32[2,1]{0,1:T(1,128)} %param.17) | copy-start | bytes 28
  136.5 0.8 copy-start.8
  137.3 22.3 %copy-start.5 = (bf16[1,2048,256]{2,1,0:T(8,128)(2,1)S(1)}, bf16[1,2048,256]{2,1,0:T(8,128)(2,1)}, u32[]{:S(2)}) copy-start(bf16[1,2048,256]{2,1,0:T(8,128)(2,1)} %param.14) | copy-start | bytes 3145732
  137.3 22.3 %all-to-all-start.4 = ((bf16[16,128,128]{2,1,0:T(8,128)(2,1)}), bf16[16,128,128]{2,1,0:T(8,128)(2,1)S(1)}, u32[]{:S(2)}, u32[]{:S(2)}) async-start(bf16[16,128,128]{2,1,0:T(8,128)(2,1)} %copy-done.8), calls=%async_computation.4 | async-start | bytes 1048576 | tf_op jit(solution)/shard_map/all_to_all | solution.py:169
  143.3 10.5 %collective-permute-start.6 = (bf16[128,256]{0,1:T(8,128)(2,1)S(1)}, bf16[128,256]{0,1:T(8,128)(2,1)S(1)}, u32[]{:S(2)}, u32[]{:S(2)}) collective-permute-start(bf16[128,256]{0,1:T(8,128)(2,1)S(1)} %bitcast.61), channel_id=1, source_target_pairs={{0,16},{2,18},{4,20},{6,22},{8,24},{10,26},{12,28},{14,30},{16,0},... | collective-permute-start | bytes 196616 | tf_op jit(solution)/shard_map/ppermute | solution.py:268
  147.2 9.5 %collective-permute-start.7 = (bf16[128,256]{1,0:T(8,128)(2,1)S(1)}, bf16[128,256]{1,0:T(8,128)(2,1)S(1)}, u32[]{:S(2)}, u32[]{:S(2)}) collective-permute-start(bf16[128,256]{1,0:T(8,128)(2,1)S(1)} %get-tuple-element.42), channel_id=1, source_target_pairs={{0,16},{2,18},{4,20},{6,22},{8,24},{10,26},{12,28},{14,30},{16,0},... | collective-permute-start | bytes 196616 | tf_op jit(solution)/shard_map/ppermute | solution.py:268
  150.7 11.8 %collective-permute-start.5 = (f32[64,256]{1,0:T(8,128)}, f32[64,256]{1,0:T(8,128)S(1)}, u32[]{:S(2)}, u32[]{:S(2)}) collective-permute-start(f32[64,256]{1,0:T(8,128)} %copy-done.11), channel_id=1, source_target_pairs={{0,1},{1,0},{2,3},{3,2},{4,5},{5,4},{6,7},{7,6},{8,9},{9,8},{10,11... | collective-permute-start | bytes 196616 | tf_op jit(solution)/shard_map/ppermute | solution.py:173
  159.6 2.9 %copy-start.13 = (bf16[2,2,512,128]{3,2,0,1:T(8,128)(2,1)S(1)}, bf16[2,2,512,128]{3,2,0,1:T(8,128)(2,1)}, u32[]{:S(2)}) copy-start(bf16[2,2,512,128]{3,2,0,1:T(8,128)(2,1)} %select_n.97) | copy-start | bytes 1572868
  160.6 3.1 %collective-permute-start.8 = (f32[64,256]{1,0:T(8,128)S(1)}, f32[64,256]{1,0:T(8,128)S(1)}, u32[]{:S(2)}, u32[]{:S(2)}) collective-permute-start(f32[64,256]{1,0:T(8,128)S(1)} %get-tuple-element.46), channel_id=1, source_target_pairs={{0,1},{1,0},{2,3},{3,2},{4,5},{5,4},{6,7},{7,6},{8,9},{9,8},{10,11... | collective-permute-start | bytes 196616 | tf_op jit(solution)/shard_map/ppermute | solution.py:173
Sparse Core Ops, SparseCore 0:
  16.4 47.3 all-gather.4
  65.9 44.1 all-gather.6
